TPU v7x, 128 devices: a whole 4x4x4 slice. The times are simulated.
128 devices in a mesh: node: 16 (over y, x), local: 8 (over z, core).
Axes of the slice: x: 4, y: 4, z: 4, core: 2. Of those that a mesh axis runs over, the one named last changes fastest.
Arguments:
- inverse: int32 [256, 256], P(('node', 'local')), may hold values from 0 to 1023, as said below
- slot_rows: int32 [16, 8, 16, 8], P('node', 'local'), may hold values from 0 to 1023, as said below
- lengths: int32 [256], P(('node', 'local')), may hold values from 64 to 256
- content: bfloat16 [131072, 1024], P(('node', 'local')), may hold values from -6 to 6
- w_tower: bfloat16 [1024, 1024], replicated, may hold values from -0.1875 to 0.1875
- w_in: bfloat16 [1024, 4096], replicated, may hold values from -0.1875 to 0.1875
- w_out: bfloat16 [1024, 1024], replicated, may hold values from -0.1875 to 0.1875
- out_grad: bfloat16 [256, 256, 1024], P(('node', 'local')), may hold values from -6 to 6
Outputs:
- events_out: bfloat16 [256, 256, 1024], P(('node', 'local'))
- content_grad: bfloat16 [131072, 1024], P(('node', 'local'))
- tower_grad: float32 [1024, 1024], replicated
Inputs may be any that keep to these rules, and one draw needn't show every extreme that they name: `inverse`: slots named by events of node n lie in buckets (l, m) whose first slots are named; the 8 slots of one bucket name distinct items, so the events of a node never name two slots of one item; some bucket of every node is full and some owner's buckets are full from every node. `slot_rows`: the 8 rows of one bucket are distinct; slots named by no event hold arbitrary rows.
All inputs are finite; a program needn't handle non-finite values.
Results may differ from a plain program's by a relative error of at most 0.018.
Values may be sent and summed in bfloat16 or wider, within the bound.
No kernel may reach another device: no remote copies, remote signals or barrier semaphores. Data moves between devices by JAX's collectives and lax.ppermute only.
A program may use at most 128 MiB of HBM per device.

v0:
```python
import jax
import jax.numpy as jnp
from jax import lax
from jax.sharding import PartitionSpec as P

HEADS = 8


def seq_layer(events, length, w_in, w_out):
    rows, width = events.shape
    head_size = width // HEADS
    normed = (events * lax.rsqrt(jnp.mean(events * events, axis=-1, keepdims=True) + 1e-06)).astype(
        jnp.bfloat16
    )
    hidden = jax.nn.silu(jnp.dot(normed, w_in, preferred_element_type=jnp.float32)).astype(
        jnp.bfloat16
    )
    gate_part, value_part, query_part, key_part = jnp.split(hidden, 4, axis=1)
    queries = query_part.reshape(rows, HEADS, head_size)
    keys = key_part.reshape(rows, HEADS, head_size)
    values = value_part.reshape(rows, HEADS, head_size)
    scores = jnp.einsum(
        "ihd,jhd->hij", queries, keys, preferred_element_type=jnp.float32
    ) * head_size ** (-0.5)
    position = jnp.arange(rows)
    allowed = (position[None, :] <= position[:, None]) & (position[:, None] < length)
    weights = (
        jnp.where(allowed[None], jax.nn.silu(scores), 0.0) / length.astype(jnp.float32)
    ).astype(jnp.bfloat16)
    mixed_heads = jnp.einsum(
        "hij,jhd->ihd", weights, values, preferred_element_type=jnp.float32
    ).reshape(rows, width)
    centred = mixed_heads - jnp.mean(mixed_heads, axis=-1, keepdims=True)
    normal = centred * lax.rsqrt(jnp.mean(centred * centred, axis=-1, keepdims=True) + 1e-05)
    gated_rows = (normal * gate_part.astype(jnp.float32)).astype(jnp.bfloat16)
    return events + jnp.dot(gated_rows, w_out, preferred_element_type=jnp.float32)


def silu_slope(values):
    sigma = jax.nn.sigmoid(values)
    return sigma * (1.0 + values * (1.0 - sigma))


def body(inverse, slot_rows, lengths, content, w_tower, w_in, w_out, out_grad):
    node_count = lax.axis_size("node")
    local_count = lax.axis_size("local")
    slot_cap = slot_rows.shape[3]
    width = content.shape[1]
    requests = lax.all_to_all(slot_rows, "node", split_axis=2, concat_axis=0, tiled=True)
    wanted_rows = requests.reshape(node_count * slot_cap)
    picked = jnp.take(content, wanted_rows, axis=0)
    pre_act = jnp.dot(picked, w_tower, preferred_element_type=jnp.float32)
    embedded = jax.nn.silu(pre_act).astype(jnp.bfloat16).reshape(node_count, slot_cap, width)
    fetched = lax.all_to_all(embedded, "node", split_axis=0, concat_axis=0, tiled=True)
    node_table = lax.all_gather(fetched, "local", axis=0, tiled=True).reshape(
        local_count * node_count * slot_cap, width
    )
    events = jnp.take(node_table, inverse, axis=0)

    def one_sequence(packed):
        seq_events, length, cotangent = packed
        layer_out, pullback = jax.vjp(
            lambda values: seq_layer(values, length, w_in, w_out), seq_events.astype(jnp.float32)
        )
        return (layer_out.astype(jnp.bfloat16), pullback(cotangent.astype(jnp.float32))[0])

    events_out, event_grads = lax.map(one_sequence, (events, lengths, out_grad))
    partial_grads = (
        jnp.zeros((node_table.shape[0], width), jnp.float32)
        .at[inverse.reshape(-1)]
        .add(event_grads.reshape(-1, width))
    )
    partial_grads = partial_grads.reshape(local_count, node_count, slot_cap, width)
    arrived = lax.all_to_all(
        lax.all_to_all(partial_grads, "node", split_axis=1, concat_axis=1, tiled=True),
        "local",
        split_axis=0,
        concat_axis=0,
        tiled=True,
    )
    owner_side = jnp.sum(arrived, axis=0)
    slot_grads = owner_side.reshape(node_count * slot_cap, width)
    pre_grads = (slot_grads * silu_slope(pre_act)).astype(jnp.bfloat16)
    row_grads = jnp.einsum("re,de->rd", pre_grads, w_tower, preferred_element_type=jnp.float32)
    content_grad = (
        jnp.zeros(content.shape, jnp.float32).at[wanted_rows].add(row_grads).astype(jnp.bfloat16)
    )
    tower_part = jnp.einsum("rd,re->de", picked, pre_grads, preferred_element_type=jnp.float32)
    tower_grad = lax.psum(tower_part, ("node", "local"))
    return (events_out, content_grad, tower_grad)


def solution(mesh):
    in_specs = (
        P(("node", "local"), None),
        P("node", "local", None, None),
        P(("node", "local")),
        P(("node", "local"), None),
        P(),
        P(),
        P(),
        P(("node", "local"), None, None),
    )
    out_specs = (P(("node", "local"), None, None), P(("node", "local"), None), P())
    return jax.shard_map(body, mesh=mesh, in_specs=in_specs, out_specs=out_specs, check_vma=False)
```

profile of v0, /device:TPU:1, one launch (start us, length us, event | category | flops | bytes accessed | tf_op | source)
XLA Modules:
  0.0 467.4 jit_solution(1915563058274840186)
XLA Ops:
  8.7 7.6 %all-to-all-start = ((s32[1,1,16,8]{3,1,0,2:T(1,128)}), s32[1,1,16,8]{3,1,0,2:T(1,128)S(1)}, u32[]{:S(2)}, u32[]{:S(2)}) async-start(s32[1,1,16,8]{3,1,0,2:T(1,128)} %copy.65), calls=%async_computation | async-start | bytes 16384 | tf_op jit(solution)/shard_map/all_to_all | solution.py:49
  16.3 6.3 %all-to-all-done = s32[1,1,16,8]{3,1,0,2:T(1,128)S(1)} async-done(((s32[1,1,16,8]{3,1,0,2:T(1,128)}), s32[1,1,16,8]{3,1,0,2:T(1,128)S(1)}, u32[]{:S(2)}, u32[]{:S(2)}) %all-to-all-start) | async-done | bytes 544 | tf_op jit(solution)/shard_map/all_to_all | solution.py:49
  24.5 2.9 gather_fusion
  28.9 10.8 %all_to_all.24 = bf16[16,8,1024]{2,1,0:T(8,128)(2,1)} all-to-all(bf16[16,8,1024]{2,1,0:T(8,128)(2,1)S(1)} %fusion.62), channel_id=1, replica_groups=mesh['node'=16,'local'=8] {'node'}, dimensions={0} | all-to-all | bytes 524288 | tf_op jit(solution)/shard_map/all_to_all | solution.py:54
  40.5 26.3 %all-gather.2.cloned.1.call-done = bf16[128,8,1024]{2,1,0:T(8,128)(2,1)} async-done(((bf16[16,8,1024]{2,1,0:T(8,128)(2,1)}), bf16[128,8,1024]{2,1,0:T(8,128)(2,1)}) %all-gather.2.cloned.1.call-update) | async-done | bytes 2097168 | tf_op jit(solution)/shard_map/all_gather | solution.py:55
  66.8 5.3 %gather_fusion.1 = bf16[512,1024]{1,0:T(8,128)(2,1)} fusion(bf16[1024,1024]{1,0:T(8,128)(2,1)} %bitcast.187, s32[1024]{0:T(1024)S(1)} %pad_clamp_fusion), kind=kCustom, calls=%fused_computation.1 | custom fusion | bytes 2099200 | tf_op jit(solution)/shard_map/jit(_take)/gather | solution.py:58
  73.5 102.7 %while.12 = (s32[]{:T(128)}, bf16[2,256,1024]{2,1,0:T(8,128)(2,1)}, f32[2,256,1024]{2,1,0:T(8,128)}, bf16[2,256,1024]{2,1,0:T(8,128)(2,1)S(1)}, bf16[1024,4096]{...) while((s32[]{:T(128)}, bf16[2,256,1024]{2,1,0:T(8,128)(2,1)}, ...), condition=%wide.region_7.8_spmd, body=%wide.region_0.7_spmd.sunk | while | flops 6222908416 | bytes 169573552 | solution.py:67
  76.0 7.9 %multiply_convert_fusion.3 = (bf16[256,4096]{1,0:T(8,128)(2,1)S(1)}, f32[256,4096]{1,0:T(8,128)}) fusion(bf16[1024,4096]{1,0:T(8,128)(2,1)} %get-tuple-element.195, f32[256]{0:T(256)S(1)} %fusion.134, bf16[2,256,1024]{2,1,0:T(8,128)(2,1)S(1)} %get-tuple-element.194, s32[]{:T(128)S(6)} %copy.125), kind=kOutput, calls=%fused_computation.10.clone.1 | convolution fusion | flops 2153512960 | bytes 15205380 | tf_op jit(solution)/shard_map/while/body/eval_jaxpr/jvp()/dot_general | solution.py:15
  93.1 3.2 multiply_reduce_fusion.2
  105.5 2.7 fusion.141
  114.6 8.6 %fusion.142 = (f32[256]{0:T(256)S(1)}, bf16[256,1024]{1,0:T(8,128)(2,1)S(1)}) fusion(bf16[2,256,1024]{2,1,0:T(8,128)(2,1)} %copy-done.12, s32[]{:T(128)S(6)} %copy.125, bf16[1024,4096]{1,0:T(8,128)(2,1)} %get-tuple-element.195, f32[256,4096]{1,0:T(8,128)} %get-tuple-element.162, bf16[256,1024]{1,0:T(8,128)(2,1)} %copy.116, ...), kind=kOutput, calls=%fused_computation.53.clone.1 | convolution fusion | flops 2166619904 | bytes 15729668 | tf_op jit(solution)/shard_map/while/body/eval_jaxpr/transpose(jvp())/dot_general | solution.py:15
  127.2 7.9 %multiply_convert_fusion.3 = (bf16[256,4096]{1,0:T(8,128)(2,1)S(1)}, f32[256,4096]{1,0:T(8,128)}) fusion(bf16[1024,4096]{1,0:T(8,128)(2,1)} %get-tuple-element.195, f32[256]{0:T(256)S(1)} %fusion.134, bf16[2,256,1024]{2,1,0:T(8,128)(2,1)S(1)} %get-tuple-element.194, s32[]{:T(128)S(6)} %copy.125), kind=kOutput, calls=%fused_computation.10.clone.1 | convolution fusion | flops 2153512960 | bytes 15205380 | tf_op jit(solution)/shard_map/while/body/eval_jaxpr/jvp()/dot_general | solution.py:15
  144.4 3.2 multiply_reduce_fusion.2
  156.7 2.7 fusion.141
  165.8 8.7 %fusion.142 = (f32[256]{0:T(256)S(1)}, bf16[256,1024]{1,0:T(8,128)(2,1)S(1)}) fusion(bf16[2,256,1024]{2,1,0:T(8,128)(2,1)} %copy-done.12, s32[]{:T(128)S(6)} %copy.125, bf16[1024,4096]{1,0:T(8,128)(2,1)} %get-tuple-element.195, f32[256,4096]{1,0:T(8,128)} %get-tuple-element.162, bf16[256,1024]{1,0:T(8,128)(2,1)} %copy.116, ...), kind=kOutput, calls=%fused_computation.53.clone.1 | convolution fusion | flops 2166619904 | bytes 15729668 | tf_op jit(solution)/shard_map/while/body/eval_jaxpr/transpose(jvp())/dot_general | solution.py:15
  176.2 7.9 %scatter_custom_fusion = f32[1024,1024]{1,0:T(8,128)} fusion(s32[512]{0:T(512)} %bitcast.194, f32[512,1024]{1,0:T(8,128)} %bitcast.195, f32[]{:T(128)} %constant.75.clone.1), kind=kCustom, calls=%fused_computation.95 | custom fusion | flops 524288 | bytes 4194816 | tf_op jit(solution)/shard_map/scatter-add | solution.py:71
  186.6 56.5 %all_to_all.25 = f32[8,16,8,1024]{3,2,0,1:T(8,128)S(1)} all-to-all(f32[8,16,8,1024]{3,2,0,1:T(8,128)S(1)} %copy.66), channel_id=1, replica_groups=mesh['node'=16,'local'=8] {'node'}, dimensions={1} | all-to-all | bytes 8388608 | tf_op jit(solution)/shard_map/all_to_all | solution.py:75
  243.7 54.4 %all_to_all.26 = f32[8,16,8,1024]{3,2,1,0:T(8,128)} all-to-all(f32[8,16,8,1024]{3,2,1,0:T(8,128)S(1)} %copy.67), channel_id=1, replica_groups=mesh['node'=16,'local'=8] {'local'}, dimensions={0} | all-to-all | bytes 8388608 | tf_op jit(solution)/shard_map/all_to_all | solution.py:74
  298.1 3.5 reduce_sum.62
  302.8 2.8 fusion.63
  306.4 4.0 scatter_custom_fusion.1
  310.4 3.9 convert_element_type.83
  314.2 141.5 %all-reduce.2.cloned.1.call-done = f32[1024,1024]{1,0:T(8,128)} async-done(((f32[1024,1024]{1,0:T(8,128)}), f32[1024,1024]{1,0:T(8,128)}) %all-reduce.2.cloned.1.call-update) | async-done | bytes 4194320 | tf_op jit(solution)/shard_map/psum | solution.py:89
  455.7 4.8 %copy.134 = f32[1024,1024]{1,0:T(8,128)} copy(f32[1024,1024]{1,0:T(8,128)} %all-reduce.2.cloned.1.call-done) | data formatting | bytes 8388608
  (173 shorter events, 68.0 us)
Async XLA Ops:
  7.2 20.3 %copy-start = (bf16[1024,1024]{1,0:T(8,128)(2,1)S(1)}, bf16[1024,1024]{1,0:T(8,128)(2,1)}, u32[]{:S(2)}) copy-start(bf16[1024,1024]{1,0:T(8,128)(2,1)} %param.14) | copy-start | bytes 6291460
  8.7 13.9 %all-to-all-start = ((s32[1,1,16,8]{3,1,0,2:T(1,128)}), s32[1,1,16,8]{3,1,0,2:T(1,128)S(1)}, u32[]{:S(2)}, u32[]{:S(2)}) async-start(s32[1,1,16,8]{3,1,0,2:T(1,128)} %copy.65), calls=%async_computation | async-start | bytes 16384 | tf_op jit(solution)/shard_map/all_to_all | solution.py:49
  16.3 50.5 %all-gather.2.cloned.1.call-start = ((), (), s32[]{:S(2)}) async-start(), calls=%async_computation.4 | async-start | bytes 2359296 | tf_op jit(solution)/shard_map/all_gather | solution.py:55
  24.5 3.5 copy-start.20
  27.5 12.3 %copy-start.17 = (bf16[128,1024]{1,0:T(8,128)(2,1)}, bf16[128,1024]{1,0:T(8,128)(2,1)S(1)}, u32[]{:S(2)}) copy-start(bf16[128,1024]{1,0:T(8,128)(2,1)S(1)} %gather_fusion) | copy-start | bytes 786436
  27.5 12.4 %copy-start.19 = (s32[2,256]{1,0:T(2,128)S(1)}, s32[2,256]{1,0:T(2,128)}, u32[]{:S(2)}) copy-start(s32[2,256]{1,0:T(2,128)} %param.10) | copy-start | bytes 6148
  39.8 416.0 %all-reduce.2.cloned.1.call-start = ((), (), s32[]{:S(2)}) async-start(), calls=%async_computation.5 | async-start | bytes 8388608 | tf_op jit(solution)/shard_map/psum | solution.py:89
  73.7 10.2 %copy-start.12 = (bf16[2,256,1024]{2,1,0:T(8,128)(2,1)}, bf16[2,256,1024]{2,1,0:T(8,128)(2,1)S(1)}, u32[]{:S(2)}) copy-start(bf16[2,256,1024]{2,1,0:T(8,128)(2,1)S(1)} %get-tuple-element.194) | copy-start | bytes 3145732 | tf_op jit(solution)/shard_map/while
  86.6 3.7 copy-start.10
  93.1 3.8 copy-start.23
  105.5 5.9 %copy-start.2 = (bf16[8,256,256]{2,1,0:T(8,128)(2,1)S(1)}, bf16[8,256,256]{2,1,0:T(8,128)(2,1)}, u32[]{:S(2)}) copy-start(bf16[8,256,256]{2,1,0:T(8,128)(2,1)} %copy-done.1) | copy-start | bytes 3145732 | tf_op jit(solution)/shard_map/while
  114.6 8.7 %copy-start.13 = (bf16[2,256,1024]{2,1,0:T(8,128)(2,1)S(1)}, bf16[2,256,1024]{2,1,0:T(8,128)(2,1)}, u32[]{:S(2)}) copy-start(bf16[2,256,1024]{2,1,0:T(8,128)(2,1)} %copy-done.12) | copy-start | bytes 3145732 | tf_op jit(solution)/shard_map/while
  114.6 8.7 %copy-start.14 = (bf16[2,256,1024]{2,1,0:T(8,128)(2,1)S(1)}, bf16[2,256,1024]{2,1,0:T(8,128)(2,1)}, u32[]{:S(2)}) copy-start(bf16[2,256,1024]{2,1,0:T(8,128)(2,1)} %get-tuple-element.198) | copy-start | bytes 3145732 | tf_op jit(solution)/shard_map/while
  114.6 8.7 %copy-start.24 = (f32[2,256,1024]{2,1,0:T(8,128)S(1)}, f32[2,256,1024]{2,1,0:T(8,128)}, u32[]{:S(2)}) copy-start(f32[2,256,1024]{2,1,0:T(8,128)} %get-tuple-element.184) | copy-start | bytes 6291460 | tf_op jit(solution)/shard_map/while
  125.0 10.2 %copy-start.12 = (bf16[2,256,1024]{2,1,0:T(8,128)(2,1)}, bf16[2,256,1024]{2,1,0:T(8,128)(2,1)S(1)}, u32[]{:S(2)}) copy-start(bf16[2,256,1024]{2,1,0:T(8,128)(2,1)S(1)} %get-tuple-element.194) | copy-start | bytes 3145732 | tf_op jit(solution)/shard_map/while
  137.8 3.7 copy-start.10
  144.4 3.8 copy-start.23
  156.7 5.9 %copy-start.2 = (bf16[8,256,256]{2,1,0:T(8,128)(2,1)S(1)}, bf16[8,256,256]{2,1,0:T(8,128)(2,1)}, u32[]{:S(2)}) copy-start(bf16[8,256,256]{2,1,0:T(8,128)(2,1)} %copy-done.1) | copy-start | bytes 3145732 | tf_op jit(solution)/shard_map/while
  165.8 8.7 %copy-start.13 = (bf16[2,256,1024]{2,1,0:T(8,128)(2,1)S(1)}, bf16[2,256,1024]{2,1,0:T(8,128)(2,1)}, u32[]{:S(2)}) copy-start(bf16[2,256,1024]{2,1,0:T(8,128)(2,1)} %copy-done.12) | copy-start | bytes 3145732 | tf_op jit(solution)/shard_map/while
  165.8 8.7 %copy-start.14 = (bf16[2,256,1024]{2,1,0:T(8,128)(2,1)S(1)}, bf16[2,256,1024]{2,1,0:T(8,128)(2,1)}, u32[]{:S(2)}) copy-start(bf16[2,256,1024]{2,1,0:T(8,128)(2,1)} %get-tuple-element.198) | copy-start | bytes 3145732 | tf_op jit(solution)/shard_map/while
  165.8 8.7 %copy-start.24 = (f32[2,256,1024]{2,1,0:T(8,128)S(1)}, f32[2,256,1024]{2,1,0:T(8,128)}, u32[]{:S(2)}) copy-start(f32[2,256,1024]{2,1,0:T(8,128)} %get-tuple-element.184) | copy-start | bytes 6291460 | tf_op jit(solution)/shard_map/while
  298.1 3.5 copy-start.16
  298.1 4.7 %copy-start.18 = (bf16[128,1024]{1,0:T(8,128)(2,1)S(1)}, bf16[128,1024]{1,0:T(8,128)(2,1)}, u32[]{:S(2)}) copy-start(bf16[128,1024]{1,0:T(8,128)(2,1)} %copy-done.17) | copy-start | bytes 786436
  298.1 4.7 %copy-start.21 = (pred[128]{0:T(512)(128)(4,1)S(1)}, pred[128]{0:T(512)(128)(4,1)}, u32[]{:S(2)}) copy-start(pred[128]{0:T(512)(128)(4,1)} %copy-done.20) | copy-start | bytes 388
  (25 other events, 50.4 us)
Sparse Core Ops, SparseCore 0:
  39.9 26.8 all-gather.1
  305.7 149.9 all-reduce.1
where the time goes:
time: 469 us; the launch traced here: 467 us
  waiting for transfers between devices  174 us (37%)
  blocking collectives  122 us (26%)
  matrix products  65.2 us (14%)
  local copies, waits for them, and re-layouts  51.7 us (11%)
  other arithmetic  31 us (7%)
  between operations  14.3 us (3%)
  starting transfers between devices  7.67 us (2%)
    psum x1, waiting for transfers between devices, body(): tower_grad = lax.psum(tower_part, ('node', 'local'))  142 us
    all_to_all x1, blocking collectives, body(): lax.all_to_all(partial_grads, 'node', split_axis=1, concat_axis=1, tiled=...  56.5 us
    all_to_all x1, blocking collectives, body(): lax.all_to_all(lax.all_to_all(partial_grads, 'node', split_axis=1, concat...  54.4 us
    dot_general x4, matrix products, seq_layer(): jnp.dot(normed, w_in, preferred_element_type=jnp.float32)  33.1 us
    all_gather x1, waiting for transfers between devices, body(): lax.all_gather(fetched, 'local', axis=0, tiled=True)  26.3 us
    while x76, local copies, waits for them, and re-layouts  14.7 us
    dot_general x4, matrix products, seq_layer(): jnp.dot(gated_rows, w_out, preferred_element_type=jnp.float32)  11.7 us
    all_to_all x1, blocking collectives, body(): lax.all_to_all(embedded, 'node', split_axis=0, concat_axis=0, tiled=True)  10.8 us
  transfers between devices with their start and end apart: 3, of which 3 were waited for; matrix products, arithmetic and copies ran while one was open for 2% of the time, Pallas kernels for 0%

commit v1 on v0

v1 whole, which is shorter than its diff:
```python
import functools

import jax
import jax.numpy as jnp
from jax import lax
from jax.experimental import pallas as pl
from jax.experimental.pallas import tpu as pltpu
from jax.sharding import PartitionSpec as P

HEADS = 8
BF = jnp.bfloat16
F32 = jnp.float32
NODES = 16
LOCALS = 8
D = 1024
SLOTS = 1024
ROWS = 512
SEQ = 256
MIB = 1 << 20

VMEM = pl.BlockSpec(memory_space=pltpu.VMEM)
SMEM = pl.BlockSpec(memory_space=pltpu.SMEM)
ANY = pl.BlockSpec(memory_space=pl.ANY)


def dot(a, b):
    return jnp.dot(a, b, preferred_element_type=F32)


def dot_nt(a, b):
    return lax.dot_general(a, b, (((1,), (1,)), ((), ())), preferred_element_type=F32)


def dot_tn(a, b):
    return lax.dot_general(a, b, (((0,), (0,)), ((), ())), preferred_element_type=F32)


def sigmoid(v):
    return 0.5 + 0.5 * jnp.tanh(0.5 * v)


def slope_of(v, sigma):
    return sigma * (1.0 + v * (1.0 - sigma))


def pick_kernel(wanted, content, out):
    ids = wanted[...].reshape(128, 128)
    lane = lax.broadcasted_iota(jnp.int32, (128, 128), 1)
    hot = jnp.concatenate(
        [jnp.where(ids == lane + j * 128, 1.0, 0.0).astype(BF) for j in range(8)], axis=1
    )
    out[...] = dot(hot, content[...]).astype(BF).reshape(NODES, 8, D)


def pick(wanted, content):
    return pl.pallas_call(
        pick_kernel,
        out_shape=jax.ShapeDtypeStruct((NODES, 8, D), BF),
        in_specs=[VMEM, VMEM],
        out_specs=VMEM,
        compiler_params=pltpu.CompilerParams(vmem_limit_bytes=12 * MIB),
        cost_estimate=pl.CostEstimate(flops=2 * 128 * D * D, bytes_accessed=3 * MIB, transcendentals=0),
    )(wanted, content)


def layer_kernel(
    pos, lengths, inverse, p0, p1, p2, p3, p4, p5, p6, p7, w_tower_h, w_in_h, w_out_h, grad_h,
    events_out_h, k0, k1, k2, k3, s0, s1, s2, s3,
    table, w_tower, w_in, w_out, grad, out_buf, events, normed, hidden, slope, attn, attn_slope,
    mixed, half, dmixed, dpre, coef, inv_rms, inv_std, hot_gather, hot_scatter,
    sem_p, sem_w, sem_in, sem_out,
):
    me = pos[0]
    pieces = (p0, p1, p2, p3, p4, p5, p6, p7)
    loads = []
    for s, piece in enumerate(pieces):
        at = pl.multiple_of((me ^ s) * 128, 128)
        loads.append(pltpu.make_async_copy(piece, table.at[pl.ds(at, 128)], sem_p.at[s]))
    tower_load = pltpu.make_async_copy(w_tower_h, w_tower, sem_w.at[0])
    out_load = pltpu.make_async_copy(w_out_h, w_out, sem_w.at[1])
    grad_load = pltpu.make_async_copy(grad_h, grad, sem_w.at[2])
    in_loads = [
        pltpu.make_async_copy(
            w_in_h.at[:, pl.ds(j * D, D)], w_in.at[:, pl.ds(j * D, D)], sem_in.at[j]
        )
        for j in range(4)
    ]
    for c in loads:
        c.start()
    tower_load.start()
    for c in in_loads:
        c.start()
    out_load.start()
    grad_load.start()

    for b in range(2):
        row = inverse[b : b + 1, :]
        column = jnp.transpose(jnp.broadcast_to(row, (128, SEQ)))
        lane = lax.broadcasted_iota(jnp.int32, (SEQ, 128), 1)
        sub = lax.broadcasted_iota(jnp.int32, (128, SEQ), 0)
        for j in range(8):
            hot_gather[b * SEQ : (b + 1) * SEQ, j * 128 : (j + 1) * 128] = jnp.where(
                column == lane + j * 128, 1.0, 0.0
            ).astype(BF)
            hot_scatter[j * 128 : (j + 1) * 128, b * SEQ : (b + 1) * SEQ] = jnp.where(
                row == sub + j * 128, 1.0, 0.0
            ).astype(BF)
        length = lengths[b]
        query = lax.broadcasted_iota(jnp.int32, (SEQ, SEQ), 0)
        key = lax.broadcasted_iota(jnp.int32, (SEQ, SEQ), 1)
        share = 1.0 / jnp.full((SEQ, SEQ), length, jnp.int32).astype(F32)
        coef[b] = jnp.where((key <= query) & (query < length), share, 0.0)

    for c in loads:
        c.wait()

    @pl.loop(0, 4)
    def _(c):
        at = pl.ds(pl.multiple_of(c * 256, 256), 256)
        half[:, at] = dot(hot_gather[...], table[:, at]).astype(BF)

    tower_load.wait()

    @pl.loop(0, 4)
    def _(c):
        at = pl.ds(pl.multiple_of(c * 256, 256), 256)
        pre = dot(half[...], w_tower[:, at])
        events[:, at] = (pre * sigmoid(pre)).astype(BF)

    @pl.loop(0, 8)
    def _(i):
        at = pl.ds(pl.multiple_of(i * 64, 64), 64)
        x = events[at, :].astype(F32)
        r = lax.rsqrt(jnp.mean(x * x, axis=-1, keepdims=True) + 1e-06)
        inv_rms[at, :] = jnp.broadcast_to(r, (64, 128))
        normed[at, :] = (x * r).astype(BF)

    for j in range(4):
        in_loads[j].wait()

        @pl.loop(0, 4)
        def _(c):
            at = pl.ds(pl.multiple_of(j * D + c * 256, 256), 256)
            pre = dot(normed[...], w_in[:, at])
            sigma = sigmoid(pre)
            hidden[:, at] = (pre * sigma).astype(BF)
            slope[:, at] = slope_of(pre, sigma).astype(BF)

    scale = 128 ** (-0.5)

    @pl.loop(0, HEADS)
    def _(h):
        for b in range(2):
            rows = slice(b * SEQ, (b + 1) * SEQ)
            head = lambda base: pl.ds(pl.multiple_of(base + h * 128, 128), 128)
            scores = dot_nt(hidden[rows, head(2 * D)], hidden[rows, head(3 * D)]) * scale
            sigma = sigmoid(scores)
            share = coef[b]
            weights = (scores * sigma * share).astype(BF)
            attn[h, b] = weights
            attn_slope[h, b] = (slope_of(scores, sigma) * (share * scale)).astype(BF)
            mixed[rows, head(0)] = dot(weights, hidden[rows, head(D)])

    @pl.loop(0, 8)
    def _(i):
        at = pl.ds(pl.multiple_of(i * 64, 64), 64)
        m = mixed[at, :]
        centred = m - jnp.mean(m, axis=-1, keepdims=True)
        r = lax.rsqrt(jnp.mean(centred * centred, axis=-1, keepdims=True) + 1e-05)
        inv_std[at, :] = jnp.broadcast_to(r, (64, 128))
        normal = centred * r
        mixed[at, :] = normal
        half[at, :] = (normal * hidden[at, 0:D].astype(F32)).astype(BF)

    out_load.wait()
    grad_load.wait()

    @pl.loop(0, 4)
    def _(c):
        at = pl.ds(pl.multiple_of(c * 256, 256), 256)
        out_buf[:, at] = (events[:, at].astype(F32) + dot(half[...], w_out[:, at])).astype(BF)

    store = pltpu.make_async_copy(out_buf, events_out_h, sem_out)
    store.start()

    @pl.loop(0, 4)
    def _(c):
        at = pl.ds(pl.multiple_of(c * 256, 256), 256)
        half[:, at] = dot_nt(grad[...], w_out[at, :]).astype(BF)

    @pl.loop(0, 8)
    def _(i):
        at = pl.ds(pl.multiple_of(i * 64, 64), 64)
        dgated = half[at, :].astype(F32)
        normal = mixed[at, :]
        dgate = (dgated * normal).astype(BF).astype(F32)
        dpre[at, 0:D] = (dgate * slope[at, 0:D].astype(F32)).astype(BF)
        dnormal = dgated * hidden[at, 0:D].astype(F32)
        m1 = jnp.mean(dnormal, axis=-1, keepdims=True)
        m2 = jnp.mean(dnormal * normal, axis=-1, keepdims=True)
        dmixed[at, :] = (inv_std[at, 0:1] * (dnormal - m1 - normal * m2)).astype(BF)

    @pl.loop(0, HEADS)
    def _(h):
        for b in range(2):
            rows = slice(b * SEQ, (b + 1) * SEQ)
            head = lambda base: pl.ds(pl.multiple_of(base + h * 128, 128), 128)
            dm = dmixed[rows, head(0)]
            dw = dot_nt(dm, hidden[rows, head(D)]).astype(BF).astype(F32)
            ds = (dw * attn_slope[h, b].astype(F32)).astype(BF)
            dv = dot_tn(attn[h, b], dm)
            dq = dot(ds, hidden[rows, head(3 * D)])
            dk = dot_tn(ds, hidden[rows, head(2 * D)])
            for base, d in ((D, dv), (2 * D, dq), (3 * D, dk)):
                d = d.astype(BF).astype(F32) * slope[rows, head(base)].astype(F32)
                dpre[rows, head(base)] = d.astype(BF)

    @pl.loop(0, 4)
    def _(c):
        at = pl.ds(pl.multiple_of(c * 256, 256), 256)
        mixed[:, at] = dot_nt(dpre[...], w_in[at, :]).astype(BF).astype(F32)

    @pl.loop(0, 8)
    def _(i):
        at = pl.ds(pl.multiple_of(i * 64, 64), 64)
        dn = mixed[at, :]
        r = inv_rms[at, 0:1]
        unit = events[at, :].astype(F32) * r
        dx = r * (dn - unit * jnp.mean(dn * unit, axis=-1, keepdims=True))
        half[at, :] = (grad[at, :].astype(F32) + dx).astype(BF)

    z, core = me // 2, me % 2
    keeps, sends = (k0, k1, k2, k3), (s0, s1, s2, s3)
    for k in range(4):
        at = pl.ds(pl.multiple_of((z ^ k) * 256, 256), 256)
        got = dot(hot_scatter[...], half[:, at])
        even, odd = got[:, :128], got[:, 128:]
        keeps[k][...] = jnp.where(core == 0, even, odd).astype(BF)
        sends[k][...] = jnp.where(core == 0, odd, even).astype(BF)
    store.wait()


def layer(pos, lengths, inverse, pieces, w_tower, w_in, w_out, out_grad):
    block = jax.ShapeDtypeStruct((SLOTS, 128), BF)
    vm = pltpu.VMEM
    return pl.pallas_call(
        layer_kernel,
        out_shape=[jax.ShapeDtypeStruct((ROWS, D), BF)] + [block] * 8,
        in_specs=[SMEM, SMEM, VMEM] + [ANY] * 12,
        out_specs=[ANY] + [VMEM] * 8,
        scratch_shapes=[
            vm((SLOTS, D), BF), vm((D, D), BF), vm((D, 4 * D), BF), vm((D, D), BF), vm((ROWS, D), BF),
            vm((ROWS, D), BF), vm((ROWS, D), BF), vm((ROWS, D), BF), vm((ROWS, 4 * D), BF),
            vm((ROWS, 4 * D), BF), vm((HEADS, 2, SEQ, SEQ), BF), vm((HEADS, 2, SEQ, SEQ), BF),
            vm((ROWS, D), F32), vm((ROWS, D), BF), vm((ROWS, D), BF), vm((ROWS, 4 * D), BF),
            vm((2, SEQ, SEQ), F32), vm((ROWS, 128), F32), vm((ROWS, 128), F32),
            vm((ROWS, SLOTS), BF), vm((SLOTS, ROWS), BF),
            pltpu.SemaphoreType.DMA((8,)), pltpu.SemaphoreType.DMA((3,)),
            pltpu.SemaphoreType.DMA((4,)), pltpu.SemaphoreType.DMA,
        ],
        compiler_params=pltpu.CompilerParams(vmem_limit_bytes=52 * MIB),
        cost_estimate=pl.CostEstimate(
            flops=14 * 10**9, bytes_accessed=18 * MIB, transcendentals=4 * MIB
        ),
    )(pos, lengths, inverse, *pieces, w_tower, w_in, w_out, out_grad)


def rows_kernel(pos, p0, p1, p2, p3, p4, p5, p6, p7, w_tower_h, turned, slope, w_cols, sem):
    me = pos[0]
    load = pltpu.make_async_copy(
        w_tower_h.at[:, pl.ds(pl.multiple_of(me * 128, 128), 128)], w_cols, sem
    )
    load.start()
    load.wait()
    for s, piece in enumerate((p0, p1, p2, p3, p4, p5, p6, p7)):
        at = pl.ds(pl.multiple_of((me ^ s) * 128, 128), 128)
        rows = piece[...]
        pre = dot(rows, w_cols[...])
        slope[at, :] = slope_of(pre, sigmoid(pre))
        turned[:, at] = jnp.transpose(rows)


def rows_of(pos, pieces, w_tower):
    return pl.pallas_call(
        rows_kernel,
        out_shape=[jax.ShapeDtypeStruct((D, SLOTS), BF), jax.ShapeDtypeStruct((SLOTS, 128), F32)],
        in_specs=[SMEM] + [VMEM] * 8 + [ANY],
        out_specs=[VMEM, VMEM],
        scratch_shapes=[pltpu.VMEM((D, 128), BF), pltpu.SemaphoreType.DMA],
        compiler_params=pltpu.CompilerParams(vmem_limit_bytes=16 * MIB),
        cost_estimate=pl.CostEstimate(
            flops=2 * SLOTS * D * 128, bytes_accessed=5 * MIB, transcendentals=SLOTS * 128
        ),
    )(pos, *pieces, w_tower)


def slots_kernel(a0, a1, a2, a3, slope, turned, out):
    total = a0[...].astype(F32) + a1[...].astype(F32) + a2[...].astype(F32) + a3[...].astype(F32)
    pre = (total * slope[...]).astype(BF)
    tower = dot(turned[...], pre).reshape(NODES, LOCALS, 8, 128)
    for l in range(LOCALS):
        mine = pre[l * 128 : (l + 1) * 128].astype(F32).reshape(NODES, 8, 128)
        both = jnp.concatenate([mine, tower[:, l]], axis=1)
        out[:, l] = both.astype(BF)


def slots(a, slope, turned):
    return pl.pallas_call(
        slots_kernel,
        out_shape=jax.ShapeDtypeStruct((NODES, LOCALS, 16, 128), BF),
        in_specs=[VMEM] * 6,
        out_specs=VMEM,
        compiler_params=pltpu.CompilerParams(vmem_limit_bytes=16 * MIB),
        cost_estimate=pl.CostEstimate(
            flops=2 * SLOTS * D * 128, bytes_accessed=5 * MIB, transcendentals=0
        ),
    )(*a, slope, turned)


def total_kernel(arrived, out):
    acc = arrived[0, :, :, :].astype(F32)
    for n in range(1, NODES):
        acc = acc + arrived[n, :, :, :].astype(F32)
    row = jnp.concatenate([acc[j, 8:, :] for j in range(LOCALS)], axis=1).astype(BF)
    for n in range(NODES):
        out[n] = row


def total(arrived):
    return pl.pallas_call(
        total_kernel,
        out_shape=jax.ShapeDtypeStruct((NODES, 8, D), BF),
        in_specs=[VMEM],
        out_specs=VMEM,
        compiler_params=pltpu.CompilerParams(vmem_limit_bytes=8 * MIB),
        cost_estimate=pl.CostEstimate(flops=MIB, bytes_accessed=MIB, transcendentals=0),
    )(arrived)


def content_kernel(wanted, arrived, w_tower, out, pre):
    for n in range(NODES):
        pre[n * 8 : (n + 1) * 8, :] = jnp.concatenate(
            [arrived[n, j].astype(F32)[:8] for j in range(LOCALS)], axis=1
        )
    rows = dot_nt(pre[...].astype(BF), w_tower[...])
    high = rows.astype(BF)
    low = (rows - high.astype(F32)).astype(BF)
    ids = jnp.transpose(wanted[...].reshape(128, 128))
    sub = lax.broadcasted_iota(jnp.int32, (128, 128), 0)
    for j in range(8):
        hot = jnp.where(ids == sub + j * 128, 1.0, 0.0).astype(BF)
        out[j * 128 : (j + 1) * 128, :] = (dot(hot, high) + dot(hot, low)).astype(BF)


def content_side(wanted, arrived, w_tower):
    return pl.pallas_call(
        content_kernel,
        out_shape=jax.ShapeDtypeStruct((1024, D), BF),
        in_specs=[VMEM] * 3,
        out_specs=VMEM,
        scratch_shapes=[pltpu.VMEM((128, D), F32)],
        compiler_params=pltpu.CompilerParams(vmem_limit_bytes=16 * MIB),
        cost_estimate=pl.CostEstimate(
            flops=6 * 128 * D * D, bytes_accessed=5 * MIB, transcendentals=0
        ),
    )(wanted, arrived, w_tower)


def tower_kernel(pos, p0, p1, p2, p3, p4, p5, p6, p7, out, buf, sem):
    me = pos[0]
    copies = []
    for s, piece in enumerate((p0, p1, p2, p3, p4, p5, p6, p7)):
        buf[s] = piece[...].astype(F32)
        copies.append(pltpu.make_async_copy(buf.at[s], out.at[:, me ^ s], sem.at[s]))
        copies[-1].start()
    for c in copies:
        c.wait()


def tower_side(pos, pieces):
    return pl.pallas_call(
        tower_kernel,
        out_shape=jax.ShapeDtypeStruct((NODES, LOCALS, 8, D), F32),
        in_specs=[SMEM] + [VMEM] * 8,
        out_specs=ANY,
        scratch_shapes=[pltpu.VMEM((8, NODES, 8, D), F32), pltpu.SemaphoreType.DMA((8,))],
        compiler_params=pltpu.CompilerParams(vmem_limit_bytes=16 * MIB),
        cost_estimate=pl.CostEstimate(flops=MIB, bytes_accessed=6 * MIB, transcendentals=0),
    )(pos, *pieces)


def swap(x, s):
    return lax.ppermute(x, "local", [(i, i ^ s) for i in range(LOCALS)])


def gather_local(x):
    got = {0: x}
    for s in (4, 2, 6):
        got[s] = swap(x, s)
    for s in (0, 4, 2, 6):
        got[s + 1] = swap(got[s], 1)
    return [got[s] for s in range(LOCALS)]


def body(inverse, slot_rows, lengths, content, w_tower, w_in, w_out, out_grad):
    pos = lax.axis_index("local").astype(jnp.int32).reshape(1)
    asked = jnp.broadcast_to(slot_rows.reshape(NODES, 8, 1), (NODES, 8, 128))
    wanted = lax.all_to_all(asked, "node", 0, 0, tiled=True)
    picked = pick(wanted, content)
    fetched = lax.all_to_all(picked, "node", 0, 0, tiled=True).reshape(128, D)
    pieces = gather_local(fetched)
    events_out, *blocks = layer(
        pos, lengths, inverse, pieces, w_tower, w_in, w_out, out_grad.reshape(ROWS, D)
    )
    keep, send = blocks[:4], blocks[4:]
    turned, slope = rows_of(pos, pieces, w_tower)
    pair = {k: keep[k] + swap(send[k], 1) for k in (2, 1, 3, 0)}
    arrived = [pair[0]] + [swap(pair[k], 2 * k) for k in (2, 1, 3)]
    out = slots(arrived, slope, turned).reshape(NODES * LOCALS, 16, 128)
    back = lax.all_to_all(out, ("node", "local"), 0, 0, tiled=True).reshape(NODES, LOCALS, 16, 128)
    rows = lax.all_to_all(total(back), "node", 0, 0, tiled=True)
    tower_grad = tower_side(pos, gather_local(rows)).reshape(D, D)
    content_grad = content_side(wanted, back, w_tower)
    return (events_out.reshape(2, SEQ, D), content_grad, tower_grad)


def solution(mesh):
    in_specs = (
        P(("node", "local"), None),
        P("node", "local", None, None),
        P(("node", "local")),
        P(("node", "local"), None),
        P(),
        P(),
        P(),
        P(("node", "local"), None, None),
    )
    out_specs = (P(("node", "local"), None, None), P(("node", "local"), None), P())
    return jax.shard_map(body, mesh=mesh, in_specs=in_specs, out_specs=out_specs, check_vma=False)
```

time: 469 us -> 166 us (0.35)
  waiting for transfers between devices: 174 us -> 8.09 us
  blocking collectives: 122 us -> 53 us
  matrix products: 65.2 us -> 0 us
  Pallas kernels: 0 us -> 52.4 us
  local copies, waits for them, and re-layouts: 51.7 us -> 9.8 us
  starting transfers between devices: 7.67 us -> 40.4 us
  other arithmetic: 31 us -> 0.29 us
  between operations: 14.3 us -> 1.04 us
    psum x1 -> x0, waiting for transfers between devices: 142 us -> none  [body(): tower_grad = lax.psum(tower_part, ('node', 'local'))]
    all_to_all x3 -> x4, blocking collectives: 122 us -> 53 us  [the longest x1 18 us: body(): lax.all_to_all(out, ('node', 'local'), 0, 0, tiled=True)]
    dot_general x23 -> x0, matrix products: 65.2 us -> none  [the longest x4 33.1 us: seq_layer(): jnp.dot(normed, w_in, preferred_element_type=jnp.float32)]
    pallas_call x0 -> x7, Pallas kernels: none -> 52.4 us  [the longest x1 44.7 us: layer(): pl.pallas_call(layer_kernel, out_shape=[jax.ShapeDtypeStruct((ROWS, D), B...]
    ppermute x0 -> x21, starting transfers between devices: none -> 40.4 us  [swap(): return lax.ppermute(x, 'local', [(i, i ^ s) for i in range(LOCALS)])]
    all_gather x1 -> x0, waiting for transfers between devices: 26.3 us -> none  [body(): lax.all_gather(fetched, 'local', axis=0, tiled=True)]
    reshape x15 -> x0, local copies, waits for them, and re-layouts: 18.8 us -> none  [the longest x4 4.88 us: seq_layer(): keys = key_part.reshape(rows, HEADS, head_size)]
    while x76 -> x0, local copies, waits for them, and re-layouts: 14.7 us -> none
  transfers between devices with their start and end apart: 3 -> 21, of which waited for: 3 -> 8; matrix products, arithmetic and copies ran while one was open for 2% -> 0% of each run, Pallas kernels for 0% -> 3%
where the time goes in v1:
time: 166 us; the launch traced here: 165 us
  blocking collectives  53 us (32%)
  Pallas kernels  52.4 us (32%)
  starting transfers between devices  40.4 us (24%)
  local copies, waits for them, and re-layouts  9.8 us (6%)
  waiting for transfers between devices  8.09 us (5%)
    pallas_call x1, Pallas kernels, layer(): pl.pallas_call(layer_kernel, out_shape=[jax.ShapeDtypeStruct((ROWS, D), B...  44.7 us
    ppermute x21, starting transfers between devices, swap(): return lax.ppermute(x, 'local', [(i, i ^ s) for i in range(LOCALS)])  40.4 us
    all_to_all x1, blocking collectives, body(): lax.all_to_all(out, ('node', 'local'), 0, 0, tiled=True)  18 us
    all_to_all x1, blocking collectives, body(): wanted = lax.all_to_all(asked, 'node', 0, 0, tiled=True)  13.9 us
    all_to_all x1, blocking collectives, body(): fetched = lax.all_to_all(picked, 'node', 0, 0, tiled=True).reshape(128, D)  10.7 us
    all_to_all x1, blocking collectives, body(): rows = lax.all_to_all(total(back), 'node', 0, 0, tiled=True)  10.4 us
    unnamed x40, local copies, waits for them, and re-layouts  8.96 us
    ppermute x21, waiting for transfers between devices, swap(): return lax.ppermute(x, 'local', [(i, i ^ s) for i in range(LOCALS)])  8.09 us
  transfers between devices with their start and end apart: 21, of which 8 were waited for; matrix products, arithmetic and copies ran while one was open for 0% of the time, Pallas kernels for 3%

profile of v1, /device:TPU:1, one launch (start us, length us, event | category | flops | bytes accessed | tf_op | source)
XLA Modules:
  0.0 165.0 jit_solution(16334921930527696235)
XLA Ops:
  1.5 13.9 %all_to_all.20.wanted = s32[16,8,128]{2,1,0:T(8,128)S(1)} all-to-all(s32[16,8,128]{2,1,0:T(8,128)S(1)} %broadcast_in_dim.8), channel_id=1, replica_groups=mesh['node'=16,'local'=8] {'node'}, dimensions={0} | all-to-all | bytes 131072 | tf_op jit(solution)/shard_map/all_to_all | solution.py:408
  15.4 1.6 copy-done.1
  17.4 10.7 %all_to_all.21 = bf16[16,8,1024]{2,1,0:T(8,128)(2,1)S(1)} all-to-all(bf16[16,8,1024]{2,1,0:T(8,128)(2,1)S(1)} %shard_map.103), channel_id=1, replica_groups=mesh['node'=16,'local'=8] {'node'}, dimensions={0} | all-to-all | bytes 524288 | tf_op jit(solution)/shard_map/all_to_all | solution.py:410
  28.1 1.6 collective-permute-start.1
  29.8 3.3 %collective-permute-start.3 = (bf16[128,1024]{1,0:T(8,128)(2,1)S(1)}, bf16[128,1024]{1,0:T(8,128)(2,1)S(1)}, u32[]{:S(2)}, u32[]{:S(2)}) collective-permute-start(bf16[128,1024]{1,0:T(8,128)(2,1)S(1)} %bitcast.12), channel_id=1, source_target_pairs={{0,4},{1,5},{2,6},{3,7},{4,0},{5,1},{6,2},{7,3},{8,12},{9,13},{10,... | collective-permute-start | bytes 786440 | tf_op jit(solution)/shard_map/ppermute | solution.py:393
  33.1 3.8 %collective-permute-start = (bf16[128,1024]{1,0:T(8,128)(2,1)S(1)}, bf16[128,1024]{1,0:T(8,128)(2,1)S(1)}, u32[]{:S(2)}, u32[]{:S(2)}) collective-permute-start(bf16[128,1024]{1,0:T(8,128)(2,1)S(1)} %bitcast.14), channel_id=1, source_target_pairs={{0,1},{1,0},{2,3},{3,2},{4,5},{5,4},{6,7},{7,6},{8,9},{9,8},{10,11... | collective-permute-start | bytes 786440 | tf_op jit(solution)/shard_map/ppermute | solution.py:393
  36.9 3.0 %collective-permute-start.2 = (bf16[128,1024]{1,0:T(8,128)(2,1)S(1)}, bf16[128,1024]{1,0:T(8,128)(2,1)S(1)}, u32[]{:S(2)}, u32[]{:S(2)}) collective-permute-start(bf16[128,1024]{1,0:T(8,128)(2,1)S(1)} %collective-permute-done.1.p2), channel_id=1, source_target_pairs={{0,1},{1,0},{2,3},{3,2},{4,5},{5,4},{6,7},{7,6},{8,9},{9,8},{10,11... | collective-permute-start | bytes 786440 | tf_op jit(solution)/shard_map/ppermute | solution.py:393
  39.9 1.7 %collective-permute-done.3.p4 = bf16[128,1024]{1,0:T(8,128)(2,1)S(1)} collective-permute-done((bf16[128,1024]{1,0:T(8,128)(2,1)S(1)}, bf16[128,1024]{1,0:T(8,128)(2,1)S(1)}, u32[]{:S(2)}, u32[]{:S(2)}) %collective-permute-start.3) | collective-permute-done | bytes 262176 | tf_op jit(solution)/shard_map/ppermute | solution.py:393
  41.5 4.5 %collective-permute-start.4 = (bf16[128,1024]{1,0:T(8,128)(2,1)S(1)}, bf16[128,1024]{1,0:T(8,128)(2,1)S(1)}, u32[]{:S(2)}, u32[]{:S(2)}) collective-permute-start(bf16[128,1024]{1,0:T(8,128)(2,1)S(1)} %collective-permute-done.3.p4), channel_id=1, source_target_pairs={{0,1},{1,0},{2,3},{3,2},{4,5},{5,4},{6,7},{7,6},{8,9},{9,8},{10,11... | collective-permute-start | bytes 786440 | tf_op jit(solution)/shard_map/ppermute | solution.py:393
  46.4 2.2 %collective-permute-start.6 = (bf16[128,1024]{1,0:T(8,128)(2,1)S(1)}, bf16[128,1024]{1,0:T(8,128)(2,1)S(1)}, u32[]{:S(2)}, u32[]{:S(2)}) collective-permute-start(bf16[128,1024]{1,0:T(8,128)(2,1)S(1)} %collective-permute-done.5.p6), channel_id=1, source_target_pairs={{0,1},{1,0},{2,3},{3,2},{4,5},{5,4},{6,7},{7,6},{8,9},{9,8},{10,11... | collective-permute-start | bytes 786440 | tf_op jit(solution)/shard_map/ppermute | solution.py:393
  48.7 1.1 collective-permute-done.6.p7
  50.5 44.7 %shard_map.104 = (bf16[512,1024]{1,0:T(8,128)(2,1)}, bf16[1024,128]{1,0:T(8,128)(2,1)S(1)}, bf16[1024,128]{1,0:T(8,128)(2,1)S(1)}, bf16[1024,128]{1,0:T(8,128)(2...) custom-call(s32[1]{0:T(128)} %bitcast.pos, ...), custom_call_target="tpu_custom_call" | custom-call | flops 14000000000 | bytes 18874368 | tf_op jit(solution)/shard_map/pallas_call | solution.py:246
  97.7 3.9 %collective-permute-start.9 = (bf16[1024,128]{1,0:T(8,128)(2,1)S(1)}, bf16[1024,128]{1,0:T(8,128)(2,1)S(1)}, u32[]{:S(2)}, u32[]{:S(2)}) collective-permute-start(bf16[1024,128]{1,0:T(8,128)(2,1)S(1)} %add.13), channel_id=1, source_target_pairs={{0,4},{1,5},{2,6},{3,7},{4,0},{5,1},{6,2},{7,3},{8,12},{9,13},{10,... | collective-permute-start | bytes 786440 | tf_op jit(solution)/shard_map/ppermute | solution.py:393
  109.4 3.3 %collective-permute-done.9.a1 = bf16[1024,128]{1,0:T(8,128)(2,1)S(1)} collective-permute-done((bf16[1024,128]{1,0:T(8,128)(2,1)S(1)}, bf16[1024,128]{1,0:T(8,128)(2,1)S(1)}, u32[]{:S(2)}, u32[]{:S(2)}) %collective-permute-start.9) | collective-permute-done | bytes 262176 | tf_op jit(solution)/shard_map/ppermute | solution.py:393
  113.4 18.0 %all_to_all.22 = bf16[128,16,128]{2,1,0:T(8,128)(2,1)S(1)} all-to-all(bf16[128,16,128]{2,1,0:T(8,128)(2,1)S(1)} %bitcast.10), channel_id=1, replica_groups=mesh['node'=16,'local'=8] {'node','local'}, dimensions={0} | all-to-all | bytes 1048576 | tf_op jit(solution)/shard_map/all_to_all | solution.py:420
  131.5 10.4 %all_to_all.23.p0 = bf16[16,8,1024]{2,1,0:T(8,128)(2,1)S(1)} all-to-all(bf16[16,8,1024]{2,1,0:T(8,128)(2,1)S(1)} %shard_map.108), channel_id=1, replica_groups=mesh['node'=16,'local'=8] {'node'}, dimensions={0} | all-to-all | bytes 524288 | tf_op jit(solution)/shard_map/all_to_all | solution.py:421
  141.9 1.1 collective-permute-start.15
  143.8 2.0 %collective-permute-start.19 = (bf16[16,8,1024]{2,1,0:T(8,128)(2,1)S(1)}, bf16[16,8,1024]{2,1,0:T(8,128)(2,1)S(1)}, u32[]{:S(2)}, u32[]{:S(2)}) collective-permute-start(bf16[16,8,1024]{2,1,0:T(8,128)(2,1)S(1)} %all_to_all.23.p0), channel_id=1, source_target_pairs={{0,6},{1,7},{2,4},{3,5},{4,2},{5,3},{6,0},{7,1},{8,14},{9,15},{10,... | collective-permute-start | bytes 786440 | tf_op jit(solution)/shard_map/ppermute | solution.py:393
  145.8 2.9 %collective-permute-start.14 = (bf16[16,8,1024]{2,1,0:T(8,128)(2,1)S(1)}, bf16[16,8,1024]{2,1,0:T(8,128)(2,1)S(1)}, u32[]{:S(2)}, u32[]{:S(2)}) collective-permute-start(bf16[16,8,1024]{2,1,0:T(8,128)(2,1)S(1)} %all_to_all.23.p0), channel_id=1, source_target_pairs={{0,1},{1,0},{2,3},{3,2},{4,5},{5,4},{6,7},{7,6},{8,9},{9,8},{10,11... | collective-permute-start | bytes 786440 | tf_op jit(solution)/shard_map/ppermute | solution.py:393
  148.7 4.5 %collective-permute-start.16 = (bf16[16,8,1024]{2,1,0:T(8,128)(2,1)S(1)}, bf16[16,8,1024]{2,1,0:T(8,128)(2,1)S(1)}, u32[]{:S(2)}, u32[]{:S(2)}) collective-permute-start(bf16[16,8,1024]{2,1,0:T(8,128)(2,1)S(1)} %collective-permute-done.15.p2), channel_id=1, source_target_pairs={{0,1},{1,0},{2,3},{3,2},{4,5},{5,4},{6,7},{7,6},{8,9},{9,8},{10,11... | collective-permute-start | bytes 786440 | tf_op jit(solution)/shard_map/ppermute | solution.py:393
  153.5 3.3 %collective-permute-start.18 = (bf16[16,8,1024]{2,1,0:T(8,128)(2,1)S(1)}, bf16[16,8,1024]{2,1,0:T(8,128)(2,1)S(1)}, u32[]{:S(2)}, u32[]{:S(2)}) collective-permute-start(bf16[16,8,1024]{2,1,0:T(8,128)(2,1)S(1)} %collective-permute-done.17.p4), channel_id=1, source_target_pairs={{0,1},{1,0},{2,3},{3,2},{4,5},{5,4},{6,7},{7,6},{8,9},{9,8},{10,11... | collective-permute-start | bytes 786440 | tf_op jit(solution)/shard_map/ppermute | solution.py:393
  157.2 2.2 %collective-permute-start.20 = (bf16[16,8,1024]{2,1,0:T(8,128)(2,1)S(1)}, bf16[16,8,1024]{2,1,0:T(8,128)(2,1)S(1)}, u32[]{:S(2)}, u32[]{:S(2)}) collective-permute-start(bf16[16,8,1024]{2,1,0:T(8,128)(2,1)S(1)} %collective-permute-done.19.p6), channel_id=1, source_target_pairs={{0,1},{1,0},{2,3},{3,2},{4,5},{5,4},{6,7},{7,6},{8,9},{9,8},{10,11... | collective-permute-start | bytes 786440 | tf_op jit(solution)/shard_map/ppermute | solution.py:393
  159.4 3.3 %shard_map.107 = bf16[1024,1024]{1,0:T(8,128)(2,1)} custom-call(s32[16,8,128]{2,1,0:T(8,128)S(1)} %all_to_all.20.wanted, bf16[16,8,16,128]{3,2,1,0:T(8,128)(2,1)S(1)} %bitcast.9, bf16[1024,1024]{1,0:T(8,128)(2,1)S(1)} %copy-done), custom_call_target="tpu_custom_call" | custom-call | flops 805306368 | bytes 5242880 | tf_op jit(solution)/shard_map/pallas_call | solution.py:356
  162.7 2.1 %shard_map.109 = f32[16,8,8,1024]{3,2,1,0:T(8,128)} custom-call(s32[1]{0:T(128)} %bitcast.pos, bf16[16,8,1024]{2,1,0:T(8,128)(2,1)S(1)} %all_to_all.23.p0, bf16[16,8,1024]{2,1,0:T(8,128)(2,1)S(1)} %collective-permute-done.14.p1, bf16[16,8,1024]{2,1,0:T(8,128)(2,1)S(1)} %collective-permute-done.15.p2, bf16[16,8,1024]{2,1,0:T(8,128)(2,1)S(1)} %collective-permute-done.16.p3, ...), custom_call_target="tpu_custom_call" | custom-call | flops 1048576 | bytes 6291456 | tf_op jit(solution)/shard_map/pallas_call | solution.py:381
  (75 shorter events, 14.8 us)
Async XLA Ops:
  0.6 49.9 %copy-start.19 = (s32[2]{0:T(128)S(1)}, s32[2]{0:T(128)}, u32[]{:S(2)}) copy-start(s32[2]{0:T(128)} %lengths.1) | copy-start | bytes 28
  0.6 49.9 %copy-start.18 = (s32[2,256]{1,0:T(2,128)S(1)}, s32[2,256]{1,0:T(2,128)}, u32[]{:S(2)}) copy-start(s32[2,256]{1,0:T(2,128)} %inverse.1) | copy-start | bytes 6148
  28.1 21.7 %copy-start.2 = (bf16[16,8,1024]{2,1,0:T(8,128)(2,1)}, bf16[16,8,1024]{2,1,0:T(8,128)(2,1)S(1)}, u32[]{:S(2)}) copy-start(bf16[16,8,1024]{2,1,0:T(8,128)(2,1)S(1)} %all_to_all.21) | copy-start | bytes 786436
  28.1 8.8 %collective-permute-start.1 = (bf16[128,1024]{1,0:T(8,128)(2,1)S(1)}, bf16[128,1024]{1,0:T(8,128)(2,1)S(1)}, u32[]{:S(2)}, u32[]{:S(2)}) collective-permute-start(bf16[128,1024]{1,0:T(8,128)(2,1)S(1)} %bitcast.11), channel_id=1, source_target_pairs={{0,2},{1,3},{2,0},{3,1},{4,6},{5,7},{6,4},{7,5},{8,10},{9,11},{10,... | collective-permute-start | bytes 786440 | tf_op jit(solution)/shard_map/ppermute | solution.py:393
  29.8 11.7 %collective-permute-start.3 = (bf16[128,1024]{1,0:T(8,128)(2,1)S(1)}, bf16[128,1024]{1,0:T(8,128)(2,1)S(1)}, u32[]{:S(2)}, u32[]{:S(2)}) collective-permute-start(bf16[128,1024]{1,0:T(8,128)(2,1)S(1)} %bitcast.12), channel_id=1, source_target_pairs={{0,4},{1,5},{2,6},{3,7},{4,0},{5,1},{6,2},{7,3},{8,12},{9,13},{10,... | collective-permute-start | bytes 786440 | tf_op jit(solution)/shard_map/ppermute | solution.py:393
  33.1 13.4 %collective-permute-start.5 = (bf16[128,1024]{1,0:T(8,128)(2,1)S(1)}, bf16[128,1024]{1,0:T(8,128)(2,1)S(1)}, u32[]{:S(2)}, u32[]{:S(2)}) collective-permute-start(bf16[128,1024]{1,0:T(8,128)(2,1)S(1)} %bitcast.13), channel_id=1, source_target_pairs={{0,6},{1,7},{2,4},{3,5},{4,2},{5,3},{6,0},{7,1},{8,14},{9,15},{10,... | collective-permute-start | bytes 786440 | tf_op jit(solution)/shard_map/ppermute | solution.py:393
  33.1 15.6 %collective-permute-start = (bf16[128,1024]{1,0:T(8,128)(2,1)S(1)}, bf16[128,1024]{1,0:T(8,128)(2,1)S(1)}, u32[]{:S(2)}, u32[]{:S(2)}) collective-permute-start(bf16[128,1024]{1,0:T(8,128)(2,1)S(1)} %bitcast.14), channel_id=1, source_target_pairs={{0,1},{1,0},{2,3},{3,2},{4,5},{5,4},{6,7},{7,6},{8,9},{9,8},{10,11... | collective-permute-start | bytes 786440 | tf_op jit(solution)/shard_map/ppermute | solution.py:393
  36.9 11.8 %collective-permute-start.2 = (bf16[128,1024]{1,0:T(8,128)(2,1)S(1)}, bf16[128,1024]{1,0:T(8,128)(2,1)S(1)}, u32[]{:S(2)}, u32[]{:S(2)}) collective-permute-start(bf16[128,1024]{1,0:T(8,128)(2,1)S(1)} %collective-permute-done.1.p2), channel_id=1, source_target_pairs={{0,1},{1,0},{2,3},{3,2},{4,5},{5,4},{6,7},{7,6},{8,9},{9,8},{10,11... | collective-permute-start | bytes 786440 | tf_op jit(solution)/shard_map/ppermute | solution.py:393
  41.5 7.1 %collective-permute-start.4 = (bf16[128,1024]{1,0:T(8,128)(2,1)S(1)}, bf16[128,1024]{1,0:T(8,128)(2,1)S(1)}, u32[]{:S(2)}, u32[]{:S(2)}) collective-permute-start(bf16[128,1024]{1,0:T(8,128)(2,1)S(1)} %collective-permute-done.3.p4), channel_id=1, source_target_pairs={{0,1},{1,0},{2,3},{3,2},{4,5},{5,4},{6,7},{7,6},{8,9},{9,8},{10,11... | collective-permute-start | bytes 786440 | tf_op jit(solution)/shard_map/ppermute | solution.py:393
  46.4 3.4 %collective-permute-start.6 = (bf16[128,1024]{1,0:T(8,128)(2,1)S(1)}, bf16[128,1024]{1,0:T(8,128)(2,1)S(1)}, u32[]{:S(2)}, u32[]{:S(2)}) collective-permute-start(bf16[128,1024]{1,0:T(8,128)(2,1)S(1)} %collective-permute-done.5.p6), channel_id=1, source_target_pairs={{0,1},{1,0},{2,3},{3,2},{4,5},{5,4},{6,7},{7,6},{8,9},{9,8},{10,11... | collective-permute-start | bytes 786440 | tf_op jit(solution)/shard_map/ppermute | solution.py:393
  95.3 1.8 %collective-permute-start.12 = (bf16[1024,128]{1,0:T(8,128)(2,1)}, bf16[1024,128]{1,0:T(8,128)(2,1)S(1)}, u32[]{:S(2)}, u32[]{:S(2)}) collective-permute-start(bf16[1024,128]{1,0:T(8,128)(2,1)} %get-tuple-element.22), channel_id=1, source_target_pairs={{0,1},{1,0},{2,3},{3,2},{4,5},{5,4},{6,7},{7,6},{8,9},{9,8},{10,11... | collective-permute-start | bytes 786440 | tf_op jit(solution)/shard_map/ppermute | solution.py:393
  95.7 1.5 collective-permute-start.10
  95.9 1.8 %collective-permute-start.8 = (bf16[1024,128]{1,0:T(8,128)(2,1)S(1)}, bf16[1024,128]{1,0:T(8,128)(2,1)S(1)}, u32[]{:S(2)}, u32[]{:S(2)}) collective-permute-start(bf16[1024,128]{1,0:T(8,128)(2,1)S(1)} %get-tuple-element.18), channel_id=1, source_target_pairs={{0,1},{1,0},{2,3},{3,2},{4,5},{5,4},{6,7},{7,6},{8,9},{9,8},{10,11... | collective-permute-start | bytes 786440 | tf_op jit(solution)/shard_map/ppermute | solution.py:393
  96.3 13.0 %collective-permute-start.7 = (bf16[1024,128]{1,0:T(8,128)(2,1)S(1)}, bf16[1024,128]{1,0:T(8,128)(2,1)S(1)}, u32[]{:S(2)}, u32[]{:S(2)}) collective-permute-start(bf16[1024,128]{1,0:T(8,128)(2,1)S(1)} %get-tuple-element.16), channel_id=1, source_target_pairs={{0,1},{1,0},{2,3},{3,2},{4,5},{5,4},{6,7},{7,6},{8,9},{9,8},{10,11... | collective-permute-start | bytes 786440 | tf_op jit(solution)/shard_map/ppermute | solution.py:393
  97.2 12.1 %collective-permute-start.13 = (bf16[1024,128]{1,0:T(8,128)(2,1)S(1)}, bf16[1024,128]{1,0:T(8,128)(2,1)S(1)}, u32[]{:S(2)}, u32[]{:S(2)}) collective-permute-start(bf16[1024,128]{1,0:T(8,128)(2,1)S(1)} %add.15), channel_id=1, source_target_pairs={{0,6},{1,7},{2,4},{3,5},{4,2},{5,3},{6,0},{7,1},{8,14},{9,15},{10,... | collective-permute-start | bytes 786440 | tf_op jit(solution)/shard_map/ppermute | solution.py:393
  97.4 12.0 %collective-permute-start.11 = (bf16[1024,128]{1,0:T(8,128)(2,1)S(1)}, bf16[1024,128]{1,0:T(8,128)(2,1)S(1)}, u32[]{:S(2)}, u32[]{:S(2)}) collective-permute-start(bf16[1024,128]{1,0:T(8,128)(2,1)S(1)} %add.14), channel_id=1, source_target_pairs={{0,2},{1,3},{2,0},{3,1},{4,6},{5,7},{6,4},{7,5},{8,10},{9,11},{10,... | collective-permute-start | bytes 786440 | tf_op jit(solution)/shard_map/ppermute | solution.py:393
  97.7 14.9 %collective-permute-start.9 = (bf16[1024,128]{1,0:T(8,128)(2,1)S(1)}, bf16[1024,128]{1,0:T(8,128)(2,1)S(1)}, u32[]{:S(2)}, u32[]{:S(2)}) collective-permute-start(bf16[1024,128]{1,0:T(8,128)(2,1)S(1)} %add.13), channel_id=1, source_target_pairs={{0,4},{1,5},{2,6},{3,7},{4,0},{5,1},{6,2},{7,3},{8,12},{9,13},{10,... | collective-permute-start | bytes 786440 | tf_op jit(solution)/shard_map/ppermute | solution.py:393
  141.9 6.8 %collective-permute-start.15 = (bf16[16,8,1024]{2,1,0:T(8,128)(2,1)S(1)}, bf16[16,8,1024]{2,1,0:T(8,128)(2,1)S(1)}, u32[]{:S(2)}, u32[]{:S(2)}) collective-permute-start(bf16[16,8,1024]{2,1,0:T(8,128)(2,1)S(1)} %all_to_all.23.p0), channel_id=1, source_target_pairs={{0,2},{1,3},{2,0},{3,1},{4,6},{5,7},{6,4},{7,5},{8,10},{9,11},{10,... | collective-permute-start | bytes 786440 | tf_op jit(solution)/shard_map/ppermute | solution.py:393
  143.0 10.5 %collective-permute-start.17 = (bf16[16,8,1024]{2,1,0:T(8,128)(2,1)S(1)}, bf16[16,8,1024]{2,1,0:T(8,128)(2,1)S(1)}, u32[]{:S(2)}, u32[]{:S(2)}) collective-permute-start(bf16[16,8,1024]{2,1,0:T(8,128)(2,1)S(1)} %all_to_all.23.p0), channel_id=1, source_target_pairs={{0,4},{1,5},{2,6},{3,7},{4,0},{5,1},{6,2},{7,3},{8,12},{9,13},{10,... | collective-permute-start | bytes 786440 | tf_op jit(solution)/shard_map/ppermute | solution.py:393
  143.8 13.4 %collective-permute-start.19 = (bf16[16,8,1024]{2,1,0:T(8,128)(2,1)S(1)}, bf16[16,8,1024]{2,1,0:T(8,128)(2,1)S(1)}, u32[]{:S(2)}, u32[]{:S(2)}) collective-permute-start(bf16[16,8,1024]{2,1,0:T(8,128)(2,1)S(1)} %all_to_all.23.p0), channel_id=1, source_target_pairs={{0,6},{1,7},{2,4},{3,5},{4,2},{5,3},{6,0},{7,1},{8,14},{9,15},{10,... | collective-permute-start | bytes 786440 | tf_op jit(solution)/shard_map/ppermute | solution.py:393
  145.8 16.9 %collective-permute-start.14 = (bf16[16,8,1024]{2,1,0:T(8,128)(2,1)S(1)}, bf16[16,8,1024]{2,1,0:T(8,128)(2,1)S(1)}, u32[]{:S(2)}, u32[]{:S(2)}) collective-permute-start(bf16[16,8,1024]{2,1,0:T(8,128)(2,1)S(1)} %all_to_all.23.p0), channel_id=1, source_target_pairs={{0,1},{1,0},{2,3},{3,2},{4,5},{5,4},{6,7},{7,6},{8,9},{9,8},{10,11... | collective-permute-start | bytes 786440 | tf_op jit(solution)/shard_map/ppermute | solution.py:393
  148.7 14.0 %collective-permute-start.16 = (bf16[16,8,1024]{2,1,0:T(8,128)(2,1)S(1)}, bf16[16,8,1024]{2,1,0:T(8,128)(2,1)S(1)}, u32[]{:S(2)}, u32[]{:S(2)}) collective-permute-start(bf16[16,8,1024]{2,1,0:T(8,128)(2,1)S(1)} %collective-permute-done.15.p2), channel_id=1, source_target_pairs={{0,1},{1,0},{2,3},{3,2},{4,5},{5,4},{6,7},{7,6},{8,9},{9,8},{10,11... | collective-permute-start | bytes 786440 | tf_op jit(solution)/shard_map/ppermute | solution.py:393
  153.5 9.2 %collective-permute-start.18 = (bf16[16,8,1024]{2,1,0:T(8,128)(2,1)S(1)}, bf16[16,8,1024]{2,1,0:T(8,128)(2,1)S(1)}, u32[]{:S(2)}, u32[]{:S(2)}) collective-permute-start(bf16[16,8,1024]{2,1,0:T(8,128)(2,1)S(1)} %collective-permute-done.17.p4), channel_id=1, source_target_pairs={{0,1},{1,0},{2,3},{3,2},{4,5},{5,4},{6,7},{7,6},{8,9},{9,8},{10,11... | collective-permute-start | bytes 786440 | tf_op jit(solution)/shard_map/ppermute | solution.py:393
  157.2 5.5 %collective-permute-start.20 = (bf16[16,8,1024]{2,1,0:T(8,128)(2,1)S(1)}, bf16[16,8,1024]{2,1,0:T(8,128)(2,1)S(1)}, u32[]{:S(2)}, u32[]{:S(2)}) collective-permute-start(bf16[16,8,1024]{2,1,0:T(8,128)(2,1)S(1)} %collective-permute-done.19.p6), channel_id=1, source_target_pairs={{0,1},{1,0},{2,3},{3,2},{4,5},{5,4},{6,7},{7,6},{8,9},{9,8},{10,11... | collective-permute-start | bytes 786440 | tf_op jit(solution)/shard_map/ppermute | solution.py:393
  (17 other events, 49.8 us)

commit v2 on v1

--- a/solution.py
+++ b/solution.py
@@ -67,15 +67,10 @@
     pos, lengths, inverse, p0, p1, p2, p3, p4, p5, p6, p7, w_tower_h, w_in_h, w_out_h, grad_h,
     events_out_h, k0, k1, k2, k3, s0, s1, s2, s3,
     table, w_tower, w_in, w_out, grad, out_buf, events, normed, hidden, slope, attn, attn_slope,
-    mixed, half, dmixed, dpre, coef, inv_rms, inv_std, hot_gather, hot_scatter,
-    sem_p, sem_w, sem_in, sem_out,
+    mixed, half, dgated, dmixed, dpre, coef, inv_rms, inv_std, hot_gather, hot_scatter, pre_a, pre_b,
+    sem_w, sem_in, sem_out,
 ):
     me = pos[0]
-    pieces = (p0, p1, p2, p3, p4, p5, p6, p7)
-    loads = []
-    for s, piece in enumerate(pieces):
-        at = pl.multiple_of((me ^ s) * 128, 128)
-        loads.append(pltpu.make_async_copy(piece, table.at[pl.ds(at, 128)], sem_p.at[s]))
     tower_load = pltpu.make_async_copy(w_tower_h, w_tower, sem_w.at[0])
     out_load = pltpu.make_async_copy(w_out_h, w_out, sem_w.at[1])
     grad_load = pltpu.make_async_copy(grad_h, grad, sem_w.at[2])
@@ -85,13 +80,11 @@
         )
         for j in range(4)
     ]
-    for c in loads:
-        c.start()
     tower_load.start()
     for c in in_loads:
         c.start()
-    out_load.start()
-    grad_load.start()
+    for s, piece in enumerate((p0, p1, p2, p3, p4, p5, p6, p7)):
+        table[pl.ds(pl.multiple_of((me ^ s) * 128, 128), 128), :] = piece[...]
 
     for b in range(2):
         row = inverse[b : b + 1, :]
@@ -108,26 +101,26 @@
         length = lengths[b]
         query = lax.broadcasted_iota(jnp.int32, (SEQ, SEQ), 0)
         key = lax.broadcasted_iota(jnp.int32, (SEQ, SEQ), 1)
-        share = 1.0 / jnp.full((SEQ, SEQ), length, jnp.int32).astype(F32)
+        share = (0.5 * 128 ** (-0.5)) / jnp.full((SEQ, SEQ), length, jnp.int32).astype(F32)
         coef[b] = jnp.where((key <= query) & (query < length), share, 0.0)
 
-    for c in loads:
-        c.wait()
-
-    @pl.loop(0, 4)
+    @pl.loop(0, 2)
     def _(c):
-        at = pl.ds(pl.multiple_of(c * 256, 256), 256)
+        at = pl.ds(pl.multiple_of(c * 512, 512), 512)
         half[:, at] = dot(hot_gather[...], table[:, at]).astype(BF)
 
     tower_load.wait()
 
-    @pl.loop(0, 4)
+    @pl.loop(0, 2)
     def _(c):
-        at = pl.ds(pl.multiple_of(c * 256, 256), 256)
+        at = pl.ds(pl.multiple_of(c * 512, 512), 512)
         pre = dot(half[...], w_tower[:, at])
         events[:, at] = (pre * sigmoid(pre)).astype(BF)
 
-    @pl.loop(0, 8)
+    out_load.start()
+    grad_load.start()
+
+    @pl.loop(0, 8, unroll=2)
     def _(i):
         at = pl.ds(pl.multiple_of(i * 64, 64), 64)
         x = events[at, :].astype(F32)
@@ -135,33 +128,65 @@
         inv_rms[at, :] = jnp.broadcast_to(r, (64, 128))
         normed[at, :] = (x * r).astype(BF)
 
-    for j in range(4):
-        in_loads[j].wait()
-
-        @pl.loop(0, 4)
-        def _(c):
-            at = pl.ds(pl.multiple_of(j * D + c * 256, 256), 256)
-            pre = dot(normed[...], w_in[:, at])
-            sigma = sigmoid(pre)
-            hidden[:, at] = (pre * sigma).astype(BF)
-            slope[:, at] = slope_of(pre, sigma).astype(BF)
+    def product(c, into):
+        into[...] = dot(normed[...], w_in[:, pl.ds(pl.multiple_of(c * 256, 256), 256)])
+
+    def activate(c, source):
+        at = pl.ds(pl.multiple_of(c * 256, 256), 256)
+        pre = source[...]
+        sigma = sigmoid(pre)
+        act = pre * sigma
+        hidden[:, at] = act.astype(BF)
+        slope[:, at] = (sigma + act * (1.0 - sigma)).astype(BF)
+
+    in_loads[0].wait()
+    in_loads[1].wait()
+    product(0, pre_a)
+    for j in range(2):
+
+        @pl.loop(4 * j, 4 * j + 3 + j)
+        def _(i):
+            product(2 * i + 1, pre_b)
+            activate(2 * i, pre_a)
+            product(jnp.minimum(2 * i + 2, 15), pre_a)
+            activate(2 * i + 1, pre_b)
+
+        if j == 0:
+            in_loads[2].wait()
+            in_loads[3].wait()
+            product(7, pre_b)
+            activate(6, pre_a)
+            product(8, pre_a)
+            activate(7, pre_b)
 
     scale = 128 ** (-0.5)
-
-    @pl.loop(0, HEADS)
-    def _(h):
-        for b in range(2):
-            rows = slice(b * SEQ, (b + 1) * SEQ)
-            head = lambda base: pl.ds(pl.multiple_of(base + h * 128, 128), 128)
-            scores = dot_nt(hidden[rows, head(2 * D)], hidden[rows, head(3 * D)]) * scale
-            sigma = sigmoid(scores)
+    out_load.wait()
+    grad_load.wait()
+
+    @pl.loop(0, HEADS // 2)
+    def _(i):
+        jobs = [(2 * i + k, b, slice(b * SEQ, (b + 1) * SEQ)) for k in range(2) for b in range(2)]
+        head = lambda h, base: pl.ds(pl.multiple_of(base + h * 128, 128), 128)
+        score = lambda h, b, rows: dot_nt(
+            hidden[rows, head(h, 2 * D)], hidden[rows, head(h, 3 * D)]
+        )
+        raw = score(*jobs[0])
+        for j, (h, b, rows) in enumerate(jobs):
+            later = score(*jobs[j + 1]) if j < 3 else None
+            turn = jnp.tanh(raw * (0.5 * scale))
             share = coef[b]
-            weights = (scores * sigma * share).astype(BF)
-            attn[h, b] = weights
-            attn_slope[h, b] = (slope_of(scores, sigma) * (share * scale)).astype(BF)
-            mixed[rows, head(0)] = dot(weights, hidden[rows, head(D)])
-
-    @pl.loop(0, 8)
+            part = share + share * turn
+            weights = raw * part
+            attn[h, b] = weights.astype(BF)
+            rest = (0.5 * scale) - (0.5 * scale) * turn
+            attn_slope[h, b] = (part + weights * rest).astype(BF)
+            raw = later
+        for h, b, rows in jobs:
+            mixed[rows, head(h, 0)] = dot(attn[h, b], hidden[rows, head(h, D)])
+        at = pl.ds(pl.multiple_of(i * 256, 256), 256)
+        dgated[:, at] = dot_nt(grad[...], w_out[at, :]).astype(BF)
+
+    @pl.loop(0, 8, unroll=2)
     def _(i):
         at = pl.ds(pl.multiple_of(i * 64, 64), 64)
         m = mixed[at, :]
@@ -172,55 +197,49 @@
         mixed[at, :] = normal
         half[at, :] = (normal * hidden[at, 0:D].astype(F32)).astype(BF)
 
-    out_load.wait()
-    grad_load.wait()
-
-    @pl.loop(0, 4)
-    def _(c):
-        at = pl.ds(pl.multiple_of(c * 256, 256), 256)
-        out_buf[:, at] = (events[:, at].astype(F32) + dot(half[...], w_out[:, at])).astype(BF)
-
-    store = pltpu.make_async_copy(out_buf, events_out_h, sem_out)
-    store.start()
-
-    @pl.loop(0, 4)
-    def _(c):
-        at = pl.ds(pl.multiple_of(c * 256, 256), 256)
-        half[:, at] = dot_nt(grad[...], w_out[at, :]).astype(BF)
-
-    @pl.loop(0, 8)
+    @pl.loop(0, 8, unroll=2)
     def _(i):
         at = pl.ds(pl.multiple_of(i * 64, 64), 64)
-        dgated = half[at, :].astype(F32)
+        dg = dgated[at, :].astype(F32)
         normal = mixed[at, :]
-        dgate = (dgated * normal).astype(BF).astype(F32)
+        dgate = (dg * normal).astype(BF).astype(F32)
         dpre[at, 0:D] = (dgate * slope[at, 0:D].astype(F32)).astype(BF)
-        dnormal = dgated * hidden[at, 0:D].astype(F32)
+        dnormal = dg * hidden[at, 0:D].astype(F32)
         m1 = jnp.mean(dnormal, axis=-1, keepdims=True)
         m2 = jnp.mean(dnormal * normal, axis=-1, keepdims=True)
         dmixed[at, :] = (inv_std[at, 0:1] * (dnormal - m1 - normal * m2)).astype(BF)
 
-    @pl.loop(0, HEADS)
-    def _(h):
-        for b in range(2):
-            rows = slice(b * SEQ, (b + 1) * SEQ)
-            head = lambda base: pl.ds(pl.multiple_of(base + h * 128, 128), 128)
-            dm = dmixed[rows, head(0)]
-            dw = dot_nt(dm, hidden[rows, head(D)]).astype(BF).astype(F32)
-            ds = (dw * attn_slope[h, b].astype(F32)).astype(BF)
-            dv = dot_tn(attn[h, b], dm)
-            dq = dot(ds, hidden[rows, head(3 * D)])
-            dk = dot_tn(ds, hidden[rows, head(2 * D)])
-            for base, d in ((D, dv), (2 * D, dq), (3 * D, dk)):
-                d = d.astype(BF).astype(F32) * slope[rows, head(base)].astype(F32)
-                dpre[rows, head(base)] = d.astype(BF)
-
-    @pl.loop(0, 4)
+    @pl.loop(0, HEADS // 2)
+    def _(i):
+        jobs = [(2 * i + k, b, slice(b * SEQ, (b + 1) * SEQ)) for k in range(2) for b in range(2)]
+        head = lambda h, base: pl.ds(pl.multiple_of(base + h * 128, 128), 128)
+
+        def put(h, rows, base, d):
+            d = d.astype(BF).astype(F32) * slope[rows, head(h, base)].astype(F32)
+            dpre[rows, head(h, base)] = d.astype(BF)
+
+        dws = [dot_nt(dmixed[rows, head(h, 0)], hidden[rows, head(h, D)]) for h, b, rows in jobs]
+        dss = [
+            (dw.astype(BF).astype(F32) * attn_slope[h, b].astype(F32)).astype(BF)
+            for dw, (h, b, rows) in zip(dws, jobs)
+        ]
+        for h, b, rows in jobs:
+            put(h, rows, D, dot_tn(attn[h, b], dmixed[rows, head(h, 0)]))
+        for ds, (h, b, rows) in zip(dss, jobs):
+            put(h, rows, 2 * D, dot(ds, hidden[rows, head(h, 3 * D)]))
+            put(h, rows, 3 * D, dot_tn(ds, hidden[rows, head(h, 2 * D)]))
+        at = pl.ds(pl.multiple_of(i * 256, 256), 256)
+        out_buf[:, at] = (events[:, at].astype(F32) + dot(half[...], w_out[:, at])).astype(BF)
+
+    store = pltpu.make_async_copy(out_buf, events_out_h, sem_out)
+    store.start()
+
+    @pl.loop(0, 2)
     def _(c):
-        at = pl.ds(pl.multiple_of(c * 256, 256), 256)
+        at = pl.ds(pl.multiple_of(c * 512, 512), 512)
         mixed[:, at] = dot_nt(dpre[...], w_in[at, :]).astype(BF).astype(F32)
 
-    @pl.loop(0, 8)
+    @pl.loop(0, 8, unroll=2)
     def _(i):
         at = pl.ds(pl.multiple_of(i * 64, 64), 64)
         dn = mixed[at, :]
@@ -246,19 +265,19 @@
     return pl.pallas_call(
         layer_kernel,
         out_shape=[jax.ShapeDtypeStruct((ROWS, D), BF)] + [block] * 8,
-        in_specs=[SMEM, SMEM, VMEM] + [ANY] * 12,
+        in_specs=[SMEM, SMEM] + [VMEM] * 9 + [ANY] * 4,
         out_specs=[ANY] + [VMEM] * 8,
         scratch_shapes=[
             vm((SLOTS, D), BF), vm((D, D), BF), vm((D, 4 * D), BF), vm((D, D), BF), vm((ROWS, D), BF),
             vm((ROWS, D), BF), vm((ROWS, D), BF), vm((ROWS, D), BF), vm((ROWS, 4 * D), BF),
             vm((ROWS, 4 * D), BF), vm((HEADS, 2, SEQ, SEQ), BF), vm((HEADS, 2, SEQ, SEQ), BF),
-            vm((ROWS, D), F32), vm((ROWS, D), BF), vm((ROWS, D), BF), vm((ROWS, 4 * D), BF),
+            vm((ROWS, D), F32), vm((ROWS, D), BF), vm((ROWS, D), BF), vm((ROWS, D), BF), vm((ROWS, 4 * D), BF),
             vm((2, SEQ, SEQ), F32), vm((ROWS, 128), F32), vm((ROWS, 128), F32),
             vm((ROWS, SLOTS), BF), vm((SLOTS, ROWS), BF),
-            pltpu.SemaphoreType.DMA((8,)), pltpu.SemaphoreType.DMA((3,)),
-            pltpu.SemaphoreType.DMA((4,)), pltpu.SemaphoreType.DMA,
+            vm((ROWS, 256), F32), vm((ROWS, 256), F32),
+            pltpu.SemaphoreType.DMA((3,)), pltpu.SemaphoreType.DMA((4,)), pltpu.SemaphoreType.DMA,
         ],
-        compiler_params=pltpu.CompilerParams(vmem_limit_bytes=52 * MIB),
+        compiler_params=pltpu.CompilerParams(vmem_limit_bytes=50 * MIB),
         cost_estimate=pl.CostEstimate(
             flops=14 * 10**9, bytes_accessed=18 * MIB, transcendentals=4 * MIB
         ),
@@ -337,7 +356,8 @@
     )(arrived)
 
 
-def content_kernel(wanted, arrived, w_tower, out, pre):
+def content_kernel(wanted, arrived, w_tower, tower_rows, out, handed, pre):
+    handed[...] = tower_rows[...]
     for n in range(NODES):
         pre[n * 8 : (n + 1) * 8, :] = jnp.concatenate(
             [arrived[n, j].astype(F32)[:8] for j in range(LOCALS)], axis=1
@@ -352,18 +372,20 @@
         out[j * 128 : (j + 1) * 128, :] = (dot(hot, high) + dot(hot, low)).astype(BF)
 
 
-def content_side(wanted, arrived, w_tower):
+def content_side(wanted, arrived, w_tower, tower_rows):
     return pl.pallas_call(
         content_kernel,
-        out_shape=jax.ShapeDtypeStruct((1024, D), BF),
-        in_specs=[VMEM] * 3,
-        out_specs=VMEM,
+        out_shape=[
+            jax.ShapeDtypeStruct((1024, D), BF), jax.ShapeDtypeStruct((NODES, 8, D), BF)
+        ],
+        in_specs=[VMEM] * 4,
+        out_specs=[VMEM, VMEM],
         scratch_shapes=[pltpu.VMEM((128, D), F32)],
         compiler_params=pltpu.CompilerParams(vmem_limit_bytes=16 * MIB),
         cost_estimate=pl.CostEstimate(
             flops=6 * 128 * D * D, bytes_accessed=5 * MIB, transcendentals=0
         ),
-    )(wanted, arrived, w_tower)
+    )(wanted, arrived, w_tower, tower_rows)
 
 
 def tower_kernel(pos, p0, p1, p2, p3, p4, p5, p6, p7, out, buf, sem):
@@ -393,10 +415,12 @@
     return lax.ppermute(x, "local", [(i, i ^ s) for i in range(LOCALS)])
 
 
-def gather_local(x):
+def gather_local(x, again=None):
     got = {0: x}
     for s in (4, 2, 6):
         got[s] = swap(x, s)
+    if again is not None:
+        got[0] = again
     for s in (0, 4, 2, 6):
         got[s + 1] = swap(got[s], 1)
     return [got[s] for s in range(LOCALS)]
@@ -419,8 +443,8 @@
     out = slots(arrived, slope, turned).reshape(NODES * LOCALS, 16, 128)
     back = lax.all_to_all(out, ("node", "local"), 0, 0, tiled=True).reshape(NODES, LOCALS, 16, 128)
     rows = lax.all_to_all(total(back), "node", 0, 0, tiled=True)
-    tower_grad = tower_side(pos, gather_local(rows)).reshape(D, D)
-    content_grad = content_side(wanted, back, w_tower)
+    content_grad, handed = content_side(wanted, back, w_tower, rows)
+    tower_grad = tower_side(pos, gather_local(rows, handed)).reshape(D, D)
     return (events_out.reshape(2, SEQ, D), content_grad, tower_grad)
 
 

time: 166 us -> 147 us (0.89)
  starting transfers between devices: 40.4 us -> 24.2 us
  waiting for transfers between devices: 8.09 us -> 24.2 us
  Pallas kernels: 52.4 us -> 40.5 us
  local copies, waits for them, and re-layouts: 9.8 us -> 2.46 us
    ppermute x21, starting transfers between devices: 40.4 us -> 24.2 us  [swap(): return lax.ppermute(x, 'local', [(i, i ^ s) for i in range(LOCALS)])]
    ppermute x21, waiting for transfers between devices: 8.09 us -> 24.2 us  [swap(): return lax.ppermute(x, 'local', [(i, i ^ s) for i in range(LOCALS)])]
    pallas_call x1, Pallas kernels: 44.7 us -> 32.9 us  [layer(): pl.pallas_call(layer_kernel, out_shape=[jax.ShapeDtypeStruct((ROWS, D), B...]
    unnamed x40 -> x12, local copies, waits for them, and re-layouts: 8.96 us -> 1.62 us
  transfers between devices with their start and end apart: 21 -> 21, of which waited for: 8 -> 11; matrix products, arithmetic and copies ran while one was open for 0% -> 0% of each run, Pallas kernels for 3% -> 3%
where the time goes in v2:
time: 147 us
  blocking collectives  54.3 us (37%)
  Pallas kernels  40.5 us (28%)
  starting transfers between devices  24.2 us (16%)
  waiting for transfers between devices  24.2 us (16%)
  local copies, waits for them, and re-layouts  2.46 us (2%)
    pallas_call x1, Pallas kernels, layer(): pl.pallas_call(layer_kernel, out_shape=[jax.ShapeDtypeStruct((ROWS, D), B...  32.9 us
    ppermute x21, waiting for transfers between devices, swap(): return lax.ppermute(x, 'local', [(i, i ^ s) for i in range(LOCALS)])  24.2 us
    ppermute x21, starting transfers between devices, swap(): return lax.ppermute(x, 'local', [(i, i ^ s) for i in range(LOCALS)])  24.2 us
    all_to_all x1, blocking collectives, body(): lax.all_to_all(out, ('node', 'local'), 0, 0, tiled=True)  19.3 us
    all_to_all x1, blocking collectives, body(): wanted = lax.all_to_all(asked, 'node', 0, 0, tiled=True)  13.9 us
    all_to_all x1, blocking collectives, body(): fetched = lax.all_to_all(picked, 'node', 0, 0, tiled=True).reshape(128, D)  10.7 us
    all_to_all x1, blocking collectives, body(): rows = lax.all_to_all(total(back), 'node', 0, 0, tiled=True)  10.4 us
    pallas_call x1, Pallas kernels, content_side(): pl.pallas_call(content_kernel, out_shape=[jax.ShapeDtypeStruct((1024, D),...  3.36 us
  transfers between devices with their start and end apart: 21, of which 11 were waited for; matrix products, arithmetic and copies ran while one was open for 0% of the time, Pallas kernels for 3%

profile of v2, /device:TPU:1, one launch (start us, length us, event | category | flops | bytes accessed | tf_op | source)
XLA Modules:
  0.0 146.9 jit_solution(17950836346748448736)
XLA Ops:
  0.7 0.8 copy.11
  1.5 13.9 %all_to_all.20.wanted = s32[16,8,128]{2,1,0:T(8,128)S(1)} all-to-all(s32[16,8,128]{2,1,0:T(8,128)S(1)} %broadcast_in_dim.8), channel_id=1, replica_groups=mesh['node'=16,'local'=8] {'node'}, dimensions={0} | all-to-all | bytes 131072 | tf_op jit(solution)/shard_map/all_to_all | solution.py:432
  15.4 1.6 %copy-done = bf16[1024,1024]{1,0:T(8,128)(2,1)S(1)} copy-done((bf16[1024,1024]{1,0:T(8,128)(2,1)S(1)}, bf16[1024,1024]{1,0:T(8,128)(2,1)}, u32[]{:S(2)}) %copy-start) | copy-done | bytes 2097176
  17.4 10.7 %all_to_all.21 = bf16[16,8,1024]{2,1,0:T(8,128)(2,1)S(1)} all-to-all(bf16[16,8,1024]{2,1,0:T(8,128)(2,1)S(1)} %shard_map.103), channel_id=1, replica_groups=mesh['node'=16,'local'=8] {'node'}, dimensions={0} | all-to-all | bytes 524288 | tf_op jit(solution)/shard_map/all_to_all | solution.py:434
  28.1 3.8 %collective-permute-start.5 = (bf16[128,1024]{1,0:T(8,128)(2,1)S(1)}, bf16[128,1024]{1,0:T(8,128)(2,1)S(1)}, u32[]{:S(2)}, u32[]{:S(2)}) collective-permute-start(bf16[128,1024]{1,0:T(8,128)(2,1)S(1)} %bitcast.11), channel_id=1, source_target_pairs={{0,6},{1,7},{2,4},{3,5},{4,2},{5,3},{6,0},{7,1},{8,14},{9,15},{10,... | collective-permute-start | bytes 786440 | tf_op jit(solution)/shard_map/ppermute | solution.py:415
  32.5 3.8 %collective-permute-start = (bf16[128,1024]{1,0:T(8,128)(2,1)S(1)}, bf16[128,1024]{1,0:T(8,128)(2,1)S(1)}, u32[]{:S(2)}, u32[]{:S(2)}) collective-permute-start(bf16[128,1024]{1,0:T(8,128)(2,1)S(1)} %bitcast.14), channel_id=1, source_target_pairs={{0,1},{1,0},{2,3},{3,2},{4,5},{5,4},{6,7},{7,6},{8,9},{9,8},{10,11... | collective-permute-start | bytes 786440 | tf_op jit(solution)/shard_map/ppermute | solution.py:415
  36.3 6.4 %collective-permute-done.5.p6 = bf16[128,1024]{1,0:T(8,128)(2,1)S(1)} collective-permute-done((bf16[128,1024]{1,0:T(8,128)(2,1)S(1)}, bf16[128,1024]{1,0:T(8,128)(2,1)S(1)}, u32[]{:S(2)}, u32[]{:S(2)}) %collective-permute-start.5) | collective-permute-done | bytes 262176 | tf_op jit(solution)/shard_map/ppermute | solution.py:415
  42.7 1.4 collective-permute-start.6
  44.0 0.9 collective-permute-start.4
  46.6 32.9 %shard_map.104 = (bf16[512,1024]{1,0:T(8,128)(2,1)}, bf16[1024,128]{1,0:T(8,128)(2,1)S(1)}, bf16[1024,128]{1,0:T(8,128)(2,1)S(1)}, bf16[1024,128]{1,0:T(8,128)(2...) custom-call(s32[1]{0:T(128)} %bitcast.pos, ...), custom_call_target="tpu_custom_call" | custom-call | flops 14000000000 | bytes 18874368 | tf_op jit(solution)/shard_map/pallas_call | solution.py:265
  81.2 2.6 %collective-permute-start.9 = (bf16[1024,128]{1,0:T(8,128)(2,1)S(1)}, bf16[1024,128]{1,0:T(8,128)(2,1)S(1)}, u32[]{:S(2)}, u32[]{:S(2)}) collective-permute-start(bf16[1024,128]{1,0:T(8,128)(2,1)S(1)} %add.13), channel_id=1, source_target_pairs={{0,4},{1,5},{2,6},{3,7},{4,0},{5,1},{6,2},{7,3},{8,12},{9,13},{10,... | collective-permute-start | bytes 786440 | tf_op jit(solution)/shard_map/ppermute | solution.py:415
  83.8 0.9 collective-permute-start.11
  85.2 0.9 shard_map.105
  86.2 4.1 %collective-permute-done.9.a1 = bf16[1024,128]{1,0:T(8,128)(2,1)S(1)} collective-permute-done((bf16[1024,128]{1,0:T(8,128)(2,1)S(1)}, bf16[1024,128]{1,0:T(8,128)(2,1)S(1)}, u32[]{:S(2)}, u32[]{:S(2)}) %collective-permute-start.9) | collective-permute-done | bytes 262176 | tf_op jit(solution)/shard_map/ppermute | solution.py:415
  90.3 6.1 %collective-permute-done.11.a2 = bf16[1024,128]{1,0:T(8,128)(2,1)S(1)} collective-permute-done((bf16[1024,128]{1,0:T(8,128)(2,1)S(1)}, bf16[1024,128]{1,0:T(8,128)(2,1)S(1)}, u32[]{:S(2)}, u32[]{:S(2)}) %collective-permute-start.11) | collective-permute-done | bytes 262176 | tf_op jit(solution)/shard_map/ppermute | solution.py:415
  96.6 0.8 shard_map.106
  97.4 19.3 %all_to_all.22 = bf16[128,16,128]{2,1,0:T(8,128)(2,1)S(1)} all-to-all(bf16[128,16,128]{2,1,0:T(8,128)(2,1)S(1)} %bitcast.10), channel_id=1, replica_groups=mesh['node'=16,'local'=8] {'node','local'}, dimensions={0} | all-to-all | bytes 1048576 | tf_op jit(solution)/shard_map/all_to_all | solution.py:444
  116.7 10.4 %all_to_all.23.tower_rows = bf16[16,8,1024]{2,1,0:T(8,128)(2,1)S(1)} all-to-all(bf16[16,8,1024]{2,1,0:T(8,128)(2,1)S(1)} %shard_map.107), channel_id=1, replica_groups=mesh['node'=16,'local'=8] {'node'}, dimensions={0} | all-to-all | bytes 524288 | tf_op jit(solution)/shard_map/all_to_all | solution.py:445
  127.9 2.2 %collective-permute-start.17 = (bf16[16,8,1024]{2,1,0:T(8,128)(2,1)S(1)}, bf16[16,8,1024]{2,1,0:T(8,128)(2,1)S(1)}, u32[]{:S(2)}, u32[]{:S(2)}) collective-permute-start(bf16[16,8,1024]{2,1,0:T(8,128)(2,1)S(1)} %all_to_all.23.tower_rows), channel_id=1, source_target_pairs={{0,4},{1,5},{2,6},{3,7},{4,0},{5,1},{6,2},{7,3},{8,12},{9,13},{10,... | collective-permute-start | bytes 786440 | tf_op jit(solution)/shard_map/ppermute | solution.py:415
  130.4 3.4 %shard_map.108 = (bf16[1024,1024]{1,0:T(8,128)(2,1)}, bf16[16,8,1024]{2,1,0:T(8,128)(2,1)S(1)}) custom-call(s32[16,8,128]{2,1,0:T(8,128)S(1)} %all_to_all.20.wanted, bf16[16,8,16,128]{3,2,1,0:T(8,128)(2,1)S(1)} %bitcast.9, bf16[1024,1024]{1,0:T(8,128)(2,1)S(1)} %copy-done.1, bf16[16,8,1024]{2,1,0:T(8,128)(2,1)S(1)} %all_to_all.23.tower_rows), custom_call_target="tpu_custom_call" | custom-call | flops 805306368 | bytes 5242880 | tf_op jit(solution)/shard_map/pallas_call | solution.py:376
  133.8 2.9 %collective-permute-start.14 = (bf16[16,8,1024]{2,1,0:T(8,128)(2,1)S(1)}, bf16[16,8,1024]{2,1,0:T(8,128)(2,1)S(1)}, u32[]{:S(2)}, u32[]{:S(2)}) collective-permute-start(bf16[16,8,1024]{2,1,0:T(8,128)(2,1)S(1)} %get-tuple-element.28.p0), channel_id=1, source_target_pairs={{0,1},{1,0},{2,3},{3,2},{4,5},{5,4},{6,7},{7,6},{8,9},{9,8},{10,11... | collective-permute-start | bytes 786440 | tf_op jit(solution)/shard_map/ppermute | solution.py:415
  136.7 4.4 %collective-permute-done.19.p6 = bf16[16,8,1024]{2,1,0:T(8,128)(2,1)S(1)} collective-permute-done((bf16[16,8,1024]{2,1,0:T(8,128)(2,1)S(1)}, bf16[16,8,1024]{2,1,0:T(8,128)(2,1)S(1)}, u32[]{:S(2)}, u32[]{:S(2)}) %collective-permute-start.19) | collective-permute-done | bytes 262176 | tf_op jit(solution)/shard_map/ppermute | solution.py:415
  141.1 1.6 %collective-permute-start.20 = (bf16[16,8,1024]{2,1,0:T(8,128)(2,1)S(1)}, bf16[16,8,1024]{2,1,0:T(8,128)(2,1)S(1)}, u32[]{:S(2)}, u32[]{:S(2)}) collective-permute-start(bf16[16,8,1024]{2,1,0:T(8,128)(2,1)S(1)} %collective-permute-done.19.p6), channel_id=1, source_target_pairs={{0,1},{1,0},{2,3},{3,2},{4,5},{5,4},{6,7},{7,6},{8,9},{9,8},{10,11... | collective-permute-start | bytes 786440 | tf_op jit(solution)/shard_map/ppermute | solution.py:415
  144.6 2.1 %shard_map.109 = f32[16,8,8,1024]{3,2,1,0:T(8,128)} custom-call(s32[1]{0:T(128)} %bitcast.pos, bf16[16,8,1024]{2,1,0:T(8,128)(2,1)S(1)} %get-tuple-element.28.p0, bf16[16,8,1024]{2,1,0:T(8,128)(2,1)S(1)} %collective-permute-done.14.p1, bf16[16,8,1024]{2,1,0:T(8,128)(2,1)S(1)} %collective-permute-done.15.p2, ...), custom_call_target="tpu_custom_call" | custom-call | flops 1048576 | bytes 6291456 | tf_op jit(solution)/shard_map/pallas_call | solution.py:403
  (47 shorter events, 8.2 us)
Async XLA Ops:
  0.6 45.9 %copy-start.5 = (s32[2]{0:T(128)S(1)}, s32[2]{0:T(128)}, u32[]{:S(2)}) copy-start(s32[2]{0:T(128)} %lengths.1) | copy-start | bytes 28
  0.6 45.9 %copy-start.4 = (s32[2,256]{1,0:T(2,128)S(1)}, s32[2,256]{1,0:T(2,128)}, u32[]{:S(2)}) copy-start(s32[2,256]{1,0:T(2,128)} %inverse.1) | copy-start | bytes 6148
  28.1 14.5 %collective-permute-start.5 = (bf16[128,1024]{1,0:T(8,128)(2,1)S(1)}, bf16[128,1024]{1,0:T(8,128)(2,1)S(1)}, u32[]{:S(2)}, u32[]{:S(2)}) collective-permute-start(bf16[128,1024]{1,0:T(8,128)(2,1)S(1)} %bitcast.11), channel_id=1, source_target_pairs={{0,6},{1,7},{2,4},{3,5},{4,2},{5,3},{6,0},{7,1},{8,14},{9,15},{10,... | collective-permute-start | bytes 786440 | tf_op jit(solution)/shard_map/ppermute | solution.py:415
  31.9 12.1 %collective-permute-start.3 = (bf16[128,1024]{1,0:T(8,128)(2,1)S(1)}, bf16[128,1024]{1,0:T(8,128)(2,1)S(1)}, u32[]{:S(2)}, u32[]{:S(2)}) collective-permute-start(bf16[128,1024]{1,0:T(8,128)(2,1)S(1)} %bitcast.12), channel_id=1, source_target_pairs={{0,4},{1,5},{2,6},{3,7},{4,0},{5,1},{6,2},{7,3},{8,12},{9,13},{10,... | collective-permute-start | bytes 786440 | tf_op jit(solution)/shard_map/ppermute | solution.py:415
  31.9 13.1 %collective-permute-start.1 = (bf16[128,1024]{1,0:T(8,128)(2,1)S(1)}, bf16[128,1024]{1,0:T(8,128)(2,1)S(1)}, u32[]{:S(2)}, u32[]{:S(2)}) collective-permute-start(bf16[128,1024]{1,0:T(8,128)(2,1)S(1)} %bitcast.13), channel_id=1, source_target_pairs={{0,2},{1,3},{2,0},{3,1},{4,6},{5,7},{6,4},{7,5},{8,10},{9,11},{10,... | collective-permute-start | bytes 786440 | tf_op jit(solution)/shard_map/ppermute | solution.py:415
  32.5 12.9 %collective-permute-start = (bf16[128,1024]{1,0:T(8,128)(2,1)S(1)}, bf16[128,1024]{1,0:T(8,128)(2,1)S(1)}, u32[]{:S(2)}, u32[]{:S(2)}) collective-permute-start(bf16[128,1024]{1,0:T(8,128)(2,1)S(1)} %bitcast.14), channel_id=1, source_target_pairs={{0,1},{1,0},{2,3},{3,2},{4,5},{5,4},{6,7},{7,6},{8,9},{9,8},{10,11... | collective-permute-start | bytes 786440 | tf_op jit(solution)/shard_map/ppermute | solution.py:415
  42.7 2.7 %collective-permute-start.6 = (bf16[128,1024]{1,0:T(8,128)(2,1)S(1)}, bf16[128,1024]{1,0:T(8,128)(2,1)S(1)}, u32[]{:S(2)}, u32[]{:S(2)}) collective-permute-start(bf16[128,1024]{1,0:T(8,128)(2,1)S(1)} %collective-permute-done.5.p6), channel_id=1, source_target_pairs={{0,1},{1,0},{2,3},{3,2},{4,5},{5,4},{6,7},{7,6},{8,9},{9,8},{10,11... | collective-permute-start | bytes 786440 | tf_op jit(solution)/shard_map/ppermute | solution.py:415
  44.0 2.1 %collective-permute-start.4 = (bf16[128,1024]{1,0:T(8,128)(2,1)S(1)}, bf16[128,1024]{1,0:T(8,128)(2,1)S(1)}, u32[]{:S(2)}, u32[]{:S(2)}) collective-permute-start(bf16[128,1024]{1,0:T(8,128)(2,1)S(1)} %collective-permute-done.3.p4), channel_id=1, source_target_pairs={{0,1},{1,0},{2,3},{3,2},{4,5},{5,4},{6,7},{7,6},{8,9},{9,8},{10,11... | collective-permute-start | bytes 786440 | tf_op jit(solution)/shard_map/ppermute | solution.py:415
  45.0 1.6 %collective-permute-start.2 = (bf16[128,1024]{1,0:T(8,128)(2,1)S(1)}, bf16[128,1024]{1,0:T(8,128)(2,1)S(1)}, u32[]{:S(2)}, u32[]{:S(2)}) collective-permute-start(bf16[128,1024]{1,0:T(8,128)(2,1)S(1)} %collective-permute-done.1.p2), channel_id=1, source_target_pairs={{0,1},{1,0},{2,3},{3,2},{4,5},{5,4},{6,7},{7,6},{8,9},{9,8},{10,11... | collective-permute-start | bytes 786440 | tf_op jit(solution)/shard_map/ppermute | solution.py:415
  79.5 5.7 %copy-start.1 = (bf16[1024,1024]{1,0:T(8,128)(2,1)S(1)}, bf16[1024,1024]{1,0:T(8,128)(2,1)}, u32[]{:S(2)}) copy-start(bf16[1024,1024]{1,0:T(8,128)(2,1)} %w_tower.1) | copy-start | bytes 6291460
  79.5 1.6 %collective-permute-start.8 = (bf16[1024,128]{1,0:T(8,128)(2,1)S(1)}, bf16[1024,128]{1,0:T(8,128)(2,1)S(1)}, u32[]{:S(2)}, u32[]{:S(2)}) collective-permute-start(bf16[1024,128]{1,0:T(8,128)(2,1)S(1)} %get-tuple-element.20), channel_id=1, source_target_pairs={{0,1},{1,0},{2,3},{3,2},{4,5},{5,4},{6,7},{7,6},{8,9},{9,8},{10,11... | collective-permute-start | bytes 786440 | tf_op jit(solution)/shard_map/ppermute | solution.py:415
  80.0 3.8 %collective-permute-start.10 = (bf16[1024,128]{1,0:T(8,128)(2,1)S(1)}, bf16[1024,128]{1,0:T(8,128)(2,1)S(1)}, u32[]{:S(2)}, u32[]{:S(2)}) collective-permute-start(bf16[1024,128]{1,0:T(8,128)(2,1)S(1)} %get-tuple-element.22), channel_id=1, source_target_pairs={{0,1},{1,0},{2,3},{3,2},{4,5},{5,4},{6,7},{7,6},{8,9},{9,8},{10,11... | collective-permute-start | bytes 786440 | tf_op jit(solution)/shard_map/ppermute | solution.py:415
  80.1 4.7 %collective-permute-start.12 = (bf16[1024,128]{1,0:T(8,128)(2,1)S(1)}, bf16[1024,128]{1,0:T(8,128)(2,1)S(1)}, u32[]{:S(2)}, u32[]{:S(2)}) collective-permute-start(bf16[1024,128]{1,0:T(8,128)(2,1)S(1)} %get-tuple-element.24), channel_id=1, source_target_pairs={{0,1},{1,0},{2,3},{3,2},{4,5},{5,4},{6,7},{7,6},{8,9},{9,8},{10,11... | collective-permute-start | bytes 786440 | tf_op jit(solution)/shard_map/ppermute | solution.py:415
  80.5 5.7 %collective-permute-start.7 = (bf16[1024,128]{1,0:T(8,128)(2,1)S(1)}, bf16[1024,128]{1,0:T(8,128)(2,1)S(1)}, u32[]{:S(2)}, u32[]{:S(2)}) collective-permute-start(bf16[1024,128]{1,0:T(8,128)(2,1)S(1)} %get-tuple-element.18), channel_id=1, source_target_pairs={{0,1},{1,0},{2,3},{3,2},{4,5},{5,4},{6,7},{7,6},{8,9},{9,8},{10,11... | collective-permute-start | bytes 786440 | tf_op jit(solution)/shard_map/ppermute | solution.py:415
  81.2 9.1 %collective-permute-start.9 = (bf16[1024,128]{1,0:T(8,128)(2,1)S(1)}, bf16[1024,128]{1,0:T(8,128)(2,1)S(1)}, u32[]{:S(2)}, u32[]{:S(2)}) collective-permute-start(bf16[1024,128]{1,0:T(8,128)(2,1)S(1)} %add.13), channel_id=1, source_target_pairs={{0,4},{1,5},{2,6},{3,7},{4,0},{5,1},{6,2},{7,3},{8,12},{9,13},{10,... | collective-permute-start | bytes 786440 | tf_op jit(solution)/shard_map/ppermute | solution.py:415
  83.8 12.5 %collective-permute-start.11 = (bf16[1024,128]{1,0:T(8,128)(2,1)S(1)}, bf16[1024,128]{1,0:T(8,128)(2,1)S(1)}, u32[]{:S(2)}, u32[]{:S(2)}) collective-permute-start(bf16[1024,128]{1,0:T(8,128)(2,1)S(1)} %add.14), channel_id=1, source_target_pairs={{0,2},{1,3},{2,0},{3,1},{4,6},{5,7},{6,4},{7,5},{8,10},{9,11},{10,... | collective-permute-start | bytes 786440 | tf_op jit(solution)/shard_map/ppermute | solution.py:415
  84.9 11.7 %collective-permute-start.13 = (bf16[1024,128]{1,0:T(8,128)(2,1)S(1)}, bf16[1024,128]{1,0:T(8,128)(2,1)S(1)}, u32[]{:S(2)}, u32[]{:S(2)}) collective-permute-start(bf16[1024,128]{1,0:T(8,128)(2,1)S(1)} %add.15), channel_id=1, source_target_pairs={{0,6},{1,7},{2,4},{3,5},{4,2},{5,3},{6,0},{7,1},{8,14},{9,15},{10,... | collective-permute-start | bytes 786440 | tf_op jit(solution)/shard_map/ppermute | solution.py:415
  127.1 14.0 %collective-permute-start.19 = (bf16[16,8,1024]{2,1,0:T(8,128)(2,1)S(1)}, bf16[16,8,1024]{2,1,0:T(8,128)(2,1)S(1)}, u32[]{:S(2)}, u32[]{:S(2)}) collective-permute-start(bf16[16,8,1024]{2,1,0:T(8,128)(2,1)S(1)} %all_to_all.23.tower_rows), channel_id=1, source_target_pairs={{0,6},{1,7},{2,4},{3,5},{4,2},{5,3},{6,0},{7,1},{8,14},{9,15},{10,... | collective-permute-start | bytes 786440 | tf_op jit(solution)/shard_map/ppermute | solution.py:415
  127.9 14.8 %collective-permute-start.17 = (bf16[16,8,1024]{2,1,0:T(8,128)(2,1)S(1)}, bf16[16,8,1024]{2,1,0:T(8,128)(2,1)S(1)}, u32[]{:S(2)}, u32[]{:S(2)}) collective-permute-start(bf16[16,8,1024]{2,1,0:T(8,128)(2,1)S(1)} %all_to_all.23.tower_rows), channel_id=1, source_target_pairs={{0,4},{1,5},{2,6},{3,7},{4,0},{5,1},{6,2},{7,3},{8,12},{9,13},{10,... | collective-permute-start | bytes 786440 | tf_op jit(solution)/shard_map/ppermute | solution.py:415
  130.1 12.7 %collective-permute-start.15 = (bf16[16,8,1024]{2,1,0:T(8,128)(2,1)S(1)}, bf16[16,8,1024]{2,1,0:T(8,128)(2,1)S(1)}, u32[]{:S(2)}, u32[]{:S(2)}) collective-permute-start(bf16[16,8,1024]{2,1,0:T(8,128)(2,1)S(1)} %all_to_all.23.tower_rows), channel_id=1, source_target_pairs={{0,2},{1,3},{2,0},{3,1},{4,6},{5,7},{6,4},{7,5},{8,10},{9,11},{10,... | collective-permute-start | bytes 786440 | tf_op jit(solution)/shard_map/ppermute | solution.py:415
  133.8 9.6 %collective-permute-start.14 = (bf16[16,8,1024]{2,1,0:T(8,128)(2,1)S(1)}, bf16[16,8,1024]{2,1,0:T(8,128)(2,1)S(1)}, u32[]{:S(2)}, u32[]{:S(2)}) collective-permute-start(bf16[16,8,1024]{2,1,0:T(8,128)(2,1)S(1)} %get-tuple-element.28.p0), channel_id=1, source_target_pairs={{0,1},{1,0},{2,3},{3,2},{4,5},{5,4},{6,7},{7,6},{8,9},{9,8},{10,11... | collective-permute-start | bytes 786440 | tf_op jit(solution)/shard_map/ppermute | solution.py:415
  141.1 2.7 %collective-permute-start.20 = (bf16[16,8,1024]{2,1,0:T(8,128)(2,1)S(1)}, bf16[16,8,1024]{2,1,0:T(8,128)(2,1)S(1)}, u32[]{:S(2)}, u32[]{:S(2)}) collective-permute-start(bf16[16,8,1024]{2,1,0:T(8,128)(2,1)S(1)} %collective-permute-done.19.p6), channel_id=1, source_target_pairs={{0,1},{1,0},{2,3},{3,2},{4,5},{5,4},{6,7},{7,6},{8,9},{9,8},{10,11... | collective-permute-start | bytes 786440 | tf_op jit(solution)/shard_map/ppermute | solution.py:415
  142.7 1.5 %collective-permute-start.18 = (bf16[16,8,1024]{2,1,0:T(8,128)(2,1)S(1)}, bf16[16,8,1024]{2,1,0:T(8,128)(2,1)S(1)}, u32[]{:S(2)}, u32[]{:S(2)}) collective-permute-start(bf16[16,8,1024]{2,1,0:T(8,128)(2,1)S(1)} %collective-permute-done.17.p4), channel_id=1, source_target_pairs={{0,1},{1,0},{2,3},{3,2},{4,5},{5,4},{6,7},{7,6},{8,9},{9,8},{10,11... | collective-permute-start | bytes 786440 | tf_op jit(solution)/shard_map/ppermute | solution.py:415
  142.7 1.9 %collective-permute-start.16 = (bf16[16,8,1024]{2,1,0:T(8,128)(2,1)S(1)}, bf16[16,8,1024]{2,1,0:T(8,128)(2,1)S(1)}, u32[]{:S(2)}, u32[]{:S(2)}) collective-permute-start(bf16[16,8,1024]{2,1,0:T(8,128)(2,1)S(1)} %collective-permute-done.15.p2), channel_id=1, source_target_pairs={{0,1},{1,0},{2,3},{3,2},{4,5},{5,4},{6,7},{7,6},{8,9},{9,8},{10,11... | collective-permute-start | bytes 786440 | tf_op jit(solution)/shard_map/ppermute | solution.py:415
  (3 other events, 8.5 us)

commit v3 on v2

--- a/solution.py
+++ b/solution.py
@@ -43,6 +43,22 @@
     return sigma * (1.0 + v * (1.0 - sigma))
 
 
+def ask_kernel(rows, out):
+    for n in range(NODES):
+        out[n] = jnp.broadcast_to(rows[:, n : n + 1], (8, 128))
+
+
+def ask(rows):
+    return pl.pallas_call(
+        ask_kernel,
+        out_shape=jax.ShapeDtypeStruct((NODES, 8, 128), jnp.int32),
+        in_specs=[VMEM],
+        out_specs=VMEM,
+        compiler_params=pltpu.CompilerParams(vmem_limit_bytes=2 * MIB),
+        cost_estimate=pl.CostEstimate(flops=20 * 10**9, bytes_accessed=MIB, transcendentals=0),
+    )(rows)
+
+
 def pick_kernel(wanted, content, out):
     ids = wanted[...].reshape(128, 128)
     lane = lax.broadcasted_iota(jnp.int32, (128, 128), 1)
@@ -67,7 +83,7 @@
     pos, lengths, inverse, p0, p1, p2, p3, p4, p5, p6, p7, w_tower_h, w_in_h, w_out_h, grad_h,
     events_out_h, k0, k1, k2, k3, s0, s1, s2, s3,
     table, w_tower, w_in, w_out, grad, out_buf, events, normed, hidden, slope, attn, attn_slope,
-    mixed, half, dgated, dmixed, dpre, coef, inv_rms, inv_std, hot_gather, hot_scatter, pre_a, pre_b,
+    mixed, half, dgated, dmixed, dpre, coef, inv_rms, hot_gather, hot_scatter, pre_a, pre_b,
     sem_w, sem_in, sem_out,
 ):
     me = pos[0]
@@ -192,22 +208,16 @@
         m = mixed[at, :]
         centred = m - jnp.mean(m, axis=-1, keepdims=True)
         r = lax.rsqrt(jnp.mean(centred * centred, axis=-1, keepdims=True) + 1e-05)
-        inv_std[at, :] = jnp.broadcast_to(r, (64, 128))
         normal = centred * r
-        mixed[at, :] = normal
-        half[at, :] = (normal * hidden[at, 0:D].astype(F32)).astype(BF)
-
-    @pl.loop(0, 8, unroll=2)
-    def _(i):
-        at = pl.ds(pl.multiple_of(i * 64, 64), 64)
+        gate = hidden[at, 0:D].astype(F32)
+        half[at, :] = (normal * gate).astype(BF)
         dg = dgated[at, :].astype(F32)
-        normal = mixed[at, :]
         dgate = (dg * normal).astype(BF).astype(F32)
         dpre[at, 0:D] = (dgate * slope[at, 0:D].astype(F32)).astype(BF)
-        dnormal = dg * hidden[at, 0:D].astype(F32)
+        dnormal = dg * gate
         m1 = jnp.mean(dnormal, axis=-1, keepdims=True)
         m2 = jnp.mean(dnormal * normal, axis=-1, keepdims=True)
-        dmixed[at, :] = (inv_std[at, 0:1] * (dnormal - m1 - normal * m2)).astype(BF)
+        dmixed[at, :] = (r * (dnormal - m1 - normal * m2)).astype(BF)
 
     @pl.loop(0, HEADS // 2)
     def _(i):
@@ -272,7 +282,7 @@
             vm((ROWS, D), BF), vm((ROWS, D), BF), vm((ROWS, D), BF), vm((ROWS, 4 * D), BF),
             vm((ROWS, 4 * D), BF), vm((HEADS, 2, SEQ, SEQ), BF), vm((HEADS, 2, SEQ, SEQ), BF),
             vm((ROWS, D), F32), vm((ROWS, D), BF), vm((ROWS, D), BF), vm((ROWS, D), BF), vm((ROWS, 4 * D), BF),
-            vm((2, SEQ, SEQ), F32), vm((ROWS, 128), F32), vm((ROWS, 128), F32),
+            vm((2, SEQ, SEQ), F32), vm((ROWS, 128), F32),
             vm((ROWS, SLOTS), BF), vm((SLOTS, ROWS), BF),
             vm((ROWS, 256), F32), vm((ROWS, 256), F32),
             pltpu.SemaphoreType.DMA((3,)), pltpu.SemaphoreType.DMA((4,)), pltpu.SemaphoreType.DMA,
@@ -428,7 +438,7 @@
 
 def body(inverse, slot_rows, lengths, content, w_tower, w_in, w_out, out_grad):
     pos = lax.axis_index("local").astype(jnp.int32).reshape(1)
-    asked = jnp.broadcast_to(slot_rows.reshape(NODES, 8, 1), (NODES, 8, 128))
+    asked = ask(slot_rows.reshape(NODES, 8).T)
     wanted = lax.all_to_all(asked, "node", 0, 0, tiled=True)
     picked = pick(wanted, content)
     fetched = lax.all_to_all(picked, "node", 0, 0, tiled=True).reshape(128, D)

time: 147 us -> 145 us (0.986)
  local copies, waits for them, and re-layouts: 2.46 us -> 0.71 us
where the time goes in v3:
time: 145 us; the launch traced here: 144 us
  blocking collectives  54.5 us (38%)
  Pallas kernels  39.6 us (27%)
  starting transfers between devices  24.2 us (17%)
  waiting for transfers between devices  24.2 us (17%)
    pallas_call x1, Pallas kernels, layer(): pl.pallas_call(layer_kernel, out_shape=[jax.ShapeDtypeStruct((ROWS, D), B...  31.9 us
    ppermute x21, waiting for transfers between devices, swap(): return lax.ppermute(x, 'local', [(i, i ^ s) for i in range(LOCALS)])  24.2 us
    ppermute x21, starting transfers between devices, swap(): return lax.ppermute(x, 'local', [(i, i ^ s) for i in range(LOCALS)])  24.2 us
    all_to_all x1, blocking collectives, body(): lax.all_to_all(out, ('node', 'local'), 0, 0, tiled=True)  19.3 us
    all_to_all x1, blocking collectives, body(): wanted = lax.all_to_all(asked, 'node', 0, 0, tiled=True)  14 us
    all_to_all x1, blocking collectives, body(): fetched = lax.all_to_all(picked, 'node', 0, 0, tiled=True).reshape(128, D)  10.7 us
    all_to_all x1, blocking collectives, body(): rows = lax.all_to_all(total(back), 'node', 0, 0, tiled=True)  10.4 us
    pallas_call x1, Pallas kernels, content_side(): pl.pallas_call(content_kernel, out_shape=[jax.ShapeDtypeStruct((1024, D),...  3.36 us
  transfers between devices with their start and end apart: 21, of which 11 were waited for; matrix products, arithmetic and copies ran while one was open for 0% of the time, Pallas kernels for 3%

profile of v3, /device:TPU:1, one launch (start us, length us, event | category | flops | bytes accessed | tf_op | source)
XLA Modules:
  0.0 144.4 jit_solution(17438327506933663958)
XLA Ops:
  1.4 14.0 %all_to_all.20.wanted = s32[16,8,128]{2,1,0:T(8,128)S(1)} all-to-all(s32[16,8,128]{2,1,0:T(8,128)S(1)} %shard_map.103), channel_id=1, replica_groups=mesh['node'=16,'local'=8] {'node'}, dimensions={0} | all-to-all | bytes 131072 | tf_op jit(solution)/shard_map/all_to_all | solution.py:442
  15.9 10.7 %all_to_all.21 = bf16[16,8,1024]{2,1,0:T(8,128)(2,1)S(1)} all-to-all(bf16[16,8,1024]{2,1,0:T(8,128)(2,1)S(1)} %shard_map.104), channel_id=1, replica_groups=mesh['node'=16,'local'=8] {'node'}, dimensions={0} | all-to-all | bytes 524288 | tf_op jit(solution)/shard_map/all_to_all | solution.py:444
  26.6 3.8 %collective-permute-start.5 = (bf16[128,1024]{1,0:T(8,128)(2,1)S(1)}, bf16[128,1024]{1,0:T(8,128)(2,1)S(1)}, u32[]{:S(2)}, u32[]{:S(2)}) collective-permute-start(bf16[128,1024]{1,0:T(8,128)(2,1)S(1)} %bitcast.13), channel_id=1, source_target_pairs={{0,6},{1,7},{2,4},{3,5},{4,2},{5,3},{6,0},{7,1},{8,14},{9,15},{10,... | collective-permute-start | bytes 786440 | tf_op jit(solution)/shard_map/ppermute | solution.py:425
  31.0 3.8 %collective-permute-start = (bf16[128,1024]{1,0:T(8,128)(2,1)S(1)}, bf16[128,1024]{1,0:T(8,128)(2,1)S(1)}, u32[]{:S(2)}, u32[]{:S(2)}) collective-permute-start(bf16[128,1024]{1,0:T(8,128)(2,1)S(1)} %bitcast.16), channel_id=1, source_target_pairs={{0,1},{1,0},{2,3},{3,2},{4,5},{5,4},{6,7},{7,6},{8,9},{9,8},{10,11... | collective-permute-start | bytes 786440 | tf_op jit(solution)/shard_map/ppermute | solution.py:425
  34.8 6.4 %collective-permute-done.5.p6 = bf16[128,1024]{1,0:T(8,128)(2,1)S(1)} collective-permute-done((bf16[128,1024]{1,0:T(8,128)(2,1)S(1)}, bf16[128,1024]{1,0:T(8,128)(2,1)S(1)}, u32[]{:S(2)}, u32[]{:S(2)}) %collective-permute-start.5) | collective-permute-done | bytes 262176 | tf_op jit(solution)/shard_map/ppermute | solution.py:425
  41.2 1.3 collective-permute-start.6
  42.5 0.9 collective-permute-start.4
  43.9 0.7 collective-permute-done.4.p5
  45.0 31.9 %shard_map.105 = (bf16[512,1024]{1,0:T(8,128)(2,1)}, bf16[1024,128]{1,0:T(8,128)(2,1)S(1)}, bf16[1024,128]{1,0:T(8,128)(2,1)S(1)}, bf16[1024,128]{1,0:T(8,128)(2...) custom-call(s32[1]{0:T(128)} %bitcast.pos, ...), custom_call_target="tpu_custom_call" | custom-call | flops 14000000000 | bytes 18874368 | tf_op jit(solution)/shard_map/pallas_call | solution.py:275
  78.7 2.6 %collective-permute-start.9 = (bf16[1024,128]{1,0:T(8,128)(2,1)S(1)}, bf16[1024,128]{1,0:T(8,128)(2,1)S(1)}, u32[]{:S(2)}, u32[]{:S(2)}) collective-permute-start(bf16[1024,128]{1,0:T(8,128)(2,1)S(1)} %add.13), channel_id=1, source_target_pairs={{0,4},{1,5},{2,6},{3,7},{4,0},{5,1},{6,2},{7,3},{8,12},{9,13},{10,... | collective-permute-start | bytes 786440 | tf_op jit(solution)/shard_map/ppermute | solution.py:425
  81.4 1.0 collective-permute-start.11
  82.7 0.9 shard_map.106
  83.8 4.0 %collective-permute-done.9.a1 = bf16[1024,128]{1,0:T(8,128)(2,1)S(1)} collective-permute-done((bf16[1024,128]{1,0:T(8,128)(2,1)S(1)}, bf16[1024,128]{1,0:T(8,128)(2,1)S(1)}, u32[]{:S(2)}, u32[]{:S(2)}) %collective-permute-start.9) | collective-permute-done | bytes 262176 | tf_op jit(solution)/shard_map/ppermute | solution.py:425
  87.8 6.1 %collective-permute-done.11.a2 = bf16[1024,128]{1,0:T(8,128)(2,1)S(1)} collective-permute-done((bf16[1024,128]{1,0:T(8,128)(2,1)S(1)}, bf16[1024,128]{1,0:T(8,128)(2,1)S(1)}, u32[]{:S(2)}, u32[]{:S(2)}) %collective-permute-start.11) | collective-permute-done | bytes 262176 | tf_op jit(solution)/shard_map/ppermute | solution.py:425
  94.1 0.8 shard_map.107
  94.9 19.3 %all_to_all.22 = bf16[128,16,128]{2,1,0:T(8,128)(2,1)S(1)} all-to-all(bf16[128,16,128]{2,1,0:T(8,128)(2,1)S(1)} %bitcast.12), channel_id=1, replica_groups=mesh['node'=16,'local'=8] {'node','local'}, dimensions={0} | all-to-all | bytes 1048576 | tf_op jit(solution)/shard_map/all_to_all | solution.py:454
  114.2 10.4 %all_to_all.23.tower_rows = bf16[16,8,1024]{2,1,0:T(8,128)(2,1)S(1)} all-to-all(bf16[16,8,1024]{2,1,0:T(8,128)(2,1)S(1)} %shard_map.108), channel_id=1, replica_groups=mesh['node'=16,'local'=8] {'node'}, dimensions={0} | all-to-all | bytes 524288 | tf_op jit(solution)/shard_map/all_to_all | solution.py:455
  124.7 0.7 collective-permute-start.19
  125.4 2.2 %collective-permute-start.17 = (bf16[16,8,1024]{2,1,0:T(8,128)(2,1)S(1)}, bf16[16,8,1024]{2,1,0:T(8,128)(2,1)S(1)}, u32[]{:S(2)}, u32[]{:S(2)}) collective-permute-start(bf16[16,8,1024]{2,1,0:T(8,128)(2,1)S(1)} %all_to_all.23.tower_rows), channel_id=1, source_target_pairs={{0,4},{1,5},{2,6},{3,7},{4,0},{5,1},{6,2},{7,3},{8,12},{9,13},{10,... | collective-permute-start | bytes 786440 | tf_op jit(solution)/shard_map/ppermute | solution.py:425
  127.9 3.4 %shard_map.109 = (bf16[1024,1024]{1,0:T(8,128)(2,1)}, bf16[16,8,1024]{2,1,0:T(8,128)(2,1)S(1)}) custom-call(s32[16,8,128]{2,1,0:T(8,128)S(1)} %all_to_all.20.wanted, bf16[16,8,16,128]{3,2,1,0:T(8,128)(2,1)S(1)} %bitcast.11, bf16[1024,1024]{1,0:T(8,128)(2,1)S(1)} %copy-done.1, bf16[16,8,1024]{2,1,0:T(8,128)(2,1)S(1)} %all_to_all.23.tower_rows), custom_call_target="tpu_custom_call" | custom-call | flops 805306368 | bytes 5242880 | tf_op jit(solution)/shard_map/pallas_call | solution.py:386
  131.3 2.9 %collective-permute-start.14 = (bf16[16,8,1024]{2,1,0:T(8,128)(2,1)S(1)}, bf16[16,8,1024]{2,1,0:T(8,128)(2,1)S(1)}, u32[]{:S(2)}, u32[]{:S(2)}) collective-permute-start(bf16[16,8,1024]{2,1,0:T(8,128)(2,1)S(1)} %get-tuple-element.28.p0), channel_id=1, source_target_pairs={{0,1},{1,0},{2,3},{3,2},{4,5},{5,4},{6,7},{7,6},{8,9},{9,8},{10,11... | collective-permute-start | bytes 786440 | tf_op jit(solution)/shard_map/ppermute | solution.py:425
  134.2 4.4 %collective-permute-done.19.p6 = bf16[16,8,1024]{2,1,0:T(8,128)(2,1)S(1)} collective-permute-done((bf16[16,8,1024]{2,1,0:T(8,128)(2,1)S(1)}, bf16[16,8,1024]{2,1,0:T(8,128)(2,1)S(1)}, u32[]{:S(2)}, u32[]{:S(2)}) %collective-permute-start.19) | collective-permute-done | bytes 262176 | tf_op jit(solution)/shard_map/ppermute | solution.py:425
  138.6 1.6 %collective-permute-start.20 = (bf16[16,8,1024]{2,1,0:T(8,128)(2,1)S(1)}, bf16[16,8,1024]{2,1,0:T(8,128)(2,1)S(1)}, u32[]{:S(2)}, u32[]{:S(2)}) collective-permute-start(bf16[16,8,1024]{2,1,0:T(8,128)(2,1)S(1)} %collective-permute-done.19.p6), channel_id=1, source_target_pairs={{0,1},{1,0},{2,3},{3,2},{4,5},{5,4},{6,7},{7,6},{8,9},{9,8},{10,11... | collective-permute-start | bytes 786440 | tf_op jit(solution)/shard_map/ppermute | solution.py:425
  142.1 2.1 %shard_map.110 = f32[16,8,8,1024]{3,2,1,0:T(8,128)} custom-call(s32[1]{0:T(128)} %bitcast.pos, bf16[16,8,1024]{2,1,0:T(8,128)(2,1)S(1)} %get-tuple-element.28.p0, bf16[16,8,1024]{2,1,0:T(8,128)(2,1)S(1)} %collective-permute-done.14.p1, bf16[16,8,1024]{2,1,0:T(8,128)(2,1)S(1)} %collective-permute-done.15.p2, ...), custom_call_target="tpu_custom_call" | custom-call | flops 1048576 | bytes 6291456 | tf_op jit(solution)/shard_map/pallas_call | solution.py:413
  (48 shorter events, 7.4 us)
Async XLA Ops:
  1.3 14.1 %copy-start = (bf16[1024,1024]{1,0:T(8,128)(2,1)S(1)}, bf16[1024,1024]{1,0:T(8,128)(2,1)}, u32[]{:S(2)}) copy-start(bf16[1024,1024]{1,0:T(8,128)(2,1)} %content.1) | copy-start | bytes 6291460
  1.4 43.6 %copy-start.5 = (s32[2,256]{1,0:T(2,128)S(1)}, s32[2,256]{1,0:T(2,128)}, u32[]{:S(2)}) copy-start(s32[2,256]{1,0:T(2,128)} %inverse.1) | copy-start | bytes 6148
  1.4 43.6 %copy-start.6 = (s32[2]{0:T(128)S(1)}, s32[2]{0:T(128)}, u32[]{:S(2)}) copy-start(s32[2]{0:T(128)} %lengths.1) | copy-start | bytes 28
  26.6 14.6 %collective-permute-start.5 = (bf16[128,1024]{1,0:T(8,128)(2,1)S(1)}, bf16[128,1024]{1,0:T(8,128)(2,1)S(1)}, u32[]{:S(2)}, u32[]{:S(2)}) collective-permute-start(bf16[128,1024]{1,0:T(8,128)(2,1)S(1)} %bitcast.13), channel_id=1, source_target_pairs={{0,6},{1,7},{2,4},{3,5},{4,2},{5,3},{6,0},{7,1},{8,14},{9,15},{10,... | collective-permute-start | bytes 786440 | tf_op jit(solution)/shard_map/ppermute | solution.py:425
  30.4 12.1 %collective-permute-start.3 = (bf16[128,1024]{1,0:T(8,128)(2,1)S(1)}, bf16[128,1024]{1,0:T(8,128)(2,1)S(1)}, u32[]{:S(2)}, u32[]{:S(2)}) collective-permute-start(bf16[128,1024]{1,0:T(8,128)(2,1)S(1)} %bitcast.14), channel_id=1, source_target_pairs={{0,4},{1,5},{2,6},{3,7},{4,0},{5,1},{6,2},{7,3},{8,12},{9,13},{10,... | collective-permute-start | bytes 786440 | tf_op jit(solution)/shard_map/ppermute | solution.py:425
  30.4 13.1 %collective-permute-start.1 = (bf16[128,1024]{1,0:T(8,128)(2,1)S(1)}, bf16[128,1024]{1,0:T(8,128)(2,1)S(1)}, u32[]{:S(2)}, u32[]{:S(2)}) collective-permute-start(bf16[128,1024]{1,0:T(8,128)(2,1)S(1)} %bitcast.15), channel_id=1, source_target_pairs={{0,2},{1,3},{2,0},{3,1},{4,6},{5,7},{6,4},{7,5},{8,10},{9,11},{10,... | collective-permute-start | bytes 786440 | tf_op jit(solution)/shard_map/ppermute | solution.py:425
  31.0 12.9 %collective-permute-start = (bf16[128,1024]{1,0:T(8,128)(2,1)S(1)}, bf16[128,1024]{1,0:T(8,128)(2,1)S(1)}, u32[]{:S(2)}, u32[]{:S(2)}) collective-permute-start(bf16[128,1024]{1,0:T(8,128)(2,1)S(1)} %bitcast.16), channel_id=1, source_target_pairs={{0,1},{1,0},{2,3},{3,2},{4,5},{5,4},{6,7},{7,6},{8,9},{9,8},{10,11... | collective-permute-start | bytes 786440 | tf_op jit(solution)/shard_map/ppermute | solution.py:425
  41.2 2.7 %collective-permute-start.6 = (bf16[128,1024]{1,0:T(8,128)(2,1)S(1)}, bf16[128,1024]{1,0:T(8,128)(2,1)S(1)}, u32[]{:S(2)}, u32[]{:S(2)}) collective-permute-start(bf16[128,1024]{1,0:T(8,128)(2,1)S(1)} %collective-permute-done.5.p6), channel_id=1, source_target_pairs={{0,1},{1,0},{2,3},{3,2},{4,5},{5,4},{6,7},{7,6},{8,9},{9,8},{10,11... | collective-permute-start | bytes 786440 | tf_op jit(solution)/shard_map/ppermute | solution.py:425
  42.5 2.1 %collective-permute-start.4 = (bf16[128,1024]{1,0:T(8,128)(2,1)S(1)}, bf16[128,1024]{1,0:T(8,128)(2,1)S(1)}, u32[]{:S(2)}, u32[]{:S(2)}) collective-permute-start(bf16[128,1024]{1,0:T(8,128)(2,1)S(1)} %collective-permute-done.3.p4), channel_id=1, source_target_pairs={{0,1},{1,0},{2,3},{3,2},{4,5},{5,4},{6,7},{7,6},{8,9},{9,8},{10,11... | collective-permute-start | bytes 786440 | tf_op jit(solution)/shard_map/ppermute | solution.py:425
  43.5 1.6 %collective-permute-start.2 = (bf16[128,1024]{1,0:T(8,128)(2,1)S(1)}, bf16[128,1024]{1,0:T(8,128)(2,1)S(1)}, u32[]{:S(2)}, u32[]{:S(2)}) collective-permute-start(bf16[128,1024]{1,0:T(8,128)(2,1)S(1)} %collective-permute-done.1.p2), channel_id=1, source_target_pairs={{0,1},{1,0},{2,3},{3,2},{4,5},{5,4},{6,7},{7,6},{8,9},{9,8},{10,11... | collective-permute-start | bytes 786440 | tf_op jit(solution)/shard_map/ppermute | solution.py:425
  77.0 1.6 %collective-permute-start.8 = (bf16[1024,128]{1,0:T(8,128)(2,1)S(1)}, bf16[1024,128]{1,0:T(8,128)(2,1)S(1)}, u32[]{:S(2)}, u32[]{:S(2)}) collective-permute-start(bf16[1024,128]{1,0:T(8,128)(2,1)S(1)} %get-tuple-element.20), channel_id=1, source_target_pairs={{0,1},{1,0},{2,3},{3,2},{4,5},{5,4},{6,7},{7,6},{8,9},{9,8},{10,11... | collective-permute-start | bytes 786440 | tf_op jit(solution)/shard_map/ppermute | solution.py:425
  77.5 3.8 %collective-permute-start.10 = (bf16[1024,128]{1,0:T(8,128)(2,1)S(1)}, bf16[1024,128]{1,0:T(8,128)(2,1)S(1)}, u32[]{:S(2)}, u32[]{:S(2)}) collective-permute-start(bf16[1024,128]{1,0:T(8,128)(2,1)S(1)} %get-tuple-element.22), channel_id=1, source_target_pairs={{0,1},{1,0},{2,3},{3,2},{4,5},{5,4},{6,7},{7,6},{8,9},{9,8},{10,11... | collective-permute-start | bytes 786440 | tf_op jit(solution)/shard_map/ppermute | solution.py:425
  77.6 4.7 %collective-permute-start.12 = (bf16[1024,128]{1,0:T(8,128)(2,1)S(1)}, bf16[1024,128]{1,0:T(8,128)(2,1)S(1)}, u32[]{:S(2)}, u32[]{:S(2)}) collective-permute-start(bf16[1024,128]{1,0:T(8,128)(2,1)S(1)} %get-tuple-element.24), channel_id=1, source_target_pairs={{0,1},{1,0},{2,3},{3,2},{4,5},{5,4},{6,7},{7,6},{8,9},{9,8},{10,11... | collective-permute-start | bytes 786440 | tf_op jit(solution)/shard_map/ppermute | solution.py:425
  78.0 5.7 %collective-permute-start.7 = (bf16[1024,128]{1,0:T(8,128)(2,1)S(1)}, bf16[1024,128]{1,0:T(8,128)(2,1)S(1)}, u32[]{:S(2)}, u32[]{:S(2)}) collective-permute-start(bf16[1024,128]{1,0:T(8,128)(2,1)S(1)} %get-tuple-element.18), channel_id=1, source_target_pairs={{0,1},{1,0},{2,3},{3,2},{4,5},{5,4},{6,7},{7,6},{8,9},{9,8},{10,11... | collective-permute-start | bytes 786440 | tf_op jit(solution)/shard_map/ppermute | solution.py:425
  78.7 9.1 %collective-permute-start.9 = (bf16[1024,128]{1,0:T(8,128)(2,1)S(1)}, bf16[1024,128]{1,0:T(8,128)(2,1)S(1)}, u32[]{:S(2)}, u32[]{:S(2)}) collective-permute-start(bf16[1024,128]{1,0:T(8,128)(2,1)S(1)} %add.13), channel_id=1, source_target_pairs={{0,4},{1,5},{2,6},{3,7},{4,0},{5,1},{6,2},{7,3},{8,12},{9,13},{10,... | collective-permute-start | bytes 786440 | tf_op jit(solution)/shard_map/ppermute | solution.py:425
  81.4 12.5 %collective-permute-start.11 = (bf16[1024,128]{1,0:T(8,128)(2,1)S(1)}, bf16[1024,128]{1,0:T(8,128)(2,1)S(1)}, u32[]{:S(2)}, u32[]{:S(2)}) collective-permute-start(bf16[1024,128]{1,0:T(8,128)(2,1)S(1)} %add.14), channel_id=1, source_target_pairs={{0,2},{1,3},{2,0},{3,1},{4,6},{5,7},{6,4},{7,5},{8,10},{9,11},{10,... | collective-permute-start | bytes 786440 | tf_op jit(solution)/shard_map/ppermute | solution.py:425
  82.4 11.7 %collective-permute-start.13 = (bf16[1024,128]{1,0:T(8,128)(2,1)S(1)}, bf16[1024,128]{1,0:T(8,128)(2,1)S(1)}, u32[]{:S(2)}, u32[]{:S(2)}) collective-permute-start(bf16[1024,128]{1,0:T(8,128)(2,1)S(1)} %add.15), channel_id=1, source_target_pairs={{0,6},{1,7},{2,4},{3,5},{4,2},{5,3},{6,0},{7,1},{8,14},{9,15},{10,... | collective-permute-start | bytes 786440 | tf_op jit(solution)/shard_map/ppermute | solution.py:425
  124.7 14.0 %collective-permute-start.19 = (bf16[16,8,1024]{2,1,0:T(8,128)(2,1)S(1)}, bf16[16,8,1024]{2,1,0:T(8,128)(2,1)S(1)}, u32[]{:S(2)}, u32[]{:S(2)}) collective-permute-start(bf16[16,8,1024]{2,1,0:T(8,128)(2,1)S(1)} %all_to_all.23.tower_rows), channel_id=1, source_target_pairs={{0,6},{1,7},{2,4},{3,5},{4,2},{5,3},{6,0},{7,1},{8,14},{9,15},{10,... | collective-permute-start | bytes 786440 | tf_op jit(solution)/shard_map/ppermute | solution.py:425
  125.4 14.8 %collective-permute-start.17 = (bf16[16,8,1024]{2,1,0:T(8,128)(2,1)S(1)}, bf16[16,8,1024]{2,1,0:T(8,128)(2,1)S(1)}, u32[]{:S(2)}, u32[]{:S(2)}) collective-permute-start(bf16[16,8,1024]{2,1,0:T(8,128)(2,1)S(1)} %all_to_all.23.tower_rows), channel_id=1, source_target_pairs={{0,4},{1,5},{2,6},{3,7},{4,0},{5,1},{6,2},{7,3},{8,12},{9,13},{10,... | collective-permute-start | bytes 786440 | tf_op jit(solution)/shard_map/ppermute | solution.py:425
  127.6 12.7 %collective-permute-start.15 = (bf16[16,8,1024]{2,1,0:T(8,128)(2,1)S(1)}, bf16[16,8,1024]{2,1,0:T(8,128)(2,1)S(1)}, u32[]{:S(2)}, u32[]{:S(2)}) collective-permute-start(bf16[16,8,1024]{2,1,0:T(8,128)(2,1)S(1)} %all_to_all.23.tower_rows), channel_id=1, source_target_pairs={{0,2},{1,3},{2,0},{3,1},{4,6},{5,7},{6,4},{7,5},{8,10},{9,11},{10,... | collective-permute-start | bytes 786440 | tf_op jit(solution)/shard_map/ppermute | solution.py:425
  131.3 9.6 %collective-permute-start.14 = (bf16[16,8,1024]{2,1,0:T(8,128)(2,1)S(1)}, bf16[16,8,1024]{2,1,0:T(8,128)(2,1)S(1)}, u32[]{:S(2)}, u32[]{:S(2)}) collective-permute-start(bf16[16,8,1024]{2,1,0:T(8,128)(2,1)S(1)} %get-tuple-element.28.p0), channel_id=1, source_target_pairs={{0,1},{1,0},{2,3},{3,2},{4,5},{5,4},{6,7},{7,6},{8,9},{9,8},{10,11... | collective-permute-start | bytes 786440 | tf_op jit(solution)/shard_map/ppermute | solution.py:425
  138.6 2.7 %collective-permute-start.20 = (bf16[16,8,1024]{2,1,0:T(8,128)(2,1)S(1)}, bf16[16,8,1024]{2,1,0:T(8,128)(2,1)S(1)}, u32[]{:S(2)}, u32[]{:S(2)}) collective-permute-start(bf16[16,8,1024]{2,1,0:T(8,128)(2,1)S(1)} %collective-permute-done.19.p6), channel_id=1, source_target_pairs={{0,1},{1,0},{2,3},{3,2},{4,5},{5,4},{6,7},{7,6},{8,9},{9,8},{10,11... | collective-permute-start | bytes 786440 | tf_op jit(solution)/shard_map/ppermute | solution.py:425
  140.2 1.5 %collective-permute-start.18 = (bf16[16,8,1024]{2,1,0:T(8,128)(2,1)S(1)}, bf16[16,8,1024]{2,1,0:T(8,128)(2,1)S(1)}, u32[]{:S(2)}, u32[]{:S(2)}) collective-permute-start(bf16[16,8,1024]{2,1,0:T(8,128)(2,1)S(1)} %collective-permute-done.17.p4), channel_id=1, source_target_pairs={{0,1},{1,0},{2,3},{3,2},{4,5},{5,4},{6,7},{7,6},{8,9},{9,8},{10,11... | collective-permute-start | bytes 786440 | tf_op jit(solution)/shard_map/ppermute | solution.py:425
  140.2 1.9 %collective-permute-start.16 = (bf16[16,8,1024]{2,1,0:T(8,128)(2,1)S(1)}, bf16[16,8,1024]{2,1,0:T(8,128)(2,1)S(1)}, u32[]{:S(2)}, u32[]{:S(2)}) collective-permute-start(bf16[16,8,1024]{2,1,0:T(8,128)(2,1)S(1)} %collective-permute-done.15.p2), channel_id=1, source_target_pairs={{0,1},{1,0},{2,3},{3,2},{4,5},{5,4},{6,7},{7,6},{8,9},{9,8},{10,11... | collective-permute-start | bytes 786440 | tf_op jit(solution)/shard_map/ppermute | solution.py:425
  (4 other events, 13.3 us)

commit v4 on v3

--- a/solution.py
+++ b/solution.py
@@ -136,44 +136,39 @@
     out_load.start()
     grad_load.start()
 
-    @pl.loop(0, 8, unroll=2)
-    def _(i):
-        at = pl.ds(pl.multiple_of(i * 64, 64), 64)
+    @pl.loop(0, 4, unroll=1)
+    def _(i):
+        at = pl.ds(pl.multiple_of(i * 128, 128), 128)
         x = events[at, :].astype(F32)
         r = lax.rsqrt(jnp.mean(x * x, axis=-1, keepdims=True) + 1e-06)
-        inv_rms[at, :] = jnp.broadcast_to(r, (64, 128))
+        inv_rms[at, :] = jnp.broadcast_to(r, (128, 128))
         normed[at, :] = (x * r).astype(BF)
 
     def product(c, into):
-        into[...] = dot(normed[...], w_in[:, pl.ds(pl.multiple_of(c * 256, 256), 256)])
+        into[...] = dot(normed[...], w_in[:, pl.ds(pl.multiple_of(c * 512, 512), 512)])
 
     def activate(c, source):
-        at = pl.ds(pl.multiple_of(c * 256, 256), 256)
+        at = pl.ds(pl.multiple_of(c * 512, 512), 512)
         pre = source[...]
         sigma = sigmoid(pre)
         act = pre * sigma
         hidden[:, at] = act.astype(BF)
         slope[:, at] = (sigma + act * (1.0 - sigma)).astype(BF)
 
-    in_loads[0].wait()
-    in_loads[1].wait()
+    for c in in_loads:
+        c.wait()
     product(0, pre_a)
-    for j in range(2):
-
-        @pl.loop(4 * j, 4 * j + 3 + j)
-        def _(i):
-            product(2 * i + 1, pre_b)
-            activate(2 * i, pre_a)
-            product(jnp.minimum(2 * i + 2, 15), pre_a)
-            activate(2 * i + 1, pre_b)
-
-        if j == 0:
-            in_loads[2].wait()
-            in_loads[3].wait()
-            product(7, pre_b)
-            activate(6, pre_a)
-            product(8, pre_a)
-            activate(7, pre_b)
+
+    @pl.loop(0, 3)
+    def _(i):
+        product(2 * i + 1, pre_b)
+        activate(2 * i, pre_a)
+        product(2 * i + 2, pre_a)
+        activate(2 * i + 1, pre_b)
+
+    product(7, pre_b)
+    activate(6, pre_a)
+    activate(7, pre_b)
 
     scale = 128 ** (-0.5)
     out_load.wait()
@@ -212,8 +207,7 @@
         gate = hidden[at, 0:D].astype(F32)
         half[at, :] = (normal * gate).astype(BF)
         dg = dgated[at, :].astype(F32)
-        dgate = (dg * normal).astype(BF).astype(F32)
-        dpre[at, 0:D] = (dgate * slope[at, 0:D].astype(F32)).astype(BF)
+        dpre[at, 0:D] = (dg * normal).astype(BF) * slope[at, 0:D]
         dnormal = dg * gate
         m1 = jnp.mean(dnormal, axis=-1, keepdims=True)
         m2 = jnp.mean(dnormal * normal, axis=-1, keepdims=True)
@@ -225,12 +219,11 @@
         head = lambda h, base: pl.ds(pl.multiple_of(base + h * 128, 128), 128)
 
         def put(h, rows, base, d):
-            d = d.astype(BF).astype(F32) * slope[rows, head(h, base)].astype(F32)
-            dpre[rows, head(h, base)] = d.astype(BF)
+            dpre[rows, head(h, base)] = d.astype(BF) * slope[rows, head(h, base)]
 
         dws = [dot_nt(dmixed[rows, head(h, 0)], hidden[rows, head(h, D)]) for h, b, rows in jobs]
         dss = [
-            (dw.astype(BF).astype(F32) * attn_slope[h, b].astype(F32)).astype(BF)
+            dw.astype(BF) * attn_slope[h, b]
             for dw, (h, b, rows) in zip(dws, jobs)
         ]
         for h, b, rows in jobs:
@@ -247,12 +240,12 @@
     @pl.loop(0, 2)
     def _(c):
         at = pl.ds(pl.multiple_of(c * 512, 512), 512)
-        mixed[:, at] = dot_nt(dpre[...], w_in[at, :]).astype(BF).astype(F32)
-
-    @pl.loop(0, 8, unroll=2)
-    def _(i):
-        at = pl.ds(pl.multiple_of(i * 64, 64), 64)
-        dn = mixed[at, :]
+        normed[:, at] = dot_nt(dpre[...], w_in[at, :]).astype(BF)
+
+    @pl.loop(0, 4, unroll=1)
+    def _(i):
+        at = pl.ds(pl.multiple_of(i * 128, 128), 128)
+        dn = normed[at, :].astype(F32)
         r = inv_rms[at, 0:1]
         unit = events[at, :].astype(F32) * r
         dx = r * (dn - unit * jnp.mean(dn * unit, axis=-1, keepdims=True))
@@ -284,7 +277,7 @@
             vm((ROWS, D), F32), vm((ROWS, D), BF), vm((ROWS, D), BF), vm((ROWS, D), BF), vm((ROWS, 4 * D), BF),
             vm((2, SEQ, SEQ), F32), vm((ROWS, 128), F32),
             vm((ROWS, SLOTS), BF), vm((SLOTS, ROWS), BF),
-            vm((ROWS, 256), F32), vm((ROWS, 256), F32),
+            vm((ROWS, 512), F32), vm((ROWS, 512), F32),
             pltpu.SemaphoreType.DMA((3,)), pltpu.SemaphoreType.DMA((4,)), pltpu.SemaphoreType.DMA,
         ],
         compiler_params=pltpu.CompilerParams(vmem_limit_bytes=50 * MIB),

time: 145 us -> 143 us (0.986)
  no operation moved by 1% of the time
where the time goes in v4:
time: 143 us
  blocking collectives  54.4 us (38%)
  Pallas kernels  38.2 us (27%)
  starting transfers between devices  24.2 us (17%)
  waiting for transfers between devices  24.2 us (17%)
    pallas_call x1, Pallas kernels, layer(): pl.pallas_call(layer_kernel, out_shape=[jax.ShapeDtypeStruct((ROWS, D), B...  30.5 us
    ppermute x21, waiting for transfers between devices, swap(): return lax.ppermute(x, 'local', [(i, i ^ s) for i in range(LOCALS)])  24.2 us
    ppermute x21, starting transfers between devices, swap(): return lax.ppermute(x, 'local', [(i, i ^ s) for i in range(LOCALS)])  24.2 us
    all_to_all x1, blocking collectives, body(): lax.all_to_all(out, ('node', 'local'), 0, 0, tiled=True)  19.3 us
    all_to_all x1, blocking collectives, body(): wanted = lax.all_to_all(asked, 'node', 0, 0, tiled=True)  14 us
    all_to_all x1, blocking collectives, body(): fetched = lax.all_to_all(picked, 'node', 0, 0, tiled=True).reshape(128, D)  10.7 us
    all_to_all x1, blocking collectives, body(): rows = lax.all_to_all(total(back), 'node', 0, 0, tiled=True)  10.4 us
    pallas_call x1, Pallas kernels, content_side(): pl.pallas_call(content_kernel, out_shape=[jax.ShapeDtypeStruct((1024, D),...  3.36 us
  transfers between devices with their start and end apart: 21, of which 11 were waited for; matrix products, arithmetic and copies ran while one was open for 0% of the time, Pallas kernels for 3%

profile of v4, /device:TPU:1, one launch (start us, length us, event | category | flops | bytes accessed | tf_op | source)
XLA Modules:
  0.0 143.0 jit_solution(1443164369063199854)
XLA Ops:
  1.4 14.0 %all_to_all.20.wanted = s32[16,8,128]{2,1,0:T(8,128)S(1)} all-to-all(s32[16,8,128]{2,1,0:T(8,128)S(1)} %shard_map.103), channel_id=1, replica_groups=mesh['node'=16,'local'=8] {'node'}, dimensions={0} | all-to-all | bytes 131072 | tf_op jit(solution)/shard_map/all_to_all | solution.py:435
  15.9 10.7 %all_to_all.21 = bf16[16,8,1024]{2,1,0:T(8,128)(2,1)S(1)} all-to-all(bf16[16,8,1024]{2,1,0:T(8,128)(2,1)S(1)} %shard_map.104), channel_id=1, replica_groups=mesh['node'=16,'local'=8] {'node'}, dimensions={0} | all-to-all | bytes 524288 | tf_op jit(solution)/shard_map/all_to_all | solution.py:437
  26.6 3.8 %collective-permute-start.5 = (bf16[128,1024]{1,0:T(8,128)(2,1)S(1)}, bf16[128,1024]{1,0:T(8,128)(2,1)S(1)}, u32[]{:S(2)}, u32[]{:S(2)}) collective-permute-start(bf16[128,1024]{1,0:T(8,128)(2,1)S(1)} %bitcast.13), channel_id=1, source_target_pairs={{0,6},{1,7},{2,4},{3,5},{4,2},{5,3},{6,0},{7,1},{8,14},{9,15},{10,... | collective-permute-start | bytes 786440 | tf_op jit(solution)/shard_map/ppermute | solution.py:418
  31.0 3.8 %collective-permute-start = (bf16[128,1024]{1,0:T(8,128)(2,1)S(1)}, bf16[128,1024]{1,0:T(8,128)(2,1)S(1)}, u32[]{:S(2)}, u32[]{:S(2)}) collective-permute-start(bf16[128,1024]{1,0:T(8,128)(2,1)S(1)} %bitcast.16), channel_id=1, source_target_pairs={{0,1},{1,0},{2,3},{3,2},{4,5},{5,4},{6,7},{7,6},{8,9},{9,8},{10,11... | collective-permute-start | bytes 786440 | tf_op jit(solution)/shard_map/ppermute | solution.py:418
  34.8 6.4 %collective-permute-done.5.p6 = bf16[128,1024]{1,0:T(8,128)(2,1)S(1)} collective-permute-done((bf16[128,1024]{1,0:T(8,128)(2,1)S(1)}, bf16[128,1024]{1,0:T(8,128)(2,1)S(1)}, u32[]{:S(2)}, u32[]{:S(2)}) %collective-permute-start.5) | collective-permute-done | bytes 262176 | tf_op jit(solution)/shard_map/ppermute | solution.py:418
  41.2 1.3 collective-permute-start.6
  42.5 0.9 collective-permute-start.4
  43.9 0.7 collective-permute-done.4.p5
  45.0 30.5 %shard_map.105 = (bf16[512,1024]{1,0:T(8,128)(2,1)}, bf16[1024,128]{1,0:T(8,128)(2,1)S(1)}, bf16[1024,128]{1,0:T(8,128)(2,1)S(1)}, bf16[1024,128]{1,0:T(8,128)(2...) custom-call(s32[1]{0:T(128)} %bitcast.pos, ...), custom_call_target="tpu_custom_call" | custom-call | flops 14000000000 | bytes 18874368 | tf_op jit(solution)/shard_map/pallas_call | solution.py:268
  77.3 2.6 %collective-permute-start.9 = (bf16[1024,128]{1,0:T(8,128)(2,1)S(1)}, bf16[1024,128]{1,0:T(8,128)(2,1)S(1)}, u32[]{:S(2)}, u32[]{:S(2)}) collective-permute-start(bf16[1024,128]{1,0:T(8,128)(2,1)S(1)} %add.13), channel_id=1, source_target_pairs={{0,4},{1,5},{2,6},{3,7},{4,0},{5,1},{6,2},{7,3},{8,12},{9,13},{10,... | collective-permute-start | bytes 786440 | tf_op jit(solution)/shard_map/ppermute | solution.py:418
  79.9 1.0 collective-permute-start.11
  81.3 0.9 shard_map.106
  82.3 4.0 %collective-permute-done.9.a1 = bf16[1024,128]{1,0:T(8,128)(2,1)S(1)} collective-permute-done((bf16[1024,128]{1,0:T(8,128)(2,1)S(1)}, bf16[1024,128]{1,0:T(8,128)(2,1)S(1)}, u32[]{:S(2)}, u32[]{:S(2)}) %collective-permute-start.9) | collective-permute-done | bytes 262176 | tf_op jit(solution)/shard_map/ppermute | solution.py:418
  86.4 6.1 %collective-permute-done.11.a2 = bf16[1024,128]{1,0:T(8,128)(2,1)S(1)} collective-permute-done((bf16[1024,128]{1,0:T(8,128)(2,1)S(1)}, bf16[1024,128]{1,0:T(8,128)(2,1)S(1)}, u32[]{:S(2)}, u32[]{:S(2)}) %collective-permute-start.11) | collective-permute-done | bytes 262176 | tf_op jit(solution)/shard_map/ppermute | solution.py:418
  92.7 0.8 shard_map.107
  93.5 19.3 %all_to_all.22 = bf16[128,16,128]{2,1,0:T(8,128)(2,1)S(1)} all-to-all(bf16[128,16,128]{2,1,0:T(8,128)(2,1)S(1)} %bitcast.12), channel_id=1, replica_groups=mesh['node'=16,'local'=8] {'node','local'}, dimensions={0} | all-to-all | bytes 1048576 | tf_op jit(solution)/shard_map/all_to_all | solution.py:447
  112.8 10.4 %all_to_all.23.tower_rows = bf16[16,8,1024]{2,1,0:T(8,128)(2,1)S(1)} all-to-all(bf16[16,8,1024]{2,1,0:T(8,128)(2,1)S(1)} %shard_map.108), channel_id=1, replica_groups=mesh['node'=16,'local'=8] {'node'}, dimensions={0} | all-to-all | bytes 524288 | tf_op jit(solution)/shard_map/all_to_all | solution.py:448
  123.2 0.7 collective-permute-start.19
  123.9 2.2 %collective-permute-start.17 = (bf16[16,8,1024]{2,1,0:T(8,128)(2,1)S(1)}, bf16[16,8,1024]{2,1,0:T(8,128)(2,1)S(1)}, u32[]{:S(2)}, u32[]{:S(2)}) collective-permute-start(bf16[16,8,1024]{2,1,0:T(8,128)(2,1)S(1)} %all_to_all.23.tower_rows), channel_id=1, source_target_pairs={{0,4},{1,5},{2,6},{3,7},{4,0},{5,1},{6,2},{7,3},{8,12},{9,13},{10,... | collective-permute-start | bytes 786440 | tf_op jit(solution)/shard_map/ppermute | solution.py:418
  126.5 3.4 %shard_map.109 = (bf16[1024,1024]{1,0:T(8,128)(2,1)}, bf16[16,8,1024]{2,1,0:T(8,128)(2,1)S(1)}) custom-call(s32[16,8,128]{2,1,0:T(8,128)S(1)} %all_to_all.20.wanted, bf16[16,8,16,128]{3,2,1,0:T(8,128)(2,1)S(1)} %bitcast.11, bf16[1024,1024]{1,0:T(8,128)(2,1)S(1)} %copy-done.1, bf16[16,8,1024]{2,1,0:T(8,128)(2,1)S(1)} %all_to_all.23.tower_rows), custom_call_target="tpu_custom_call" | custom-call | flops 805306368 | bytes 5242880 | tf_op jit(solution)/shard_map/pallas_call | solution.py:379
  129.8 2.9 %collective-permute-start.14 = (bf16[16,8,1024]{2,1,0:T(8,128)(2,1)S(1)}, bf16[16,8,1024]{2,1,0:T(8,128)(2,1)S(1)}, u32[]{:S(2)}, u32[]{:S(2)}) collective-permute-start(bf16[16,8,1024]{2,1,0:T(8,128)(2,1)S(1)} %get-tuple-element.28.p0), channel_id=1, source_target_pairs={{0,1},{1,0},{2,3},{3,2},{4,5},{5,4},{6,7},{7,6},{8,9},{9,8},{10,11... | collective-permute-start | bytes 786440 | tf_op jit(solution)/shard_map/ppermute | solution.py:418
  132.8 4.4 %collective-permute-done.19.p6 = bf16[16,8,1024]{2,1,0:T(8,128)(2,1)S(1)} collective-permute-done((bf16[16,8,1024]{2,1,0:T(8,128)(2,1)S(1)}, bf16[16,8,1024]{2,1,0:T(8,128)(2,1)S(1)}, u32[]{:S(2)}, u32[]{:S(2)}) %collective-permute-start.19) | collective-permute-done | bytes 262176 | tf_op jit(solution)/shard_map/ppermute | solution.py:418
  137.2 1.6 %collective-permute-start.20 = (bf16[16,8,1024]{2,1,0:T(8,128)(2,1)S(1)}, bf16[16,8,1024]{2,1,0:T(8,128)(2,1)S(1)}, u32[]{:S(2)}, u32[]{:S(2)}) collective-permute-start(bf16[16,8,1024]{2,1,0:T(8,128)(2,1)S(1)} %collective-permute-done.19.p6), channel_id=1, source_target_pairs={{0,1},{1,0},{2,3},{3,2},{4,5},{5,4},{6,7},{7,6},{8,9},{9,8},{10,11... | collective-permute-start | bytes 786440 | tf_op jit(solution)/shard_map/ppermute | solution.py:418
  140.7 2.1 %shard_map.110 = f32[16,8,8,1024]{3,2,1,0:T(8,128)} custom-call(s32[1]{0:T(128)} %bitcast.pos, bf16[16,8,1024]{2,1,0:T(8,128)(2,1)S(1)} %get-tuple-element.28.p0, bf16[16,8,1024]{2,1,0:T(8,128)(2,1)S(1)} %collective-permute-done.14.p1, bf16[16,8,1024]{2,1,0:T(8,128)(2,1)S(1)} %collective-permute-done.15.p2, ...), custom_call_target="tpu_custom_call" | custom-call | flops 1048576 | bytes 6291456 | tf_op jit(solution)/shard_map/pallas_call | solution.py:406
  (48 shorter events, 7.5 us)
Async XLA Ops:
  1.3 14.1 %copy-start = (bf16[1024,1024]{1,0:T(8,128)(2,1)S(1)}, bf16[1024,1024]{1,0:T(8,128)(2,1)}, u32[]{:S(2)}) copy-start(bf16[1024,1024]{1,0:T(8,128)(2,1)} %content.1) | copy-start | bytes 6291460
  1.4 43.6 %copy-start.5 = (s32[2,256]{1,0:T(2,128)S(1)}, s32[2,256]{1,0:T(2,128)}, u32[]{:S(2)}) copy-start(s32[2,256]{1,0:T(2,128)} %inverse.1) | copy-start | bytes 6148
  1.4 43.6 %copy-start.6 = (s32[2]{0:T(128)S(1)}, s32[2]{0:T(128)}, u32[]{:S(2)}) copy-start(s32[2]{0:T(128)} %lengths.1) | copy-start | bytes 28
  26.6 14.6 %collective-permute-start.5 = (bf16[128,1024]{1,0:T(8,128)(2,1)S(1)}, bf16[128,1024]{1,0:T(8,128)(2,1)S(1)}, u32[]{:S(2)}, u32[]{:S(2)}) collective-permute-start(bf16[128,1024]{1,0:T(8,128)(2,1)S(1)} %bitcast.13), channel_id=1, source_target_pairs={{0,6},{1,7},{2,4},{3,5},{4,2},{5,3},{6,0},{7,1},{8,14},{9,15},{10,... | collective-permute-start | bytes 786440 | tf_op jit(solution)/shard_map/ppermute | solution.py:418
  30.4 12.1 %collective-permute-start.3 = (bf16[128,1024]{1,0:T(8,128)(2,1)S(1)}, bf16[128,1024]{1,0:T(8,128)(2,1)S(1)}, u32[]{:S(2)}, u32[]{:S(2)}) collective-permute-start(bf16[128,1024]{1,0:T(8,128)(2,1)S(1)} %bitcast.14), channel_id=1, source_target_pairs={{0,4},{1,5},{2,6},{3,7},{4,0},{5,1},{6,2},{7,3},{8,12},{9,13},{10,... | collective-permute-start | bytes 786440 | tf_op jit(solution)/shard_map/ppermute | solution.py:418
  30.4 13.1 %collective-permute-start.1 = (bf16[128,1024]{1,0:T(8,128)(2,1)S(1)}, bf16[128,1024]{1,0:T(8,128)(2,1)S(1)}, u32[]{:S(2)}, u32[]{:S(2)}) collective-permute-start(bf16[128,1024]{1,0:T(8,128)(2,1)S(1)} %bitcast.15), channel_id=1, source_target_pairs={{0,2},{1,3},{2,0},{3,1},{4,6},{5,7},{6,4},{7,5},{8,10},{9,11},{10,... | collective-permute-start | bytes 786440 | tf_op jit(solution)/shard_map/ppermute | solution.py:418
  31.0 12.9 %collective-permute-start = (bf16[128,1024]{1,0:T(8,128)(2,1)S(1)}, bf16[128,1024]{1,0:T(8,128)(2,1)S(1)}, u32[]{:S(2)}, u32[]{:S(2)}) collective-permute-start(bf16[128,1024]{1,0:T(8,128)(2,1)S(1)} %bitcast.16), channel_id=1, source_target_pairs={{0,1},{1,0},{2,3},{3,2},{4,5},{5,4},{6,7},{7,6},{8,9},{9,8},{10,11... | collective-permute-start | bytes 786440 | tf_op jit(solution)/shard_map/ppermute | solution.py:418
  41.2 2.7 %collective-permute-start.6 = (bf16[128,1024]{1,0:T(8,128)(2,1)S(1)}, bf16[128,1024]{1,0:T(8,128)(2,1)S(1)}, u32[]{:S(2)}, u32[]{:S(2)}) collective-permute-start(bf16[128,1024]{1,0:T(8,128)(2,1)S(1)} %collective-permute-done.5.p6), channel_id=1, source_target_pairs={{0,1},{1,0},{2,3},{3,2},{4,5},{5,4},{6,7},{7,6},{8,9},{9,8},{10,11... | collective-permute-start | bytes 786440 | tf_op jit(solution)/shard_map/ppermute | solution.py:418
  42.5 2.1 %collective-permute-start.4 = (bf16[128,1024]{1,0:T(8,128)(2,1)S(1)}, bf16[128,1024]{1,0:T(8,128)(2,1)S(1)}, u32[]{:S(2)}, u32[]{:S(2)}) collective-permute-start(bf16[128,1024]{1,0:T(8,128)(2,1)S(1)} %collective-permute-done.3.p4), channel_id=1, source_target_pairs={{0,1},{1,0},{2,3},{3,2},{4,5},{5,4},{6,7},{7,6},{8,9},{9,8},{10,11... | collective-permute-start | bytes 786440 | tf_op jit(solution)/shard_map/ppermute | solution.py:418
  43.5 1.6 %collective-permute-start.2 = (bf16[128,1024]{1,0:T(8,128)(2,1)S(1)}, bf16[128,1024]{1,0:T(8,128)(2,1)S(1)}, u32[]{:S(2)}, u32[]{:S(2)}) collective-permute-start(bf16[128,1024]{1,0:T(8,128)(2,1)S(1)} %collective-permute-done.1.p2), channel_id=1, source_target_pairs={{0,1},{1,0},{2,3},{3,2},{4,5},{5,4},{6,7},{7,6},{8,9},{9,8},{10,11... | collective-permute-start | bytes 786440 | tf_op jit(solution)/shard_map/ppermute | solution.py:418
  75.6 1.6 %collective-permute-start.8 = (bf16[1024,128]{1,0:T(8,128)(2,1)S(1)}, bf16[1024,128]{1,0:T(8,128)(2,1)S(1)}, u32[]{:S(2)}, u32[]{:S(2)}) collective-permute-start(bf16[1024,128]{1,0:T(8,128)(2,1)S(1)} %get-tuple-element.20), channel_id=1, source_target_pairs={{0,1},{1,0},{2,3},{3,2},{4,5},{5,4},{6,7},{7,6},{8,9},{9,8},{10,11... | collective-permute-start | bytes 786440 | tf_op jit(solution)/shard_map/ppermute | solution.py:418
  76.0 3.8 %collective-permute-start.10 = (bf16[1024,128]{1,0:T(8,128)(2,1)S(1)}, bf16[1024,128]{1,0:T(8,128)(2,1)S(1)}, u32[]{:S(2)}, u32[]{:S(2)}) collective-permute-start(bf16[1024,128]{1,0:T(8,128)(2,1)S(1)} %get-tuple-element.22), channel_id=1, source_target_pairs={{0,1},{1,0},{2,3},{3,2},{4,5},{5,4},{6,7},{7,6},{8,9},{9,8},{10,11... | collective-permute-start | bytes 786440 | tf_op jit(solution)/shard_map/ppermute | solution.py:418
  76.2 4.7 %collective-permute-start.12 = (bf16[1024,128]{1,0:T(8,128)(2,1)S(1)}, bf16[1024,128]{1,0:T(8,128)(2,1)S(1)}, u32[]{:S(2)}, u32[]{:S(2)}) collective-permute-start(bf16[1024,128]{1,0:T(8,128)(2,1)S(1)} %get-tuple-element.24), channel_id=1, source_target_pairs={{0,1},{1,0},{2,3},{3,2},{4,5},{5,4},{6,7},{7,6},{8,9},{9,8},{10,11... | collective-permute-start | bytes 786440 | tf_op jit(solution)/shard_map/ppermute | solution.py:418
  76.5 5.7 %collective-permute-start.7 = (bf16[1024,128]{1,0:T(8,128)(2,1)S(1)}, bf16[1024,128]{1,0:T(8,128)(2,1)S(1)}, u32[]{:S(2)}, u32[]{:S(2)}) collective-permute-start(bf16[1024,128]{1,0:T(8,128)(2,1)S(1)} %get-tuple-element.18), channel_id=1, source_target_pairs={{0,1},{1,0},{2,3},{3,2},{4,5},{5,4},{6,7},{7,6},{8,9},{9,8},{10,11... | collective-permute-start | bytes 786440 | tf_op jit(solution)/shard_map/ppermute | solution.py:418
  77.3 9.1 %collective-permute-start.9 = (bf16[1024,128]{1,0:T(8,128)(2,1)S(1)}, bf16[1024,128]{1,0:T(8,128)(2,1)S(1)}, u32[]{:S(2)}, u32[]{:S(2)}) collective-permute-start(bf16[1024,128]{1,0:T(8,128)(2,1)S(1)} %add.13), channel_id=1, source_target_pairs={{0,4},{1,5},{2,6},{3,7},{4,0},{5,1},{6,2},{7,3},{8,12},{9,13},{10,... | collective-permute-start | bytes 786440 | tf_op jit(solution)/shard_map/ppermute | solution.py:418
  79.9 12.5 %collective-permute-start.11 = (bf16[1024,128]{1,0:T(8,128)(2,1)S(1)}, bf16[1024,128]{1,0:T(8,128)(2,1)S(1)}, u32[]{:S(2)}, u32[]{:S(2)}) collective-permute-start(bf16[1024,128]{1,0:T(8,128)(2,1)S(1)} %add.14), channel_id=1, source_target_pairs={{0,2},{1,3},{2,0},{3,1},{4,6},{5,7},{6,4},{7,5},{8,10},{9,11},{10,... | collective-permute-start | bytes 786440 | tf_op jit(solution)/shard_map/ppermute | solution.py:418
  81.0 11.7 %collective-permute-start.13 = (bf16[1024,128]{1,0:T(8,128)(2,1)S(1)}, bf16[1024,128]{1,0:T(8,128)(2,1)S(1)}, u32[]{:S(2)}, u32[]{:S(2)}) collective-permute-start(bf16[1024,128]{1,0:T(8,128)(2,1)S(1)} %add.15), channel_id=1, source_target_pairs={{0,6},{1,7},{2,4},{3,5},{4,2},{5,3},{6,0},{7,1},{8,14},{9,15},{10,... | collective-permute-start | bytes 786440 | tf_op jit(solution)/shard_map/ppermute | solution.py:418
  123.2 14.0 %collective-permute-start.19 = (bf16[16,8,1024]{2,1,0:T(8,128)(2,1)S(1)}, bf16[16,8,1024]{2,1,0:T(8,128)(2,1)S(1)}, u32[]{:S(2)}, u32[]{:S(2)}) collective-permute-start(bf16[16,8,1024]{2,1,0:T(8,128)(2,1)S(1)} %all_to_all.23.tower_rows), channel_id=1, source_target_pairs={{0,6},{1,7},{2,4},{3,5},{4,2},{5,3},{6,0},{7,1},{8,14},{9,15},{10,... | collective-permute-start | bytes 786440 | tf_op jit(solution)/shard_map/ppermute | solution.py:418
  123.9 14.8 %collective-permute-start.17 = (bf16[16,8,1024]{2,1,0:T(8,128)(2,1)S(1)}, bf16[16,8,1024]{2,1,0:T(8,128)(2,1)S(1)}, u32[]{:S(2)}, u32[]{:S(2)}) collective-permute-start(bf16[16,8,1024]{2,1,0:T(8,128)(2,1)S(1)} %all_to_all.23.tower_rows), channel_id=1, source_target_pairs={{0,4},{1,5},{2,6},{3,7},{4,0},{5,1},{6,2},{7,3},{8,12},{9,13},{10,... | collective-permute-start | bytes 786440 | tf_op jit(solution)/shard_map/ppermute | solution.py:418
  126.1 12.7 %collective-permute-start.15 = (bf16[16,8,1024]{2,1,0:T(8,128)(2,1)S(1)}, bf16[16,8,1024]{2,1,0:T(8,128)(2,1)S(1)}, u32[]{:S(2)}, u32[]{:S(2)}) collective-permute-start(bf16[16,8,1024]{2,1,0:T(8,128)(2,1)S(1)} %all_to_all.23.tower_rows), channel_id=1, source_target_pairs={{0,2},{1,3},{2,0},{3,1},{4,6},{5,7},{6,4},{7,5},{8,10},{9,11},{10,... | collective-permute-start | bytes 786440 | tf_op jit(solution)/shard_map/ppermute | solution.py:418
  129.8 9.6 %collective-permute-start.14 = (bf16[16,8,1024]{2,1,0:T(8,128)(2,1)S(1)}, bf16[16,8,1024]{2,1,0:T(8,128)(2,1)S(1)}, u32[]{:S(2)}, u32[]{:S(2)}) collective-permute-start(bf16[16,8,1024]{2,1,0:T(8,128)(2,1)S(1)} %get-tuple-element.28.p0), channel_id=1, source_target_pairs={{0,1},{1,0},{2,3},{3,2},{4,5},{5,4},{6,7},{7,6},{8,9},{9,8},{10,11... | collective-permute-start | bytes 786440 | tf_op jit(solution)/shard_map/ppermute | solution.py:418
  137.2 2.7 %collective-permute-start.20 = (bf16[16,8,1024]{2,1,0:T(8,128)(2,1)S(1)}, bf16[16,8,1024]{2,1,0:T(8,128)(2,1)S(1)}, u32[]{:S(2)}, u32[]{:S(2)}) collective-permute-start(bf16[16,8,1024]{2,1,0:T(8,128)(2,1)S(1)} %collective-permute-done.19.p6), channel_id=1, source_target_pairs={{0,1},{1,0},{2,3},{3,2},{4,5},{5,4},{6,7},{7,6},{8,9},{9,8},{10,11... | collective-permute-start | bytes 786440 | tf_op jit(solution)/shard_map/ppermute | solution.py:418
  138.8 1.5 %collective-permute-start.18 = (bf16[16,8,1024]{2,1,0:T(8,128)(2,1)S(1)}, bf16[16,8,1024]{2,1,0:T(8,128)(2,1)S(1)}, u32[]{:S(2)}, u32[]{:S(2)}) collective-permute-start(bf16[16,8,1024]{2,1,0:T(8,128)(2,1)S(1)} %collective-permute-done.17.p4), channel_id=1, source_target_pairs={{0,1},{1,0},{2,3},{3,2},{4,5},{5,4},{6,7},{7,6},{8,9},{9,8},{10,11... | collective-permute-start | bytes 786440 | tf_op jit(solution)/shard_map/ppermute | solution.py:418
  138.8 1.9 %collective-permute-start.16 = (bf16[16,8,1024]{2,1,0:T(8,128)(2,1)S(1)}, bf16[16,8,1024]{2,1,0:T(8,128)(2,1)S(1)}, u32[]{:S(2)}, u32[]{:S(2)}) collective-permute-start(bf16[16,8,1024]{2,1,0:T(8,128)(2,1)S(1)} %collective-permute-done.15.p2), channel_id=1, source_target_pairs={{0,1},{1,0},{2,3},{3,2},{4,5},{5,4},{6,7},{7,6},{8,9},{9,8},{10,11... | collective-permute-start | bytes 786440 | tf_op jit(solution)/shard_map/ppermute | solution.py:418
  (4 other events, 13.3 us)

commit v5 on v4

--- a/solution.py
+++ b/solution.py
@@ -391,27 +391,29 @@
     )(wanted, arrived, w_tower, tower_rows)
 
 
-def tower_kernel(pos, p0, p1, p2, p3, p4, p5, p6, p7, out, buf, sem):
+def tower_kernel(which, pos, *refs):
+    pieces, out, buf, sem = refs[:4], refs[-3], refs[-2], refs[-1]
     me = pos[0]
     copies = []
-    for s, piece in enumerate((p0, p1, p2, p3, p4, p5, p6, p7)):
-        buf[s] = piece[...].astype(F32)
-        copies.append(pltpu.make_async_copy(buf.at[s], out.at[:, me ^ s], sem.at[s]))
+    for i, (s, piece) in enumerate(zip(which, pieces)):
+        buf[i] = piece[...].astype(F32)
+        copies.append(pltpu.make_async_copy(buf.at[i], out.at[:, me ^ s], sem.at[i]))
         copies[-1].start()
     for c in copies:
         c.wait()
 
 
-def tower_side(pos, pieces):
-    return pl.pallas_call(
-        tower_kernel,
+def tower_side(which, pos, pieces, *begun):
+    return pl.pallas_call(
+        functools.partial(tower_kernel, which),
         out_shape=jax.ShapeDtypeStruct((NODES, LOCALS, 8, D), F32),
-        in_specs=[SMEM] + [VMEM] * 8,
+        in_specs=[SMEM] + [VMEM] * 4 + [ANY] * len(begun),
         out_specs=ANY,
-        scratch_shapes=[pltpu.VMEM((8, NODES, 8, D), F32), pltpu.SemaphoreType.DMA((8,))],
+        scratch_shapes=[pltpu.VMEM((4, NODES, 8, D), F32), pltpu.SemaphoreType.DMA((4,))],
+        input_output_aliases={5: 0} if begun else {},
         compiler_params=pltpu.CompilerParams(vmem_limit_bytes=16 * MIB),
-        cost_estimate=pl.CostEstimate(flops=MIB, bytes_accessed=6 * MIB, transcendentals=0),
-    )(pos, *pieces)
+        cost_estimate=pl.CostEstimate(flops=MIB, bytes_accessed=3 * MIB, transcendentals=0),
+    )(pos, *[pieces[s] for s in which], *begun)
 
 
 def swap(x, s):
@@ -447,7 +449,9 @@
     back = lax.all_to_all(out, ("node", "local"), 0, 0, tiled=True).reshape(NODES, LOCALS, 16, 128)
     rows = lax.all_to_all(total(back), "node", 0, 0, tiled=True)
     content_grad, handed = content_side(wanted, back, w_tower, rows)
-    tower_grad = tower_side(pos, gather_local(rows, handed)).reshape(D, D)
+    near = gather_local(rows, handed)
+    begun = tower_side((0, 2, 4, 6), pos, near)
+    tower_grad = tower_side((1, 3, 5, 7), pos, near, begun).reshape(D, D)
     return (events_out.reshape(2, SEQ, D), content_grad, tower_grad)
 
 

time: 143 us -> 143 us (level)
  transfers between devices with their start and end apart: 21 -> 21, of which waited for: 11 -> 8; matrix products, arithmetic and copies ran while one was open for 0% -> 0% of each run, Pallas kernels for 3% -> 4%
where the time goes in v5:
time: 143 us; the launch traced here: 142 us
  blocking collectives  54.4 us (38%)
  Pallas kernels  38.9 us (27%)
  starting transfers between devices  24.2 us (17%)
  waiting for transfers between devices  22.9 us (16%)
    pallas_call x1, Pallas kernels, layer(): pl.pallas_call(layer_kernel, out_shape=[jax.ShapeDtypeStruct((ROWS, D), B...  30.5 us
    ppermute x21, starting transfers between devices, swap(): return lax.ppermute(x, 'local', [(i, i ^ s) for i in range(LOCALS)])  24.2 us
    ppermute x21, waiting for transfers between devices, swap(): return lax.ppermute(x, 'local', [(i, i ^ s) for i in range(LOCALS)])  22.9 us
    all_to_all x1, blocking collectives, body(): lax.all_to_all(out, ('node', 'local'), 0, 0, tiled=True)  19.3 us
    all_to_all x1, blocking collectives, body(): wanted = lax.all_to_all(asked, 'node', 0, 0, tiled=True)  14 us
    all_to_all x1, blocking collectives, body(): fetched = lax.all_to_all(picked, 'node', 0, 0, tiled=True).reshape(128, D)  10.7 us
    all_to_all x1, blocking collectives, body(): rows = lax.all_to_all(total(back), 'node', 0, 0, tiled=True)  10.4 us
    pallas_call x1, Pallas kernels, content_side(): pl.pallas_call(content_kernel, out_shape=[jax.ShapeDtypeStruct((1024, D),...  3.36 us
  transfers between devices with their start and end apart: 21, of which 8 were waited for; matrix products, arithmetic and copies ran while one was open for 0% of the time, Pallas kernels for 4%

profile of v5, /device:TPU:1, one launch (start us, length us, event | category | flops | bytes accessed | tf_op | source)
XLA Modules:
  0.0 142.4 jit_solution(9297068751251201803)
XLA Ops:
  1.4 14.0 %all_to_all.20.wanted = s32[16,8,128]{2,1,0:T(8,128)S(1)} all-to-all(s32[16,8,128]{2,1,0:T(8,128)S(1)} %shard_map.103), channel_id=1, replica_groups=mesh['node'=16,'local'=8] {'node'}, dimensions={0} | all-to-all | bytes 131072 | tf_op jit(solution)/shard_map/all_to_all | solution.py:437
  15.9 10.7 %all_to_all.21 = bf16[16,8,1024]{2,1,0:T(8,128)(2,1)S(1)} all-to-all(bf16[16,8,1024]{2,1,0:T(8,128)(2,1)S(1)} %shard_map.104), channel_id=1, replica_groups=mesh['node'=16,'local'=8] {'node'}, dimensions={0} | all-to-all | bytes 524288 | tf_op jit(solution)/shard_map/all_to_all | solution.py:439
  26.6 3.8 %collective-permute-start.5 = (bf16[128,1024]{1,0:T(8,128)(2,1)S(1)}, bf16[128,1024]{1,0:T(8,128)(2,1)S(1)}, u32[]{:S(2)}, u32[]{:S(2)}) collective-permute-start(bf16[128,1024]{1,0:T(8,128)(2,1)S(1)} %bitcast.13), channel_id=1, source_target_pairs={{0,6},{1,7},{2,4},{3,5},{4,2},{5,3},{6,0},{7,1},{8,14},{9,15},{10,... | collective-permute-start | bytes 786440 | tf_op jit(solution)/shard_map/ppermute | solution.py:420
  31.0 3.8 %collective-permute-start = (bf16[128,1024]{1,0:T(8,128)(2,1)S(1)}, bf16[128,1024]{1,0:T(8,128)(2,1)S(1)}, u32[]{:S(2)}, u32[]{:S(2)}) collective-permute-start(bf16[128,1024]{1,0:T(8,128)(2,1)S(1)} %bitcast.16), channel_id=1, source_target_pairs={{0,1},{1,0},{2,3},{3,2},{4,5},{5,4},{6,7},{7,6},{8,9},{9,8},{10,11... | collective-permute-start | bytes 786440 | tf_op jit(solution)/shard_map/ppermute | solution.py:420
  34.8 6.4 %collective-permute-done.5.p6 = bf16[128,1024]{1,0:T(8,128)(2,1)S(1)} collective-permute-done((bf16[128,1024]{1,0:T(8,128)(2,1)S(1)}, bf16[128,1024]{1,0:T(8,128)(2,1)S(1)}, u32[]{:S(2)}, u32[]{:S(2)}) %collective-permute-start.5) | collective-permute-done | bytes 262176 | tf_op jit(solution)/shard_map/ppermute | solution.py:420
  41.2 1.3 collective-permute-start.6
  42.5 0.9 collective-permute-start.4
  43.9 0.7 collective-permute-done.4.p5
  45.0 30.5 %shard_map.105 = (bf16[512,1024]{1,0:T(8,128)(2,1)}, bf16[1024,128]{1,0:T(8,128)(2,1)S(1)}, bf16[1024,128]{1,0:T(8,128)(2,1)S(1)}, bf16[1024,128]{1,0:T(8,128)(2...) custom-call(s32[1]{0:T(128)} %bitcast.pos, ...), custom_call_target="tpu_custom_call" | custom-call | flops 14000000000 | bytes 18874368 | tf_op jit(solution)/shard_map/pallas_call | solution.py:268
  77.3 2.6 %collective-permute-start.9 = (bf16[1024,128]{1,0:T(8,128)(2,1)S(1)}, bf16[1024,128]{1,0:T(8,128)(2,1)S(1)}, u32[]{:S(2)}, u32[]{:S(2)}) collective-permute-start(bf16[1024,128]{1,0:T(8,128)(2,1)S(1)} %add.13), channel_id=1, source_target_pairs={{0,4},{1,5},{2,6},{3,7},{4,0},{5,1},{6,2},{7,3},{8,12},{9,13},{10,... | collective-permute-start | bytes 786440 | tf_op jit(solution)/shard_map/ppermute | solution.py:420
  79.9 1.0 collective-permute-start.11
  81.3 0.9 shard_map.106
  82.3 4.0 %collective-permute-done.9.a1 = bf16[1024,128]{1,0:T(8,128)(2,1)S(1)} collective-permute-done((bf16[1024,128]{1,0:T(8,128)(2,1)S(1)}, bf16[1024,128]{1,0:T(8,128)(2,1)S(1)}, u32[]{:S(2)}, u32[]{:S(2)}) %collective-permute-start.9) | collective-permute-done | bytes 262176 | tf_op jit(solution)/shard_map/ppermute | solution.py:420
  86.4 6.1 %collective-permute-done.11.a2 = bf16[1024,128]{1,0:T(8,128)(2,1)S(1)} collective-permute-done((bf16[1024,128]{1,0:T(8,128)(2,1)S(1)}, bf16[1024,128]{1,0:T(8,128)(2,1)S(1)}, u32[]{:S(2)}, u32[]{:S(2)}) %collective-permute-start.11) | collective-permute-done | bytes 262176 | tf_op jit(solution)/shard_map/ppermute | solution.py:420
  92.7 0.8 shard_map.107
  93.5 19.3 %all_to_all.22 = bf16[128,16,128]{2,1,0:T(8,128)(2,1)S(1)} all-to-all(bf16[128,16,128]{2,1,0:T(8,128)(2,1)S(1)} %bitcast.12), channel_id=1, replica_groups=mesh['node'=16,'local'=8] {'node','local'}, dimensions={0} | all-to-all | bytes 1048576 | tf_op jit(solution)/shard_map/all_to_all | solution.py:449
  112.8 10.4 %all_to_all.23.tower_rows = bf16[16,8,1024]{2,1,0:T(8,128)(2,1)S(1)} all-to-all(bf16[16,8,1024]{2,1,0:T(8,128)(2,1)S(1)} %shard_map.108), channel_id=1, replica_groups=mesh['node'=16,'local'=8] {'node'}, dimensions={0} | all-to-all | bytes 524288 | tf_op jit(solution)/shard_map/all_to_all | solution.py:450
  123.9 2.2 %collective-permute-start.17 = (bf16[16,8,1024]{2,1,0:T(8,128)(2,1)S(1)}, bf16[16,8,1024]{2,1,0:T(8,128)(2,1)S(1)}, u32[]{:S(2)}, u32[]{:S(2)}) collective-permute-start(bf16[16,8,1024]{2,1,0:T(8,128)(2,1)S(1)} %all_to_all.23.tower_rows), channel_id=1, source_target_pairs={{0,4},{1,5},{2,6},{3,7},{4,0},{5,1},{6,2},{7,3},{8,12},{9,13},{10,... | collective-permute-start | bytes 786440 | tf_op jit(solution)/shard_map/ppermute | solution.py:420
  126.5 3.4 %shard_map.109 = (bf16[1024,1024]{1,0:T(8,128)(2,1)}, bf16[16,8,1024]{2,1,0:T(8,128)(2,1)S(1)}) custom-call(s32[16,8,128]{2,1,0:T(8,128)S(1)} %all_to_all.20.wanted, bf16[16,8,16,128]{3,2,1,0:T(8,128)(2,1)S(1)} %bitcast.11, bf16[1024,1024]{1,0:T(8,128)(2,1)S(1)} %copy-done.1, bf16[16,8,1024]{2,1,0:T(8,128)(2,1)S(1)} %all_to_all.23.tower_rows), custom_call_target="tpu_custom_call" | custom-call | flops 805306368 | bytes 5242880 | tf_op jit(solution)/shard_map/pallas_call | solution.py:379
  129.8 2.9 %collective-permute-start.14 = (bf16[16,8,1024]{2,1,0:T(8,128)(2,1)S(1)}, bf16[16,8,1024]{2,1,0:T(8,128)(2,1)S(1)}, u32[]{:S(2)}, u32[]{:S(2)}) collective-permute-start(bf16[16,8,1024]{2,1,0:T(8,128)(2,1)S(1)} %get-tuple-element.28.refs_0_), channel_id=1, source_target_pairs={{0,1},{1,0},{2,3},{3,2},{4,5},{5,4},{6,7},{7,6},{8,9},{9,8},{10,11... | collective-permute-start | bytes 786440 | tf_op jit(solution)/shard_map/ppermute | solution.py:420
  132.8 4.4 %collective-permute-done.19.refs_3_ = bf16[16,8,1024]{2,1,0:T(8,128)(2,1)S(1)} collective-permute-done((bf16[16,8,1024]{2,1,0:T(8,128)(2,1)S(1)}, bf16[16,8,1024]{2,1,0:T(8,128)(2,1)S(1)}, u32[]{:S(2)}, u32[]{:S(2)}) %collective-permute-start.19) | collective-permute-done | bytes 262176 | tf_op jit(solution)/shard_map/ppermute | solution.py:420
  137.2 1.6 %collective-permute-start.20 = (bf16[16,8,1024]{2,1,0:T(8,128)(2,1)S(1)}, bf16[16,8,1024]{2,1,0:T(8,128)(2,1)S(1)}, u32[]{:S(2)}, u32[]{:S(2)}) collective-permute-start(bf16[16,8,1024]{2,1,0:T(8,128)(2,1)S(1)} %collective-permute-done.19.refs_3_), channel_id=1, source_target_pairs={{0,1},{1,0},{2,3},{3,2},{4,5},{5,4},{6,7},{7,6},{8,9},{9,8},{10,11... | collective-permute-start | bytes 786440 | tf_op jit(solution)/shard_map/ppermute | solution.py:420
  139.4 1.4 shard_map.110.refs_4_
  140.8 1.4 shard_map.111
  (49 shorter events, 6.9 us)
Async XLA Ops:
  1.3 14.1 %copy-start = (bf16[1024,1024]{1,0:T(8,128)(2,1)S(1)}, bf16[1024,1024]{1,0:T(8,128)(2,1)}, u32[]{:S(2)}) copy-start(bf16[1024,1024]{1,0:T(8,128)(2,1)} %content.1) | copy-start | bytes 6291460
  1.4 43.6 %copy-start.5 = (s32[2,256]{1,0:T(2,128)S(1)}, s32[2,256]{1,0:T(2,128)}, u32[]{:S(2)}) copy-start(s32[2,256]{1,0:T(2,128)} %inverse.1) | copy-start | bytes 6148
  1.4 43.6 %copy-start.6 = (s32[2]{0:T(128)S(1)}, s32[2]{0:T(128)}, u32[]{:S(2)}) copy-start(s32[2]{0:T(128)} %lengths.1) | copy-start | bytes 28
  26.6 14.6 %collective-permute-start.5 = (bf16[128,1024]{1,0:T(8,128)(2,1)S(1)}, bf16[128,1024]{1,0:T(8,128)(2,1)S(1)}, u32[]{:S(2)}, u32[]{:S(2)}) collective-permute-start(bf16[128,1024]{1,0:T(8,128)(2,1)S(1)} %bitcast.13), channel_id=1, source_target_pairs={{0,6},{1,7},{2,4},{3,5},{4,2},{5,3},{6,0},{7,1},{8,14},{9,15},{10,... | collective-permute-start | bytes 786440 | tf_op jit(solution)/shard_map/ppermute | solution.py:420
  30.4 12.1 %collective-permute-start.3 = (bf16[128,1024]{1,0:T(8,128)(2,1)S(1)}, bf16[128,1024]{1,0:T(8,128)(2,1)S(1)}, u32[]{:S(2)}, u32[]{:S(2)}) collective-permute-start(bf16[128,1024]{1,0:T(8,128)(2,1)S(1)} %bitcast.14), channel_id=1, source_target_pairs={{0,4},{1,5},{2,6},{3,7},{4,0},{5,1},{6,2},{7,3},{8,12},{9,13},{10,... | collective-permute-start | bytes 786440 | tf_op jit(solution)/shard_map/ppermute | solution.py:420
  30.4 13.1 %collective-permute-start.1 = (bf16[128,1024]{1,0:T(8,128)(2,1)S(1)}, bf16[128,1024]{1,0:T(8,128)(2,1)S(1)}, u32[]{:S(2)}, u32[]{:S(2)}) collective-permute-start(bf16[128,1024]{1,0:T(8,128)(2,1)S(1)} %bitcast.15), channel_id=1, source_target_pairs={{0,2},{1,3},{2,0},{3,1},{4,6},{5,7},{6,4},{7,5},{8,10},{9,11},{10,... | collective-permute-start | bytes 786440 | tf_op jit(solution)/shard_map/ppermute | solution.py:420
  31.0 12.9 %collective-permute-start = (bf16[128,1024]{1,0:T(8,128)(2,1)S(1)}, bf16[128,1024]{1,0:T(8,128)(2,1)S(1)}, u32[]{:S(2)}, u32[]{:S(2)}) collective-permute-start(bf16[128,1024]{1,0:T(8,128)(2,1)S(1)} %bitcast.16), channel_id=1, source_target_pairs={{0,1},{1,0},{2,3},{3,2},{4,5},{5,4},{6,7},{7,6},{8,9},{9,8},{10,11... | collective-permute-start | bytes 786440 | tf_op jit(solution)/shard_map/ppermute | solution.py:420
  41.2 2.7 %collective-permute-start.6 = (bf16[128,1024]{1,0:T(8,128)(2,1)S(1)}, bf16[128,1024]{1,0:T(8,128)(2,1)S(1)}, u32[]{:S(2)}, u32[]{:S(2)}) collective-permute-start(bf16[128,1024]{1,0:T(8,128)(2,1)S(1)} %collective-permute-done.5.p6), channel_id=1, source_target_pairs={{0,1},{1,0},{2,3},{3,2},{4,5},{5,4},{6,7},{7,6},{8,9},{9,8},{10,11... | collective-permute-start | bytes 786440 | tf_op jit(solution)/shard_map/ppermute | solution.py:420
  42.5 2.1 %collective-permute-start.4 = (bf16[128,1024]{1,0:T(8,128)(2,1)S(1)}, bf16[128,1024]{1,0:T(8,128)(2,1)S(1)}, u32[]{:S(2)}, u32[]{:S(2)}) collective-permute-start(bf16[128,1024]{1,0:T(8,128)(2,1)S(1)} %collective-permute-done.3.p4), channel_id=1, source_target_pairs={{0,1},{1,0},{2,3},{3,2},{4,5},{5,4},{6,7},{7,6},{8,9},{9,8},{10,11... | collective-permute-start | bytes 786440 | tf_op jit(solution)/shard_map/ppermute | solution.py:420
  43.5 1.6 %collective-permute-start.2 = (bf16[128,1024]{1,0:T(8,128)(2,1)S(1)}, bf16[128,1024]{1,0:T(8,128)(2,1)S(1)}, u32[]{:S(2)}, u32[]{:S(2)}) collective-permute-start(bf16[128,1024]{1,0:T(8,128)(2,1)S(1)} %collective-permute-done.1.p2), channel_id=1, source_target_pairs={{0,1},{1,0},{2,3},{3,2},{4,5},{5,4},{6,7},{7,6},{8,9},{9,8},{10,11... | collective-permute-start | bytes 786440 | tf_op jit(solution)/shard_map/ppermute | solution.py:420
  75.6 1.6 %collective-permute-start.8 = (bf16[1024,128]{1,0:T(8,128)(2,1)S(1)}, bf16[1024,128]{1,0:T(8,128)(2,1)S(1)}, u32[]{:S(2)}, u32[]{:S(2)}) collective-permute-start(bf16[1024,128]{1,0:T(8,128)(2,1)S(1)} %get-tuple-element.20), channel_id=1, source_target_pairs={{0,1},{1,0},{2,3},{3,2},{4,5},{5,4},{6,7},{7,6},{8,9},{9,8},{10,11... | collective-permute-start | bytes 786440 | tf_op jit(solution)/shard_map/ppermute | solution.py:420
  76.0 3.8 %collective-permute-start.10 = (bf16[1024,128]{1,0:T(8,128)(2,1)S(1)}, bf16[1024,128]{1,0:T(8,128)(2,1)S(1)}, u32[]{:S(2)}, u32[]{:S(2)}) collective-permute-start(bf16[1024,128]{1,0:T(8,128)(2,1)S(1)} %get-tuple-element.22), channel_id=1, source_target_pairs={{0,1},{1,0},{2,3},{3,2},{4,5},{5,4},{6,7},{7,6},{8,9},{9,8},{10,11... | collective-permute-start | bytes 786440 | tf_op jit(solution)/shard_map/ppermute | solution.py:420
  76.2 4.7 %collective-permute-start.12 = (bf16[1024,128]{1,0:T(8,128)(2,1)S(1)}, bf16[1024,128]{1,0:T(8,128)(2,1)S(1)}, u32[]{:S(2)}, u32[]{:S(2)}) collective-permute-start(bf16[1024,128]{1,0:T(8,128)(2,1)S(1)} %get-tuple-element.24), channel_id=1, source_target_pairs={{0,1},{1,0},{2,3},{3,2},{4,5},{5,4},{6,7},{7,6},{8,9},{9,8},{10,11... | collective-permute-start | bytes 786440 | tf_op jit(solution)/shard_map/ppermute | solution.py:420
  76.5 5.7 %collective-permute-start.7 = (bf16[1024,128]{1,0:T(8,128)(2,1)S(1)}, bf16[1024,128]{1,0:T(8,128)(2,1)S(1)}, u32[]{:S(2)}, u32[]{:S(2)}) collective-permute-start(bf16[1024,128]{1,0:T(8,128)(2,1)S(1)} %get-tuple-element.18), channel_id=1, source_target_pairs={{0,1},{1,0},{2,3},{3,2},{4,5},{5,4},{6,7},{7,6},{8,9},{9,8},{10,11... | collective-permute-start | bytes 786440 | tf_op jit(solution)/shard_map/ppermute | solution.py:420
  77.3 9.1 %collective-permute-start.9 = (bf16[1024,128]{1,0:T(8,128)(2,1)S(1)}, bf16[1024,128]{1,0:T(8,128)(2,1)S(1)}, u32[]{:S(2)}, u32[]{:S(2)}) collective-permute-start(bf16[1024,128]{1,0:T(8,128)(2,1)S(1)} %add.13), channel_id=1, source_target_pairs={{0,4},{1,5},{2,6},{3,7},{4,0},{5,1},{6,2},{7,3},{8,12},{9,13},{10,... | collective-permute-start | bytes 786440 | tf_op jit(solution)/shard_map/ppermute | solution.py:420
  79.9 12.5 %collective-permute-start.11 = (bf16[1024,128]{1,0:T(8,128)(2,1)S(1)}, bf16[1024,128]{1,0:T(8,128)(2,1)S(1)}, u32[]{:S(2)}, u32[]{:S(2)}) collective-permute-start(bf16[1024,128]{1,0:T(8,128)(2,1)S(1)} %add.14), channel_id=1, source_target_pairs={{0,2},{1,3},{2,0},{3,1},{4,6},{5,7},{6,4},{7,5},{8,10},{9,11},{10,... | collective-permute-start | bytes 786440 | tf_op jit(solution)/shard_map/ppermute | solution.py:420
  81.0 11.7 %collective-permute-start.13 = (bf16[1024,128]{1,0:T(8,128)(2,1)S(1)}, bf16[1024,128]{1,0:T(8,128)(2,1)S(1)}, u32[]{:S(2)}, u32[]{:S(2)}) collective-permute-start(bf16[1024,128]{1,0:T(8,128)(2,1)S(1)} %add.15), channel_id=1, source_target_pairs={{0,6},{1,7},{2,4},{3,5},{4,2},{5,3},{6,0},{7,1},{8,14},{9,15},{10,... | collective-permute-start | bytes 786440 | tf_op jit(solution)/shard_map/ppermute | solution.py:420
  123.2 14.0 %collective-permute-start.19 = (bf16[16,8,1024]{2,1,0:T(8,128)(2,1)S(1)}, bf16[16,8,1024]{2,1,0:T(8,128)(2,1)S(1)}, u32[]{:S(2)}, u32[]{:S(2)}) collective-permute-start(bf16[16,8,1024]{2,1,0:T(8,128)(2,1)S(1)} %all_to_all.23.tower_rows), channel_id=1, source_target_pairs={{0,6},{1,7},{2,4},{3,5},{4,2},{5,3},{6,0},{7,1},{8,14},{9,15},{10,... | collective-permute-start | bytes 786440 | tf_op jit(solution)/shard_map/ppermute | solution.py:420
  123.9 14.8 %collective-permute-start.17 = (bf16[16,8,1024]{2,1,0:T(8,128)(2,1)S(1)}, bf16[16,8,1024]{2,1,0:T(8,128)(2,1)S(1)}, u32[]{:S(2)}, u32[]{:S(2)}) collective-permute-start(bf16[16,8,1024]{2,1,0:T(8,128)(2,1)S(1)} %all_to_all.23.tower_rows), channel_id=1, source_target_pairs={{0,4},{1,5},{2,6},{3,7},{4,0},{5,1},{6,2},{7,3},{8,12},{9,13},{10,... | collective-permute-start | bytes 786440 | tf_op jit(solution)/shard_map/ppermute | solution.py:420
  126.1 12.7 %collective-permute-start.15 = (bf16[16,8,1024]{2,1,0:T(8,128)(2,1)S(1)}, bf16[16,8,1024]{2,1,0:T(8,128)(2,1)S(1)}, u32[]{:S(2)}, u32[]{:S(2)}) collective-permute-start(bf16[16,8,1024]{2,1,0:T(8,128)(2,1)S(1)} %all_to_all.23.tower_rows), channel_id=1, source_target_pairs={{0,2},{1,3},{2,0},{3,1},{4,6},{5,7},{6,4},{7,5},{8,10},{9,11},{10,... | collective-permute-start | bytes 786440 | tf_op jit(solution)/shard_map/ppermute | solution.py:420
  129.8 10.9 %collective-permute-start.14 = (bf16[16,8,1024]{2,1,0:T(8,128)(2,1)S(1)}, bf16[16,8,1024]{2,1,0:T(8,128)(2,1)S(1)}, u32[]{:S(2)}, u32[]{:S(2)}) collective-permute-start(bf16[16,8,1024]{2,1,0:T(8,128)(2,1)S(1)} %get-tuple-element.28.refs_0_), channel_id=1, source_target_pairs={{0,1},{1,0},{2,3},{3,2},{4,5},{5,4},{6,7},{7,6},{8,9},{9,8},{10,11... | collective-permute-start | bytes 786440 | tf_op jit(solution)/shard_map/ppermute | solution.py:420
  137.2 3.6 %collective-permute-start.20 = (bf16[16,8,1024]{2,1,0:T(8,128)(2,1)S(1)}, bf16[16,8,1024]{2,1,0:T(8,128)(2,1)S(1)}, u32[]{:S(2)}, u32[]{:S(2)}) collective-permute-start(bf16[16,8,1024]{2,1,0:T(8,128)(2,1)S(1)} %collective-permute-done.19.refs_3_), channel_id=1, source_target_pairs={{0,1},{1,0},{2,3},{3,2},{4,5},{5,4},{6,7},{7,6},{8,9},{9,8},{10,11... | collective-permute-start | bytes 786440 | tf_op jit(solution)/shard_map/ppermute | solution.py:420
  138.8 2.0 %collective-permute-start.18 = (bf16[16,8,1024]{2,1,0:T(8,128)(2,1)S(1)}, bf16[16,8,1024]{2,1,0:T(8,128)(2,1)S(1)}, u32[]{:S(2)}, u32[]{:S(2)}) collective-permute-start(bf16[16,8,1024]{2,1,0:T(8,128)(2,1)S(1)} %collective-permute-done.17.refs_2_), channel_id=1, source_target_pairs={{0,1},{1,0},{2,3},{3,2},{4,5},{5,4},{6,7},{7,6},{8,9},{9,8},{10,11... | collective-permute-start | bytes 786440 | tf_op jit(solution)/shard_map/ppermute | solution.py:420
  138.8 2.0 %collective-permute-start.16 = (bf16[16,8,1024]{2,1,0:T(8,128)(2,1)S(1)}, bf16[16,8,1024]{2,1,0:T(8,128)(2,1)S(1)}, u32[]{:S(2)}, u32[]{:S(2)}) collective-permute-start(bf16[16,8,1024]{2,1,0:T(8,128)(2,1)S(1)} %collective-permute-done.15.refs_1_), channel_id=1, source_target_pairs={{0,1},{1,0},{2,3},{3,2},{4,5},{5,4},{6,7},{7,6},{8,9},{9,8},{10,11... | collective-permute-start | bytes 786440 | tf_op jit(solution)/shard_map/ppermute | solution.py:420
  (4 other events, 13.3 us)

commit v6 on v5

--- a/solution.py
+++ b/solution.py
@@ -392,7 +392,7 @@
 
 
 def tower_kernel(which, pos, *refs):
-    pieces, out, buf, sem = refs[:4], refs[-3], refs[-2], refs[-1]
+    pieces, out, buf, sem = refs[: len(which)], refs[-3], refs[-2], refs[-1]
     me = pos[0]
     copies = []
     for i, (s, piece) in enumerate(zip(which, pieces)):
@@ -407,10 +407,10 @@
     return pl.pallas_call(
         functools.partial(tower_kernel, which),
         out_shape=jax.ShapeDtypeStruct((NODES, LOCALS, 8, D), F32),
-        in_specs=[SMEM] + [VMEM] * 4 + [ANY] * len(begun),
+        in_specs=[SMEM] + [VMEM] * len(which) + [ANY] * len(begun),
         out_specs=ANY,
-        scratch_shapes=[pltpu.VMEM((4, NODES, 8, D), F32), pltpu.SemaphoreType.DMA((4,))],
-        input_output_aliases={5: 0} if begun else {},
+        scratch_shapes=[pltpu.VMEM((5, NODES, 8, D), F32), pltpu.SemaphoreType.DMA((5,))],
+        input_output_aliases={1 + len(which): 0} if begun else {},
         compiler_params=pltpu.CompilerParams(vmem_limit_bytes=16 * MIB),
         cost_estimate=pl.CostEstimate(flops=MIB, bytes_accessed=3 * MIB, transcendentals=0),
     )(pos, *[pieces[s] for s in which], *begun)
@@ -450,8 +450,8 @@
     rows = lax.all_to_all(total(back), "node", 0, 0, tiled=True)
     content_grad, handed = content_side(wanted, back, w_tower, rows)
     near = gather_local(rows, handed)
-    begun = tower_side((0, 2, 4, 6), pos, near)
-    tower_grad = tower_side((1, 3, 5, 7), pos, near, begun).reshape(D, D)
+    begun = tower_side((0, 1, 2, 4, 6), pos, near)
+    tower_grad = tower_side((3, 5, 7), pos, near, begun).reshape(D, D)
     return (events_out.reshape(2, SEQ, D), content_grad, tower_grad)
 
 

time: 143 us -> 143 us (level)
  no operation moved by 1% of the time
where the time goes in v6:
time: 143 us; the launch traced here: 142 us
  blocking collectives  54.4 us (38%)
  Pallas kernels  38.9 us (27%)
  starting transfers between devices  24.2 us (17%)
  waiting for transfers between devices  22.9 us (16%)
    pallas_call x1, Pallas kernels, layer(): pl.pallas_call(layer_kernel, out_shape=[jax.ShapeDtypeStruct((ROWS, D), B...  30.5 us
    ppermute x21, starting transfers between devices, swap(): return lax.ppermute(x, 'local', [(i, i ^ s) for i in range(LOCALS)])  24.2 us
    ppermute x21, waiting for transfers between devices, swap(): return lax.ppermute(x, 'local', [(i, i ^ s) for i in range(LOCALS)])  22.9 us
    all_to_all x1, blocking collectives, body(): lax.all_to_all(out, ('node', 'local'), 0, 0, tiled=True)  19.3 us
    all_to_all x1, blocking collectives, body(): wanted = lax.all_to_all(asked, 'node', 0, 0, tiled=True)  14 us
    all_to_all x1, blocking collectives, body(): fetched = lax.all_to_all(picked, 'node', 0, 0, tiled=True).reshape(128, D)  10.7 us
    all_to_all x1, blocking collectives, body(): rows = lax.all_to_all(total(back), 'node', 0, 0, tiled=True)  10.4 us
    pallas_call x1, Pallas kernels, content_side(): pl.pallas_call(content_kernel, out_shape=[jax.ShapeDtypeStruct((1024, D),...  3.36 us
  transfers between devices with their start and end apart: 21, of which 8 were waited for; matrix products, arithmetic and copies ran while one was open for 0% of the time, Pallas kernels for 4%

profile of v6, /device:TPU:1, one launch (start us, length us, event | category | flops | bytes accessed | tf_op | source)
XLA Modules:
  0.0 142.4 jit_solution(4445259017262894135)
XLA Ops:
  1.4 14.0 %all_to_all.20.wanted = s32[16,8,128]{2,1,0:T(8,128)S(1)} all-to-all(s32[16,8,128]{2,1,0:T(8,128)S(1)} %shard_map.103), channel_id=1, replica_groups=mesh['node'=16,'local'=8] {'node'}, dimensions={0} | all-to-all | bytes 131072 | tf_op jit(solution)/shard_map/all_to_all | solution.py:437
  15.9 10.7 %all_to_all.21 = bf16[16,8,1024]{2,1,0:T(8,128)(2,1)S(1)} all-to-all(bf16[16,8,1024]{2,1,0:T(8,128)(2,1)S(1)} %shard_map.104), channel_id=1, replica_groups=mesh['node'=16,'local'=8] {'node'}, dimensions={0} | all-to-all | bytes 524288 | tf_op jit(solution)/shard_map/all_to_all | solution.py:439
  26.6 3.8 %collective-permute-start.5 = (bf16[128,1024]{1,0:T(8,128)(2,1)S(1)}, bf16[128,1024]{1,0:T(8,128)(2,1)S(1)}, u32[]{:S(2)}, u32[]{:S(2)}) collective-permute-start(bf16[128,1024]{1,0:T(8,128)(2,1)S(1)} %bitcast.13), channel_id=1, source_target_pairs={{0,6},{1,7},{2,4},{3,5},{4,2},{5,3},{6,0},{7,1},{8,14},{9,15},{10,... | collective-permute-start | bytes 786440 | tf_op jit(solution)/shard_map/ppermute | solution.py:420
  31.0 3.8 %collective-permute-start = (bf16[128,1024]{1,0:T(8,128)(2,1)S(1)}, bf16[128,1024]{1,0:T(8,128)(2,1)S(1)}, u32[]{:S(2)}, u32[]{:S(2)}) collective-permute-start(bf16[128,1024]{1,0:T(8,128)(2,1)S(1)} %bitcast.16), channel_id=1, source_target_pairs={{0,1},{1,0},{2,3},{3,2},{4,5},{5,4},{6,7},{7,6},{8,9},{9,8},{10,11... | collective-permute-start | bytes 786440 | tf_op jit(solution)/shard_map/ppermute | solution.py:420
  34.8 6.4 %collective-permute-done.5.p6 = bf16[128,1024]{1,0:T(8,128)(2,1)S(1)} collective-permute-done((bf16[128,1024]{1,0:T(8,128)(2,1)S(1)}, bf16[128,1024]{1,0:T(8,128)(2,1)S(1)}, u32[]{:S(2)}, u32[]{:S(2)}) %collective-permute-start.5) | collective-permute-done | bytes 262176 | tf_op jit(solution)/shard_map/ppermute | solution.py:420
  41.2 1.3 collective-permute-start.6
  42.5 0.9 collective-permute-start.4
  43.9 0.7 collective-permute-done.4.p5
  45.0 30.5 %shard_map.105 = (bf16[512,1024]{1,0:T(8,128)(2,1)}, bf16[1024,128]{1,0:T(8,128)(2,1)S(1)}, bf16[1024,128]{1,0:T(8,128)(2,1)S(1)}, bf16[1024,128]{1,0:T(8,128)(2...) custom-call(s32[1]{0:T(128)} %bitcast.pos, ...), custom_call_target="tpu_custom_call" | custom-call | flops 14000000000 | bytes 18874368 | tf_op jit(solution)/shard_map/pallas_call | solution.py:268
  77.3 2.6 %collective-permute-start.9 = (bf16[1024,128]{1,0:T(8,128)(2,1)S(1)}, bf16[1024,128]{1,0:T(8,128)(2,1)S(1)}, u32[]{:S(2)}, u32[]{:S(2)}) collective-permute-start(bf16[1024,128]{1,0:T(8,128)(2,1)S(1)} %add.13), channel_id=1, source_target_pairs={{0,4},{1,5},{2,6},{3,7},{4,0},{5,1},{6,2},{7,3},{8,12},{9,13},{10,... | collective-permute-start | bytes 786440 | tf_op jit(solution)/shard_map/ppermute | solution.py:420
  79.9 1.0 collective-permute-start.11
  81.3 0.9 shard_map.106
  82.3 4.0 %collective-permute-done.9.a1 = bf16[1024,128]{1,0:T(8,128)(2,1)S(1)} collective-permute-done((bf16[1024,128]{1,0:T(8,128)(2,1)S(1)}, bf16[1024,128]{1,0:T(8,128)(2,1)S(1)}, u32[]{:S(2)}, u32[]{:S(2)}) %collective-permute-start.9) | collective-permute-done | bytes 262176 | tf_op jit(solution)/shard_map/ppermute | solution.py:420
  86.4 6.1 %collective-permute-done.11.a2 = bf16[1024,128]{1,0:T(8,128)(2,1)S(1)} collective-permute-done((bf16[1024,128]{1,0:T(8,128)(2,1)S(1)}, bf16[1024,128]{1,0:T(8,128)(2,1)S(1)}, u32[]{:S(2)}, u32[]{:S(2)}) %collective-permute-start.11) | collective-permute-done | bytes 262176 | tf_op jit(solution)/shard_map/ppermute | solution.py:420
  92.7 0.8 shard_map.107
  93.5 19.3 %all_to_all.22 = bf16[128,16,128]{2,1,0:T(8,128)(2,1)S(1)} all-to-all(bf16[128,16,128]{2,1,0:T(8,128)(2,1)S(1)} %bitcast.12), channel_id=1, replica_groups=mesh['node'=16,'local'=8] {'node','local'}, dimensions={0} | all-to-all | bytes 1048576 | tf_op jit(solution)/shard_map/all_to_all | solution.py:449
  112.8 10.4 %all_to_all.23.tower_rows = bf16[16,8,1024]{2,1,0:T(8,128)(2,1)S(1)} all-to-all(bf16[16,8,1024]{2,1,0:T(8,128)(2,1)S(1)} %shard_map.108), channel_id=1, replica_groups=mesh['node'=16,'local'=8] {'node'}, dimensions={0} | all-to-all | bytes 524288 | tf_op jit(solution)/shard_map/all_to_all | solution.py:450
  123.9 2.2 %collective-permute-start.16 = (bf16[16,8,1024]{2,1,0:T(8,128)(2,1)S(1)}, bf16[16,8,1024]{2,1,0:T(8,128)(2,1)S(1)}, u32[]{:S(2)}, u32[]{:S(2)}) collective-permute-start(bf16[16,8,1024]{2,1,0:T(8,128)(2,1)S(1)} %all_to_all.23.tower_rows), channel_id=1, source_target_pairs={{0,4},{1,5},{2,6},{3,7},{4,0},{5,1},{6,2},{7,3},{8,12},{9,13},{10,... | collective-permute-start | bytes 786440 | tf_op jit(solution)/shard_map/ppermute | solution.py:420
  126.5 3.4 %shard_map.109 = (bf16[1024,1024]{1,0:T(8,128)(2,1)}, bf16[16,8,1024]{2,1,0:T(8,128)(2,1)S(1)}) custom-call(s32[16,8,128]{2,1,0:T(8,128)S(1)} %all_to_all.20.wanted, bf16[16,8,16,128]{3,2,1,0:T(8,128)(2,1)S(1)} %bitcast.11, bf16[1024,1024]{1,0:T(8,128)(2,1)S(1)} %copy-done.1, bf16[16,8,1024]{2,1,0:T(8,128)(2,1)S(1)} %all_to_all.23.tower_rows), custom_call_target="tpu_custom_call" | custom-call | flops 805306368 | bytes 5242880 | tf_op jit(solution)/shard_map/pallas_call | solution.py:379
  129.8 2.9 %collective-permute-start.20 = (bf16[16,8,1024]{2,1,0:T(8,128)(2,1)S(1)}, bf16[16,8,1024]{2,1,0:T(8,128)(2,1)S(1)}, u32[]{:S(2)}, u32[]{:S(2)}) collective-permute-start(bf16[16,8,1024]{2,1,0:T(8,128)(2,1)S(1)} %get-tuple-element.28.refs_0_), channel_id=1, source_target_pairs={{0,1},{1,0},{2,3},{3,2},{4,5},{5,4},{6,7},{7,6},{8,9},{9,8},{10,11... | collective-permute-start | bytes 786440 | tf_op jit(solution)/shard_map/ppermute | solution.py:420
  132.8 4.4 %collective-permute-done.18.refs_4_ = bf16[16,8,1024]{2,1,0:T(8,128)(2,1)S(1)} collective-permute-done((bf16[16,8,1024]{2,1,0:T(8,128)(2,1)S(1)}, bf16[16,8,1024]{2,1,0:T(8,128)(2,1)S(1)}, u32[]{:S(2)}, u32[]{:S(2)}) %collective-permute-start.18) | collective-permute-done | bytes 262176 | tf_op jit(solution)/shard_map/ppermute | solution.py:420
  137.2 1.6 %collective-permute-start.19 = (bf16[16,8,1024]{2,1,0:T(8,128)(2,1)S(1)}, bf16[16,8,1024]{2,1,0:T(8,128)(2,1)S(1)}, u32[]{:S(2)}, u32[]{:S(2)}) collective-permute-start(bf16[16,8,1024]{2,1,0:T(8,128)(2,1)S(1)} %collective-permute-done.18.refs_4_), channel_id=1, source_target_pairs={{0,1},{1,0},{2,3},{3,2},{4,5},{5,4},{6,7},{7,6},{8,9},{9,8},{10,11... | collective-permute-start | bytes 786440 | tf_op jit(solution)/shard_map/ppermute | solution.py:420
  139.4 1.6 %shard_map.110.refs_3_ = f32[16,8,8,1024]{3,2,1,0:T(8,128)} custom-call(s32[1]{0:T(128)} %bitcast.pos, bf16[16,8,1024]{2,1,0:T(8,128)(2,1)S(1)} %get-tuple-element.28.refs_0_, bf16[16,8,1024]{2,1,0:T(8,128)(2,1)S(1)} %collective-permute-done.20.refs_1_, bf16[16,8,1024]{2,1,0:T(8,128)(2,1)S(1)} %collective-permute-done.14.refs_2_, ...), custom_call_target="tpu_custom_call" | custom-call | flops 1048576 | bytes 3145728 | tf_op jit(solution)/shard_map/pallas_call | solution.py:407
  141.0 1.2 shard_map.111
  (49 shorter events, 6.9 us)
Async XLA Ops:
  1.3 14.1 %copy-start = (bf16[1024,1024]{1,0:T(8,128)(2,1)S(1)}, bf16[1024,1024]{1,0:T(8,128)(2,1)}, u32[]{:S(2)}) copy-start(bf16[1024,1024]{1,0:T(8,128)(2,1)} %content.1) | copy-start | bytes 6291460
  1.4 43.6 %copy-start.5 = (s32[2,256]{1,0:T(2,128)S(1)}, s32[2,256]{1,0:T(2,128)}, u32[]{:S(2)}) copy-start(s32[2,256]{1,0:T(2,128)} %inverse.1) | copy-start | bytes 6148
  1.4 43.6 %copy-start.6 = (s32[2]{0:T(128)S(1)}, s32[2]{0:T(128)}, u32[]{:S(2)}) copy-start(s32[2]{0:T(128)} %lengths.1) | copy-start | bytes 28
  26.6 14.6 %collective-permute-start.5 = (bf16[128,1024]{1,0:T(8,128)(2,1)S(1)}, bf16[128,1024]{1,0:T(8,128)(2,1)S(1)}, u32[]{:S(2)}, u32[]{:S(2)}) collective-permute-start(bf16[128,1024]{1,0:T(8,128)(2,1)S(1)} %bitcast.13), channel_id=1, source_target_pairs={{0,6},{1,7},{2,4},{3,5},{4,2},{5,3},{6,0},{7,1},{8,14},{9,15},{10,... | collective-permute-start | bytes 786440 | tf_op jit(solution)/shard_map/ppermute | solution.py:420
  30.4 12.1 %collective-permute-start.3 = (bf16[128,1024]{1,0:T(8,128)(2,1)S(1)}, bf16[128,1024]{1,0:T(8,128)(2,1)S(1)}, u32[]{:S(2)}, u32[]{:S(2)}) collective-permute-start(bf16[128,1024]{1,0:T(8,128)(2,1)S(1)} %bitcast.14), channel_id=1, source_target_pairs={{0,4},{1,5},{2,6},{3,7},{4,0},{5,1},{6,2},{7,3},{8,12},{9,13},{10,... | collective-permute-start | bytes 786440 | tf_op jit(solution)/shard_map/ppermute | solution.py:420
  30.4 13.1 %collective-permute-start.1 = (bf16[128,1024]{1,0:T(8,128)(2,1)S(1)}, bf16[128,1024]{1,0:T(8,128)(2,1)S(1)}, u32[]{:S(2)}, u32[]{:S(2)}) collective-permute-start(bf16[128,1024]{1,0:T(8,128)(2,1)S(1)} %bitcast.15), channel_id=1, source_target_pairs={{0,2},{1,3},{2,0},{3,1},{4,6},{5,7},{6,4},{7,5},{8,10},{9,11},{10,... | collective-permute-start | bytes 786440 | tf_op jit(solution)/shard_map/ppermute | solution.py:420
  31.0 12.9 %collective-permute-start = (bf16[128,1024]{1,0:T(8,128)(2,1)S(1)}, bf16[128,1024]{1,0:T(8,128)(2,1)S(1)}, u32[]{:S(2)}, u32[]{:S(2)}) collective-permute-start(bf16[128,1024]{1,0:T(8,128)(2,1)S(1)} %bitcast.16), channel_id=1, source_target_pairs={{0,1},{1,0},{2,3},{3,2},{4,5},{5,4},{6,7},{7,6},{8,9},{9,8},{10,11... | collective-permute-start | bytes 786440 | tf_op jit(solution)/shard_map/ppermute | solution.py:420
  41.2 2.7 %collective-permute-start.6 = (bf16[128,1024]{1,0:T(8,128)(2,1)S(1)}, bf16[128,1024]{1,0:T(8,128)(2,1)S(1)}, u32[]{:S(2)}, u32[]{:S(2)}) collective-permute-start(bf16[128,1024]{1,0:T(8,128)(2,1)S(1)} %collective-permute-done.5.p6), channel_id=1, source_target_pairs={{0,1},{1,0},{2,3},{3,2},{4,5},{5,4},{6,7},{7,6},{8,9},{9,8},{10,11... | collective-permute-start | bytes 786440 | tf_op jit(solution)/shard_map/ppermute | solution.py:420
  42.5 2.1 %collective-permute-start.4 = (bf16[128,1024]{1,0:T(8,128)(2,1)S(1)}, bf16[128,1024]{1,0:T(8,128)(2,1)S(1)}, u32[]{:S(2)}, u32[]{:S(2)}) collective-permute-start(bf16[128,1024]{1,0:T(8,128)(2,1)S(1)} %collective-permute-done.3.p4), channel_id=1, source_target_pairs={{0,1},{1,0},{2,3},{3,2},{4,5},{5,4},{6,7},{7,6},{8,9},{9,8},{10,11... | collective-permute-start | bytes 786440 | tf_op jit(solution)/shard_map/ppermute | solution.py:420
  43.5 1.6 %collective-permute-start.2 = (bf16[128,1024]{1,0:T(8,128)(2,1)S(1)}, bf16[128,1024]{1,0:T(8,128)(2,1)S(1)}, u32[]{:S(2)}, u32[]{:S(2)}) collective-permute-start(bf16[128,1024]{1,0:T(8,128)(2,1)S(1)} %collective-permute-done.1.p2), channel_id=1, source_target_pairs={{0,1},{1,0},{2,3},{3,2},{4,5},{5,4},{6,7},{7,6},{8,9},{9,8},{10,11... | collective-permute-start | bytes 786440 | tf_op jit(solution)/shard_map/ppermute | solution.py:420
  75.6 1.6 %collective-permute-start.8 = (bf16[1024,128]{1,0:T(8,128)(2,1)S(1)}, bf16[1024,128]{1,0:T(8,128)(2,1)S(1)}, u32[]{:S(2)}, u32[]{:S(2)}) collective-permute-start(bf16[1024,128]{1,0:T(8,128)(2,1)S(1)} %get-tuple-element.20), channel_id=1, source_target_pairs={{0,1},{1,0},{2,3},{3,2},{4,5},{5,4},{6,7},{7,6},{8,9},{9,8},{10,11... | collective-permute-start | bytes 786440 | tf_op jit(solution)/shard_map/ppermute | solution.py:420
  76.0 3.8 %collective-permute-start.10 = (bf16[1024,128]{1,0:T(8,128)(2,1)S(1)}, bf16[1024,128]{1,0:T(8,128)(2,1)S(1)}, u32[]{:S(2)}, u32[]{:S(2)}) collective-permute-start(bf16[1024,128]{1,0:T(8,128)(2,1)S(1)} %get-tuple-element.22), channel_id=1, source_target_pairs={{0,1},{1,0},{2,3},{3,2},{4,5},{5,4},{6,7},{7,6},{8,9},{9,8},{10,11... | collective-permute-start | bytes 786440 | tf_op jit(solution)/shard_map/ppermute | solution.py:420
  76.2 4.7 %collective-permute-start.12 = (bf16[1024,128]{1,0:T(8,128)(2,1)S(1)}, bf16[1024,128]{1,0:T(8,128)(2,1)S(1)}, u32[]{:S(2)}, u32[]{:S(2)}) collective-permute-start(bf16[1024,128]{1,0:T(8,128)(2,1)S(1)} %get-tuple-element.24), channel_id=1, source_target_pairs={{0,1},{1,0},{2,3},{3,2},{4,5},{5,4},{6,7},{7,6},{8,9},{9,8},{10,11... | collective-permute-start | bytes 786440 | tf_op jit(solution)/shard_map/ppermute | solution.py:420
  76.5 5.7 %collective-permute-start.7 = (bf16[1024,128]{1,0:T(8,128)(2,1)S(1)}, bf16[1024,128]{1,0:T(8,128)(2,1)S(1)}, u32[]{:S(2)}, u32[]{:S(2)}) collective-permute-start(bf16[1024,128]{1,0:T(8,128)(2,1)S(1)} %get-tuple-element.18), channel_id=1, source_target_pairs={{0,1},{1,0},{2,3},{3,2},{4,5},{5,4},{6,7},{7,6},{8,9},{9,8},{10,11... | collective-permute-start | bytes 786440 | tf_op jit(solution)/shard_map/ppermute | solution.py:420
  77.3 9.1 %collective-permute-start.9 = (bf16[1024,128]{1,0:T(8,128)(2,1)S(1)}, bf16[1024,128]{1,0:T(8,128)(2,1)S(1)}, u32[]{:S(2)}, u32[]{:S(2)}) collective-permute-start(bf16[1024,128]{1,0:T(8,128)(2,1)S(1)} %add.13), channel_id=1, source_target_pairs={{0,4},{1,5},{2,6},{3,7},{4,0},{5,1},{6,2},{7,3},{8,12},{9,13},{10,... | collective-permute-start | bytes 786440 | tf_op jit(solution)/shard_map/ppermute | solution.py:420
  79.9 12.5 %collective-permute-start.11 = (bf16[1024,128]{1,0:T(8,128)(2,1)S(1)}, bf16[1024,128]{1,0:T(8,128)(2,1)S(1)}, u32[]{:S(2)}, u32[]{:S(2)}) collective-permute-start(bf16[1024,128]{1,0:T(8,128)(2,1)S(1)} %add.14), channel_id=1, source_target_pairs={{0,2},{1,3},{2,0},{3,1},{4,6},{5,7},{6,4},{7,5},{8,10},{9,11},{10,... | collective-permute-start | bytes 786440 | tf_op jit(solution)/shard_map/ppermute | solution.py:420
  81.0 11.7 %collective-permute-start.13 = (bf16[1024,128]{1,0:T(8,128)(2,1)S(1)}, bf16[1024,128]{1,0:T(8,128)(2,1)S(1)}, u32[]{:S(2)}, u32[]{:S(2)}) collective-permute-start(bf16[1024,128]{1,0:T(8,128)(2,1)S(1)} %add.15), channel_id=1, source_target_pairs={{0,6},{1,7},{2,4},{3,5},{4,2},{5,3},{6,0},{7,1},{8,14},{9,15},{10,... | collective-permute-start | bytes 786440 | tf_op jit(solution)/shard_map/ppermute | solution.py:420
  123.2 14.0 %collective-permute-start.18 = (bf16[16,8,1024]{2,1,0:T(8,128)(2,1)S(1)}, bf16[16,8,1024]{2,1,0:T(8,128)(2,1)S(1)}, u32[]{:S(2)}, u32[]{:S(2)}) collective-permute-start(bf16[16,8,1024]{2,1,0:T(8,128)(2,1)S(1)} %all_to_all.23.tower_rows), channel_id=1, source_target_pairs={{0,6},{1,7},{2,4},{3,5},{4,2},{5,3},{6,0},{7,1},{8,14},{9,15},{10,... | collective-permute-start | bytes 786440 | tf_op jit(solution)/shard_map/ppermute | solution.py:420
  123.9 14.8 %collective-permute-start.16 = (bf16[16,8,1024]{2,1,0:T(8,128)(2,1)S(1)}, bf16[16,8,1024]{2,1,0:T(8,128)(2,1)S(1)}, u32[]{:S(2)}, u32[]{:S(2)}) collective-permute-start(bf16[16,8,1024]{2,1,0:T(8,128)(2,1)S(1)} %all_to_all.23.tower_rows), channel_id=1, source_target_pairs={{0,4},{1,5},{2,6},{3,7},{4,0},{5,1},{6,2},{7,3},{8,12},{9,13},{10,... | collective-permute-start | bytes 786440 | tf_op jit(solution)/shard_map/ppermute | solution.py:420
  126.1 12.7 %collective-permute-start.14 = (bf16[16,8,1024]{2,1,0:T(8,128)(2,1)S(1)}, bf16[16,8,1024]{2,1,0:T(8,128)(2,1)S(1)}, u32[]{:S(2)}, u32[]{:S(2)}) collective-permute-start(bf16[16,8,1024]{2,1,0:T(8,128)(2,1)S(1)} %all_to_all.23.tower_rows), channel_id=1, source_target_pairs={{0,2},{1,3},{2,0},{3,1},{4,6},{5,7},{6,4},{7,5},{8,10},{9,11},{10,... | collective-permute-start | bytes 786440 | tf_op jit(solution)/shard_map/ppermute | solution.py:420
  129.8 9.6 %collective-permute-start.20 = (bf16[16,8,1024]{2,1,0:T(8,128)(2,1)S(1)}, bf16[16,8,1024]{2,1,0:T(8,128)(2,1)S(1)}, u32[]{:S(2)}, u32[]{:S(2)}) collective-permute-start(bf16[16,8,1024]{2,1,0:T(8,128)(2,1)S(1)} %get-tuple-element.28.refs_0_), channel_id=1, source_target_pairs={{0,1},{1,0},{2,3},{3,2},{4,5},{5,4},{6,7},{7,6},{8,9},{9,8},{10,11... | collective-permute-start | bytes 786440 | tf_op jit(solution)/shard_map/ppermute | solution.py:420
  137.2 3.8 %collective-permute-start.19 = (bf16[16,8,1024]{2,1,0:T(8,128)(2,1)S(1)}, bf16[16,8,1024]{2,1,0:T(8,128)(2,1)S(1)}, u32[]{:S(2)}, u32[]{:S(2)}) collective-permute-start(bf16[16,8,1024]{2,1,0:T(8,128)(2,1)S(1)} %collective-permute-done.18.refs_4_), channel_id=1, source_target_pairs={{0,1},{1,0},{2,3},{3,2},{4,5},{5,4},{6,7},{7,6},{8,9},{9,8},{10,11... | collective-permute-start | bytes 786440 | tf_op jit(solution)/shard_map/ppermute | solution.py:420
  138.8 2.2 %collective-permute-start.17 = (bf16[16,8,1024]{2,1,0:T(8,128)(2,1)S(1)}, bf16[16,8,1024]{2,1,0:T(8,128)(2,1)S(1)}, u32[]{:S(2)}, u32[]{:S(2)}) collective-permute-start(bf16[16,8,1024]{2,1,0:T(8,128)(2,1)S(1)} %collective-permute-done.16.refs_3_), channel_id=1, source_target_pairs={{0,1},{1,0},{2,3},{3,2},{4,5},{5,4},{6,7},{7,6},{8,9},{9,8},{10,11... | collective-permute-start | bytes 786440 | tf_op jit(solution)/shard_map/ppermute | solution.py:420
  138.8 2.2 %collective-permute-start.15 = (bf16[16,8,1024]{2,1,0:T(8,128)(2,1)S(1)}, bf16[16,8,1024]{2,1,0:T(8,128)(2,1)S(1)}, u32[]{:S(2)}, u32[]{:S(2)}) collective-permute-start(bf16[16,8,1024]{2,1,0:T(8,128)(2,1)S(1)} %collective-permute-done.14.refs_2_), channel_id=1, source_target_pairs={{0,1},{1,0},{2,3},{3,2},{4,5},{5,4},{6,7},{7,6},{8,9},{9,8},{10,11... | collective-permute-start | bytes 786440 | tf_op jit(solution)/shard_map/ppermute | solution.py:420
  (4 other events, 13.3 us)
